TPU v7x, 32 devices: a whole 2x2x4 slice. The times are simulated.
32 devices in a mesh: dp: 8 (over z, y), tensor: 4 (over x, core).
Axes of the slice: x: 2, y: 2, z: 4, core: 2. Of those that a mesh axis runs over, the one named last changes fastest.
Arguments:
- inputs: bfloat16 [16384, 1024], P(('dp', 'tensor')), may hold values from -6 to 6
- qkv_weight: bfloat16 [3, 1024, 1024], P(None, 'dp', 'tensor'), may hold values from -0.25 to 0.25
- qv_bias: bfloat16 [2, 1024], P(None, ('tensor', 'dp')), may hold values from -2 to 2
- proj_weight: bfloat16 [1024, 1024], P('tensor', 'dp'), may hold values from -0.5 to 0.5
- proj_bias: bfloat16 [1024], P('dp'), may hold values from -2 to 2
- fc_weight: bfloat16 [1024, 4096], P('dp', 'tensor'), may hold values from -0.1875 to 0.1875
- fc_bias: bfloat16 [4096], P(('tensor', 'dp')), may hold values from -2 to 2
- out_weight: bfloat16 [4096, 1024], P('tensor', 'dp'), may hold values from -0.1875 to 0.1875
- out_bias: bfloat16 [1024], P('dp'), may hold values from -2 to 2
- attn_norm_gain: bfloat16 [1024], P('dp'), may hold values from 0.5 to 1.5
- attn_norm_bias: bfloat16 [1024], P('dp'), may hold values from -2 to 2
- mlp_norm_gain: bfloat16 [1024], P('dp'), may hold values from 0.5 to 1.5
- mlp_norm_bias: bfloat16 [1024], P('dp'), may hold values from -2 to 2
- cotangent: bfloat16 [16384, 1024], P(('dp', 'tensor')), may hold values from -6 to 6
Outputs:
- outputs: bfloat16 [16384, 1024], P(('dp', 'tensor'))
- grad_inputs: bfloat16 [16384, 1024], P(('dp', 'tensor'))
- grad_qkv_weight: float32 [3, 1024, 1024], P(None, 'dp', 'tensor')
- grad_qv_bias: float32 [2, 1024], P(None, ('tensor', 'dp'))
- grad_proj_weight: float32 [1024, 1024], P('tensor', 'dp')
- grad_proj_bias: float32 [1024], P('dp')
- grad_fc_weight: float32 [1024, 4096], P('dp', 'tensor')
- grad_fc_bias: float32 [4096], P(('tensor', 'dp'))
- grad_out_weight: float32 [4096, 1024], P('tensor', 'dp')
- grad_out_bias: float32 [1024], P('dp')
- grad_attn_norm_gain: float32 [1024], P('dp')
- grad_attn_norm_bias: float32 [1024], P('dp')
- grad_mlp_norm_gain: float32 [1024], P('dp')
- grad_mlp_norm_bias: float32 [1024], P('dp')
All inputs are finite; a program needn't handle non-finite values.
Results may differ from a plain program's by a relative error of at most 0.02.
Values may be sent and summed in bfloat16 or wider, within the bound.
No kernel may reach another device: no remote copies, remote signals or barrier semaphores. Data moves between devices by JAX's collectives and lax.ppermute only.
A program may use at most 192 MiB of HBM per device.

v0:
```python
import functools

import jax
import jax.numpy as jnp
from jax import lax
from jax.experimental import pallas as pl
from jax.experimental.pallas import tpu as pltpu
from jax.sharding import PartitionSpec as P

HD = 64
PAIR = 2 * HD
EPSILON = 1e-05
NEGATIVE = -1e30
ROOT_TWO_PI = 0.7978845608028654
F32 = jnp.float32
BF16 = jnp.bfloat16
MIB = 1024 * 1024
SCALE = 0.25
ANY_SPACE = pl.BlockSpec(memory_space=pl.ANY)
SCALARS = pl.BlockSpec(memory_space=pltpu.SMEM)


def params(mib):
    return pltpu.CompilerParams(vmem_limit_bytes=mib * MIB)


def cost(micros):
    return pl.CostEstimate(
        flops=int(micros * SCALE * 1.1e9),
        bytes_accessed=int(micros * SCALE * 1e6),
        transcendentals=0,
    )


def swap_x(value):
    return lax.ppermute(value, "tensor", [(0, 2), (2, 0), (1, 3), (3, 1)])


def swap_core(value):
    return lax.ppermute(value, "tensor", [(0, 1), (1, 0), (2, 3), (3, 2)])


def dot(a, b, contract, kind=F32):
    return lax.dot_general(a, b, (contract, ((), ())), preferred_element_type=kind)


NN = ((1,), (0,))
NT = ((1,), (1,))
TN = ((0,), (0,))


def normalize(values):
    average = jnp.mean(values, axis=-1, keepdims=True)
    centered = values - average
    spread = jnp.mean(centered * centered, axis=-1, keepdims=True)
    factor = lax.rsqrt(spread + EPSILON)
    return centered * factor, factor


def norm_back(unit, factor, gain, grad):
    scaled = grad * gain
    return factor * (
        scaled
        - jnp.mean(scaled, axis=-1, keepdims=True)
        - unit * jnp.mean(scaled * unit, axis=-1, keepdims=True)
    )


def gelu_both(values):
    squared = values * values
    bent = jnp.tanh(ROOT_TWO_PI * values * (1.0 + 0.044715 * squared))
    half = 0.5 * (1.0 + bent)
    slope = half + 0.5 * values * (1.0 - bent * bent) * ROOT_TWO_PI * (
        1.0 + 3.0 * 0.044715 * squared
    )
    return values * half, slope


def split_heads(block):
    first = lax.broadcasted_iota(jnp.int32, block.shape, 1) < HD
    return [jnp.where(first, block, 0.0).astype(BF16), jnp.where(first, 0.0, block).astype(BF16)]


def attend_kernel(qkv_ref, *rest, row0, block):
    mixed_ref, total_ref, kept, acc = rest[-4:]
    count = mixed_ref.shape[0] // block
    first = lax.broadcasted_iota(jnp.int32, (PAIR, block), 0) < HD
    causal = lax.broadcasted_iota(jnp.int32, (block, block), 0) <= lax.broadcasted_iota(
        jnp.int32, (block, block), 1
    )
    for i in range(count):
        start = row0 + i * block
        heads = split_heads(qkv_ref[pl.ds(start, block), 0:PAIR].astype(F32) * (HD**-0.5))
        keys = qkv_ref[pl.ds(start, block), PAIR : 2 * PAIR]
        tops = []
        for h in range(2):
            scores = jnp.where(causal, dot(keys, heads[h], NT), NEGATIVE)
            kept[h, pl.ds(start, block), :] = scores
            tops.append(jnp.max(scores, axis=0, keepdims=True))

        def score_step(j, tops):
            at = pl.multiple_of(j * block, block)
            tile_keys = qkv_ref[pl.ds(at, block), PAIR : 2 * PAIR]
            found = []
            for h in range(2):
                scores = dot(tile_keys, heads[h], NT)
                kept[h, pl.ds(at, block), :] = scores
                found.append(jnp.maximum(tops[h], jnp.max(scores, axis=0, keepdims=True)))
            return tuple(found)

        tops = lax.fori_loop(0, start // block, score_step, tuple(tops))
        acc[...] = jnp.zeros(acc.shape, F32)

        def value_step(j, sums):
            at = pl.multiple_of(j * block, block)
            tile_values = qkv_ref[pl.ds(at, block), 2 * PAIR : 3 * PAIR]
            found = []
            for h in range(2):
                powers = jnp.exp(kept[h, pl.ds(at, block), :] - tops[h])
                found.append(sums[h] + jnp.sum(powers, axis=0, keepdims=True))
                acc[h] += dot(powers.astype(BF16), tile_values, TN)
            return tuple(found)

        zero = jnp.zeros((1, block), F32)
        sums = lax.fori_loop(0, start // block + 1, value_step, (zero, zero))
        inverse = jnp.transpose(jnp.where(first, 1.0 / sums[0], 1.0 / sums[1]))
        lane = lax.broadcasted_iota(jnp.int32, (block, PAIR), 1) < HD
        local = slice(i * block, (i + 1) * block)
        mixed_ref[local, :] = (jnp.where(lane, acc[0], acc[1]) * inverse).astype(BF16)
        for h in range(2):
            total_ref[0, h : h + 1, local] = tops[h] + jnp.log(sums[h])


def attend(qkv, row0, rows, block, after=()):
    pairs = qkv.shape[1] // (3 * PAIR)
    return pl.pallas_call(
        functools.partial(attend_kernel, row0=row0, block=block),
        grid=(pairs,),
        in_specs=[pl.BlockSpec((row0 + rows, 3 * PAIR), lambda j: (0, j))]
        + [ANY_SPACE] * len(after),
        out_specs=[
            pl.BlockSpec((rows, PAIR), lambda j: (0, j)),
            pl.BlockSpec((1, 2, rows), lambda j: (j, 0, 0)),
        ],
        out_shape=[
            jax.ShapeDtypeStruct((rows, pairs * PAIR), BF16),
            jax.ShapeDtypeStruct((pairs, 2, rows), F32),
        ],
        scratch_shapes=[
            pltpu.VMEM((2, row0 + rows, block), F32),
            pltpu.VMEM((2, block, PAIR), F32),
        ],
        compiler_params=params(16),
        cost_estimate=cost(16 if row0 else 6),
        name="attend_%d" % row0,
    )(qkv, *after)


def attend_back_kernel(
    core_ref, qkv_ref, mixed_ref, grad_ref, total_ref, *rest, row0, block, has_before
):
    before_ref = rest[0]
    sent_ref = None
    if has_before:
        out_ref, sums_ref, sent_ref, key_acc, value_acc, query_acc = rest[-6:]
    else:
        out_ref, sums_ref, key_acc, value_acc, query_acc = rest[-5:]
    rows = mixed_ref.shape[0]
    count = rows // block
    lane = lax.broadcasted_iota(jnp.int32, (block, PAIR), 1)
    first = lane < HD
    causal = lax.broadcasted_iota(jnp.int32, (block, block), 0) <= lax.broadcasted_iota(
        jnp.int32, (block, block), 1
    )
    if has_before:
        key_acc[0:row0, :] = before_ref[:, PAIR : 2 * PAIR]
        value_acc[0:row0, :] = before_ref[:, 2 * PAIR : 3 * PAIR]
        key_acc[row0:, :] = jnp.zeros((rows, PAIR), F32)
        value_acc[row0:, :] = jnp.zeros((rows, PAIR), F32)
    else:
        key_acc[...] = jnp.zeros(key_acc.shape, F32)
        value_acc[...] = jnp.zeros(value_acc.shape, F32)
    for i in range(count):
        start = row0 + i * block
        local = slice(i * block, (i + 1) * block)
        query_heads = split_heads(
            qkv_ref[pl.ds(start, block), 0:PAIR].astype(F32) * (HD**-0.5)
        )
        grads = grad_ref[local, :].astype(F32)
        grad_heads = split_heads(grads)
        inner = jnp.transpose(grads * mixed_ref[local, :].astype(F32))
        total_rows = [total_ref[0, h : h + 1, local] for h in range(2)]
        inner_rows = [
            jnp.sum(inner[h * HD : (h + 1) * HD, :], axis=0, keepdims=True) for h in range(2)
        ]

        def tile(at, masked):
            tile_keys = qkv_ref[pl.ds(at, block), PAIR : 2 * PAIR]
            tile_values = qkv_ref[pl.ds(at, block), 2 * PAIR : 3 * PAIR]
            key_sum, value_sum = None, None
            for h in range(2):
                scores = dot(tile_keys, query_heads[h], NT)
                weights = jnp.exp(scores - total_rows[h])
                if masked:
                    weights = jnp.where(causal, weights, 0.0)
                grad_weights = dot(tile_values, grad_heads[h], NT)
                grad_scores = (weights * (grad_weights - inner_rows[h])).astype(BF16)
                value_part = dot(weights.astype(BF16), grad_heads[h], NN)
                key_part = dot(grad_scores, query_heads[h], NN)
                query_part = dot(grad_scores, tile_keys, TN)
                key_sum = key_part if key_sum is None else key_sum + key_part
                value_sum = value_part if value_sum is None else value_sum + value_part
                if masked:
                    query_acc[h] = query_part
                else:
                    query_acc[h] += query_part
            key_acc[pl.ds(at, block), :] += key_sum
            value_acc[pl.ds(at, block), :] += value_sum

        tile(start, True)

        def step(j, carry):
            tile(pl.multiple_of(j * block, block), False)
            return carry

        if start:
            lax.fori_loop(0, start // block, step, 0)
        query_grad = jnp.where(first, query_acc[0], query_acc[1]) * (HD**-0.5)
        out_ref[start : start + block, 0:PAIR] = query_grad.astype(out_ref.dtype)
    if has_before:
        out_ref[0:row0, 0:PAIR] = before_ref[:, 0:PAIR].astype(out_ref.dtype)
    out_ref[:, PAIR : 2 * PAIR] = key_acc[...].astype(out_ref.dtype)
    out_ref[:, 2 * PAIR : 3 * PAIR] = value_acc[...].astype(out_ref.dtype)
    sums_ref[...] = jnp.sum(out_ref[...].astype(F32), axis=0, keepdims=True)
    if has_before:
        size = sent_ref.shape[0] // 2
        for half in range(2):
            at = pl.multiple_of((2 * half + 1 - core_ref[0]) * size, size)
            sent_ref[half * size : (half + 1) * size, :] = out_ref[pl.ds(at, size), :]


def attend_back(qkv, mixed, grads, totals, before, row0, block, pair, pairs, after=(), core=None):
    rows = mixed.shape[0]
    extent = row0 + rows
    narrow = pl.BlockSpec((rows, PAIR), lambda j: (0, pair + j))
    in_specs = [
        SCALARS,
        pl.BlockSpec((extent, 3 * PAIR), lambda j: (0, pair + j)),
        narrow,
        narrow,
        pl.BlockSpec((1, 2, rows), lambda j: (pair + j, 0, 0)),
    ]
    core = jnp.zeros((), jnp.int32) if core is None else core
    operands = [core.reshape(1).astype(jnp.int32), qkv, mixed, grads, totals]
    if before is not None:
        in_specs.append(pl.BlockSpec((row0, 3 * PAIR), lambda j: (0, pair + j)))
        operands.append(before)
    in_specs += [ANY_SPACE] * len(after)
    return pl.pallas_call(
        functools.partial(
            attend_back_kernel, row0=row0, block=block, has_before=before is not None
        ),
        grid=(pairs,),
        in_specs=in_specs,
        out_specs=[
            pl.BlockSpec((extent, 3 * PAIR), lambda j: (0, j)),
            pl.BlockSpec((1, 3 * PAIR), lambda j: (0, j)),
        ]
        + ([] if before is None else [pl.BlockSpec((extent // 2, 3 * PAIR), lambda j: (0, j))]),
        out_shape=[
            jax.ShapeDtypeStruct((extent, pairs * 3 * PAIR), F32 if before is None else BF16),
            jax.ShapeDtypeStruct((1, pairs * 3 * PAIR), F32),
        ]
        + (
            []
            if before is None
            else [jax.ShapeDtypeStruct((extent // 2, pairs * 3 * PAIR), BF16)]
        ),
        scratch_shapes=[
            pltpu.VMEM((extent, PAIR), F32),
            pltpu.VMEM((extent, PAIR), F32),
            pltpu.VMEM((2, block, PAIR), F32),
        ],
        compiler_params=params(20),
        cost_estimate=cost(5.5 * pairs if before is None else 13 * pairs),
        name="attend_back_%d_%d" % (row0, pair),
    )(*operands, *after)


def norm_two_kernel(
    back_ref, recv_ref, residual_ref, cot_ref, vec_ref, proj_ref, *rest, steps
):
    grad_ref, branch_ref, both_ref, sums_ref = rest[-4:]
    z = back_ref[...].astype(F32) + recv_ref[...].astype(F32)
    unit, factor = normalize(residual_ref[...])
    cot = cot_ref[...].astype(F32)
    grad = cot + norm_back(unit, factor, vec_ref[4:5, :], z)
    grad_ref[...] = grad
    branch = grad.astype(BF16)
    branch_ref[...] = branch
    both_ref[...] = dot(branch, proj_ref[...], NN).astype(BF16)

    @pl.when(pl.program_id(0) == 0)
    def _():
        sums_ref[...] = jnp.zeros(sums_ref.shape, F32)

    for at, part in enumerate((branch.astype(F32), cot, z * unit, z)):
        sums_ref[at : at + 1, :] += jnp.sum(part, axis=0, keepdims=True)


def norm_two(back, recv, residual, cot, vectors, proj, after=()):
    rows, width = back.shape
    steps = 2
    block = rows // steps
    strip = pl.BlockSpec((block, width), lambda i: (i, 0))
    return pl.pallas_call(
        functools.partial(norm_two_kernel, steps=steps),
        grid=(steps,),
        in_specs=[
            strip,
            strip,
            strip,
            strip,
            pl.BlockSpec(vectors.shape, lambda i: (0, 0)),
            pl.BlockSpec(proj.shape, lambda i: (0, 0)),
        ]
        + [ANY_SPACE] * len(after),
        out_specs=[
            strip,
            strip,
            pl.BlockSpec((block, proj.shape[1]), lambda i: (i, 0)),
            pl.BlockSpec((8, width), lambda i: (0, 0)),
        ],
        out_shape=[
            jax.ShapeDtypeStruct((rows, width), F32),
            jax.ShapeDtypeStruct((rows, width), BF16),
            jax.ShapeDtypeStruct((rows, proj.shape[1]), BF16),
            jax.ShapeDtypeStruct((8, width), F32),
        ],
        compiler_params=params(10),
        cost_estimate=cost(4),
        name="norm_two",
    )(back, recv, residual, cot, vectors, proj, *after)


def norm_one_kernel(place_ref, low_ref, high_ref, *refs, terms):
    grads, weights = refs[:terms], refs[terms : 2 * terms]
    own_ref, sent_ref, sums_ref = refs[-3:]
    i = pl.program_id(0)
    z = None
    for grad_ref, weight_ref in zip(grads, weights):
        part = dot(grad_ref[...], weight_ref[...], NT)
        z = part if z is None else z + part
    rows = jnp.where(i == 0, low_ref[...].astype(F32), high_ref[...].astype(F32))
    unit, _ = normalize(rows)

    @pl.when(i == 0)
    def _():
        sums_ref[...] = jnp.zeros(sums_ref.shape, F32)

    sums_ref[0:1, :] += jnp.sum(z * unit, axis=0, keepdims=True)
    sums_ref[1:2, :] += jnp.sum(z, axis=0, keepdims=True)

    @pl.when(i == place_ref[0])
    def _():
        own_ref[...] = z

    @pl.when(i != place_ref[0])
    def _():
        sent_ref[...] = z.astype(BF16)


def norm_one(places, low, high, full, received, own_weights, sib_weights, after=()):
    rows, width = low.shape
    pairs = len(full)
    cols = full[0].shape[1]
    whole = pl.BlockSpec((rows, width), lambda i, at: (0, 0))
    weight_specs = [
        pl.BlockSpec((width, cols), functools.partial(lambda pair, i, at: (0, pair), pair))
        for pair in range(pairs)
    ]
    return pl.pallas_call(
        functools.partial(norm_one_kernel, terms=2 * pairs),
        grid_spec=pltpu.PrefetchScalarGridSpec(
            num_scalar_prefetch=1,
            grid=(2,),
            in_specs=[whole, whole]
            + [pl.BlockSpec((rows, cols), lambda i, at: (2 * i + at[1], 0))] * pairs
            + [pl.BlockSpec((rows, cols), lambda i, at: (i, 0))] * pairs
            + weight_specs * 2
            + [ANY_SPACE] * len(after),
            out_specs=[whole, whole, pl.BlockSpec((8, width), lambda i, at: (0, 0))],
        ),
        out_shape=[
            jax.ShapeDtypeStruct((rows, width), F32),
            jax.ShapeDtypeStruct((rows, width), BF16),
            jax.ShapeDtypeStruct((8, width), F32),
        ],
        compiler_params=params(20),
        cost_estimate=cost(8),
        name="norm_one",
    )(
        places,
        low,
        high,
        *full,
        *received,
        *[own_weights] * pairs,
        *[sib_weights] * pairs,
        *after,
    )


def tie_kernel(value_ref, *rest):
    pass


def tie(value, *after):
    return pl.pallas_call(
        tie_kernel,
        in_specs=[ANY_SPACE] * (1 + len(after)),
        out_specs=ANY_SPACE,
        out_shape=jax.ShapeDtypeStruct(value.shape, value.dtype),
        input_output_aliases={0: 0},
        cost_estimate=cost(0.1),
        name="tie",
    )(value, *after)


def place_kernel(me_ref, *refs, parts, side_rows):
    full_ref = refs[-1]
    rows = refs[0].shape[0] - side_rows
    for k in range(parts):
        at = lax.bitwise_xor(me_ref[0], k)
        full_ref[pl.ds(pl.multiple_of(at * rows, rows), rows), :] = refs[k][0:rows, :]
        if side_rows:
            side = pl.multiple_of(parts * rows + at * side_rows, side_rows)
            full_ref[pl.ds(side, side_rows), :] = refs[k][rows:, :]


def place_shares(me, pieces, side_rows, after):
    total, cols = pieces[0].shape
    parts, kind = len(pieces), pieces[0].dtype
    return pl.pallas_call(
        functools.partial(place_kernel, parts=parts, side_rows=side_rows),
        grid=(1,),
        in_specs=[SCALARS]
        + [pl.BlockSpec((total, cols), lambda i: (0, 0))] * parts
        + [ANY_SPACE] * len(after),
        out_specs=pl.BlockSpec((parts * total, cols), lambda i: (0, 0)),
        out_shape=jax.ShapeDtypeStruct((parts * total, cols), kind),
        compiler_params=params(18),
        cost_estimate=cost(3),
        name="place_shares",
    )(me.reshape(1).astype(jnp.int32), *pieces, *after)


def feed_grads_kernel(*refs, tiles, received):
    normed, cots, grads, acts = refs[0:2], refs[2:4], refs[4:6], refs[6:8]
    out_ref = refs[-1]
    i = pl.program_id(0)

    def work(left, right):
        total = dot(left[0][...], right[0][...], TN) + dot(left[1][...], right[1][...], TN)
        if received:
            total = total + refs[8][...].astype(F32)
        out_ref[...] = total.astype(BF16)

    @pl.when(i < tiles)
    def _():
        work(normed, grads)

    @pl.when(i >= tiles)
    def _():
        work(cots, acts)


def feed_grads(normed, cots, grads, acts, first, received, after=()):
    rows, width = normed[0].shape
    hidden_cols = grads[0].shape[1] // 2
    tile = min(512, hidden_cols)
    tiles = hidden_cols // tile
    base = first // tile
    whole = pl.BlockSpec((rows, width), lambda i: (0, 0))
    grad_spec = pl.BlockSpec((rows, tile), lambda i: (0, base + jnp.minimum(i, tiles - 1)))
    act_spec = pl.BlockSpec((rows, tile), lambda i: (0, base + jnp.maximum(i - tiles, 0)))
    out_spec = pl.BlockSpec((width, tile), lambda i: (0, i))
    return pl.pallas_call(
        functools.partial(feed_grads_kernel, tiles=tiles, received=received is not None),
        grid=(2 * tiles,),
        in_specs=[whole] * 4
        + [grad_spec] * 2
        + [act_spec] * 2
        + ([] if received is None else [out_spec])
        + [ANY_SPACE] * len(after),
        out_specs=out_spec,
        out_shape=jax.ShapeDtypeStruct((width, 2 * hidden_cols), BF16),
        compiler_params=params(24),
        cost_estimate=cost(6),
        name="feed_grads",
    )(*normed, *cots, *grads, *acts, *([] if received is None else [received]), *after)


def weight_grads_kernel(y_ref, normed_ref, grad_ref, *refs, with_proj):
    kept_ref, sent_ref = refs[-2:]
    share = kept_ref.shape[1]
    total = dot(normed_ref[...], grad_ref[...], TN)
    if with_proj:
        low_ref, high_ref, low_mixed_ref, high_mixed_ref, recv_ref = refs[:5]
        proj = dot(low_ref[...], low_mixed_ref[...], TN) + dot(
            high_ref[...], high_mixed_ref[...], TN
        )
        proj = proj + recv_ref[...].astype(F32)
        total = jnp.concatenate([total, proj], axis=1)
    even, odd = total[:share], total[share:]
    stays = y_ref[0] == 0
    kept_ref[0] = jnp.where(stays, even, odd)
    sent_ref[0] = jnp.where(stays, odd, even).astype(BF16)


def weight_grads(y, normed, grads, proj, after=()):
    length, width = normed.shape
    cols = grads.shape[1]
    steps, share = 4, width // 8
    in_specs = [
        SCALARS,
        pl.BlockSpec((length, 2 * share), lambda i: (0, i)),
        pl.BlockSpec((length, cols), lambda i: (0, 0)),
    ]
    operands = [y.reshape(1).astype(jnp.int32), normed, grads]
    total = cols
    if proj is not None:
        branches, mixed, received = proj
        rows, head_cols = mixed[0].shape
        total += head_cols
        in_specs += [pl.BlockSpec((rows, 2 * share), lambda i: (0, i))] * 2
        in_specs += [pl.BlockSpec((rows, head_cols), lambda i: (0, 0))] * 2
        in_specs += [pl.BlockSpec((2 * share, head_cols), lambda i: (i, 0))]
        operands += [*branches, *mixed, received]
    return pl.pallas_call(
        functools.partial(weight_grads_kernel, with_proj=proj is not None),
        grid=(steps,),
        in_specs=in_specs + [ANY_SPACE] * len(after),
        out_specs=[pl.BlockSpec((1, share, total), lambda i: (i, 0, 0))] * 2,
        out_shape=[
            jax.ShapeDtypeStruct((steps, share, total), F32),
            jax.ShapeDtypeStruct((steps, share, total), BF16),
        ],
        compiler_params=params(16),
        cost_estimate=cost(4),
        name="weight_grads",
    )(*operands, *after)


def finish_kernel(*refs, pairs, counts):
    qkv_ref, proj_ref, side_ref, fc_ref, out_ref = refs[-5:]
    feed_ref = refs[sum(counts)]
    hidden_cols = fc_ref.shape[1]
    fc_ref[...] = feed_ref[:, :hidden_cols].astype(F32)
    out_ref[...] = jnp.transpose(feed_ref[:, hidden_cols:].astype(F32))
    at = 0
    for pair in range(pairs):
        total = refs[at][...].astype(F32)
        for part in range(1, counts[pair]):
            total = total + refs[at + part][...].astype(F32)
        at += counts[pair]
        share = qkv_ref.shape[1]
        for j in range(3):
            qkv_ref[j, :, pair * PAIR : (pair + 1) * PAIR] = total[:share, j * PAIR : (j + 1) * PAIR]
        if pair == 0:
            proj_ref[...] = jnp.transpose(total[:share, 3 * PAIR :])
        if pair == pairs - 1:
            side_ref[...] = total[share:, : 3 * PAIR]


def finish(terms, feed_sum, share, head_cols, side_rows, after=()):
    pairs = len(terms)
    flat = [term for pair in terms for term in pair]
    hidden_cols = feed_sum.shape[1] // 2
    return pl.pallas_call(
        functools.partial(
            finish_kernel, pairs=pairs, counts=[len(pair) for pair in terms]
        ),
        grid=(1,),
        in_specs=[pl.BlockSpec(term.shape, lambda i: (0, 0)) for term in flat + [feed_sum]]
        + [ANY_SPACE] * len(after),
        out_specs=[
            pl.BlockSpec((3, share, head_cols), lambda i: (0, 0, 0)),
            pl.BlockSpec((head_cols, share), lambda i: (0, 0)),
            pl.BlockSpec((side_rows, 3 * PAIR), lambda i: (0, 0)),
            pl.BlockSpec((share, hidden_cols), lambda i: (0, 0)),
            pl.BlockSpec((hidden_cols, share), lambda i: (0, 0)),
        ],
        out_shape=[
            jax.ShapeDtypeStruct((3, share, head_cols), F32),
            jax.ShapeDtypeStruct((head_cols, share), F32),
            jax.ShapeDtypeStruct((side_rows, 3 * PAIR), F32),
            jax.ShapeDtypeStruct((share, hidden_cols), F32),
            jax.ShapeDtypeStruct((hidden_cols, share), F32),
        ],
        compiler_params=params(12),
        cost_estimate=cost(3),
        name="finish",
    )(*flat, feed_sum, *after)


def project_kernel(rows_ref, vec_ref, shift_ref, weight_ref, *rest):
    normed_ref, out_ref = rest[-2:]
    unit, _ = normalize(rows_ref[...].astype(F32))
    normed_ref[...] = (unit * vec_ref[2:3, :] + vec_ref[3:4, :]).astype(BF16)
    out_ref[...] = (dot(normed_ref[...], weight_ref[...], NN) + shift_ref[...]).astype(BF16)


def project(sequence, vectors, shift, weights, block, after=()):
    length, width = sequence.shape
    cols = shift.shape[1]
    return pl.pallas_call(
        project_kernel,
        grid=(length // block,),
        in_specs=[
            pl.BlockSpec((block, width), lambda i: (i, 0)),
            pl.BlockSpec(vectors.shape, lambda i: (0, 0)),
            pl.BlockSpec(shift.shape, lambda i: (0, 0)),
            pl.BlockSpec((width, cols), lambda i: (0, 0)),
        ]
        + [ANY_SPACE] * len(after),
        out_specs=[
            pl.BlockSpec((block, width), lambda i: (i, 0)),
            pl.BlockSpec((block, cols), lambda i: (i, 0)),
        ],
        out_shape=[
            jax.ShapeDtypeStruct((length, width), BF16),
            jax.ShapeDtypeStruct((length, cols), BF16),
        ],
        compiler_params=params(16),
        cost_estimate=cost(6),
        name="project",
    )(sequence, vectors, shift, weights, *after)


def feed_kernel(
    base_ref,
    part_ref,
    recv_ref,
    cot_ref,
    vec_ref,
    shift_own_ref,
    shift_sib_ref,
    fc_own_ref,
    out_own_ref,
    fc_sib_ref,
    out_sib_ref,
    *rest,
    tiles,
):
    residual_ref, normed_ref, act_ref, grad_ref, back_ref, sent_ref, sums_ref = rest[-9:-2]
    back_acc, out_acc = rest[-2:]
    i = pl.program_id(0)
    rows = base_ref.shape[0]

    @pl.when(i == 0)
    def _():
        residual = (
            base_ref[...].astype(F32)
            + part_ref[...].astype(F32)
            + recv_ref[...].astype(F32)
            + vec_ref[0:1, :]
        )
        residual_ref[...] = residual
        unit, _ = normalize(residual)
        normed_ref[...] = (unit * vec_ref[4:5, :] + vec_ref[5:6, :]).astype(BF16)
        back_acc[...] = jnp.zeros(back_acc.shape, F32)
        out_acc[...] = jnp.zeros(out_acc.shape, F32)

    def work(shift_ref, fc_ref, out_ref):
        step = rows // 2
        total = None
        for r in range(2):
            at = slice(r * step, (r + 1) * step)
            hidden = dot(normed_ref[at, :], fc_ref[...], NN) + shift_ref[...]
            grad_act = dot(cot_ref[at, :], out_ref[...], NN)
            act, slope = gelu_both(hidden)
            act = act.astype(BF16)
            grad = (grad_act * slope).astype(BF16)
            act_ref[at, :] = act
            grad_ref[at, :] = grad
            part = jnp.sum(grad.astype(F32), axis=0, keepdims=True)
            total = part if total is None else total + part
            back_acc[at, :] += dot(grad, fc_ref[...], NT)
            out_acc[at, :] += dot(act, out_ref[...], NT)
        sums_ref[...] = total

    @pl.when(i < tiles)
    def _():
        work(shift_own_ref, fc_own_ref, out_own_ref)

    @pl.when(i >= tiles)
    def _():
        work(shift_sib_ref, fc_sib_ref, out_sib_ref)

    @pl.when(i == 2 * tiles - 1)
    def _():
        back_ref[...] = back_acc[...].astype(BF16)
        sent_ref[...] = out_acc[...].astype(BF16)


def feed(base, part, recv, cot, vectors, shift_own, shift_sib, own, sib, after=()):
    rows, width = base.shape
    hidden_cols = shift_own.shape[1]
    tile = min(512, hidden_cols)
    tiles = hidden_cols // tile
    whole = pl.BlockSpec((rows, width), lambda i: (0, 0))

    def low(i):
        return jnp.minimum(i, tiles - 1)

    def high(i):
        return jnp.maximum(i - tiles, 0)

    return pl.pallas_call(
        functools.partial(feed_kernel, tiles=tiles),
        grid=(2 * tiles,),
        in_specs=[
            whole,
            whole,
            whole,
            whole,
            pl.BlockSpec(vectors.shape, lambda i: (0, 0)),
            pl.BlockSpec((1, tile), lambda i: (0, low(i))),
            pl.BlockSpec((1, tile), lambda i: (0, high(i))),
            pl.BlockSpec((width, tile), lambda i: (0, low(i))),
            pl.BlockSpec((width, tile), lambda i: (0, tiles + low(i))),
            pl.BlockSpec((width, tile), lambda i: (0, high(i))),
            pl.BlockSpec((width, tile), lambda i: (0, tiles + high(i))),
        ]
        + [ANY_SPACE] * len(after),
        out_specs=[
            whole,
            whole,
            pl.BlockSpec((rows, tile), lambda i: (0, i)),
            pl.BlockSpec((rows, tile), lambda i: (0, i)),
            whole,
            whole,
            pl.BlockSpec((1, tile), lambda i: (0, i)),
        ],
        out_shape=[
            jax.ShapeDtypeStruct((rows, width), F32),
            jax.ShapeDtypeStruct((rows, width), BF16),
            jax.ShapeDtypeStruct((rows, 2 * hidden_cols), BF16),
            jax.ShapeDtypeStruct((rows, 2 * hidden_cols), BF16),
            jax.ShapeDtypeStruct((rows, width), BF16),
            jax.ShapeDtypeStruct((rows, width), BF16),
            jax.ShapeDtypeStruct((1, 2 * hidden_cols), F32),
        ],
        scratch_shapes=[pltpu.VMEM((rows, width), F32), pltpu.VMEM((rows, width), F32)],
        compiler_params=params(32),
        cost_estimate=cost(16),
        name="feed",
    )(
        base, part, recv, cot, vectors, shift_own, shift_sib, own, own, sib, sib, *after
    )


def swap_dp(value, mask):
    size = lax.axis_size("dp")
    return lax.ppermute(value, "dp", [(i, i ^ mask) for i in range(size)])


def gather_z(shard):
    return {k: swap_dp(shard, k) for k in (6, 4, 2)}


def gather_whole(shard, side_rows):
    rows, cols = shard.shape[0] - side_rows, shard.shape[1]
    full = lax.all_gather(shard, "dp", axis=0)
    return jnp.concatenate(
        [full[:, :rows].reshape(-1, cols), full[:, rows:].reshape(-1, cols)], axis=0
    )


def scatter_y(sent, parts):
    return swap_dp(sent, 1) if parts == 8 else None


def scatter_z(kept, sent, received, side, parts):
    if parts != 8:
        whole = jnp.concatenate([kept, sent.astype(F32)], axis=1)
        whole = whole.reshape(parts, -1, whole.shape[2])
        if side is not None:
            whole = jnp.concatenate([whole, side], axis=1)
        return [lax.psum_scatter(whole.astype(BF16), "dp", scatter_dimension=0)]
    sums = kept + received.astype(F32)
    if side is not None:
        sums = jnp.concatenate([sums, side], axis=1)
    z = lax.axis_index("dp") // 2
    terms = [lax.dynamic_index_in_dim(sums, z, 0, keepdims=False)]
    for k in (3, 2, 1):
        sent = lax.dynamic_index_in_dim(sums, z ^ k, 0, keepdims=False).astype(BF16)
        terms.append(swap_dp(sent, 2 * k))
    return terms


def local(
    inputs,
    qkv_weight,
    qv_bias,
    proj_weight,
    proj_bias,
    fc_weight,
    fc_bias,
    out_weight,
    out_bias,
    attn_norm_gain,
    attn_norm_bias,
    mlp_norm_gain,
    mlp_norm_bias,
    cotangent,
):
    width = inputs.shape[1]
    rows = inputs.shape[0]
    share = proj_bias.shape[0]
    parts = width // share
    head_cols = qkv_weight.shape[2]
    pairs = head_cols // PAIR
    qkv_cols = 3 * head_cols
    hidden_cols = fc_weight.shape[1]
    place = lax.axis_index("tensor")
    core = place % 2
    is_low = place < 2
    is_first = core == 0

    def pick_x(low, high):
        return jnp.where(is_low, low, high)

    mlp_shard = jnp.concatenate([fc_weight, out_weight.T], axis=1)
    qv_row = jnp.pad(qv_bias.reshape(-1), (0, share - qv_bias.size))
    vectors = jnp.stack(
        [
            proj_bias,
            out_bias,
            attn_norm_gain,
            attn_norm_bias,
            mlp_norm_gain,
            mlp_norm_bias,
            fc_bias,
            qv_row,
        ]
    )
    qkv_shard = jnp.transpose(
        qkv_weight.reshape(3, share, pairs, PAIR), (1, 2, 0, 3)
    ).reshape(share, qkv_cols)
    attn_shard = jnp.concatenate([qkv_shard, proj_weight.T], axis=1)
    side_rows = 16
    vectors = jnp.pad(
        vectors.reshape(1, -1), ((0, side_rows - 1), (0, attn_shard.shape[1] - vectors.size))
    )
    attn_shard = jnp.concatenate([attn_shard, vectors], axis=0)

    input_x_sent = swap_x(inputs)
    input_core = swap_core(inputs)
    cot_x = swap_x(cotangent)
    blocks = []

    def assemble(late):
        input_x = tie(input_x_sent, *late)
        input_far = swap_core(input_x)
        low, high = pick_x(inputs, input_x), pick_x(input_x, inputs)
        far_low, far_high = pick_x(input_core, input_far), pick_x(input_far, input_core)
        sequence = jnp.concatenate(
            [
                jnp.where(is_first, low, far_low),
                jnp.where(is_first, far_low, low),
                jnp.where(is_first, high, far_high),
                jnp.where(is_first, far_high, high),
            ],
            axis=0,
        )
        blocks.extend([low, high, sequence])
        return (sequence, cot_x)

    if parts == 8:
        shares = {0: attn_shard, **gather_z(attn_shard)}
        mlp_shares = {0: mlp_shard, 1: swap_dp(mlp_shard, 1)}
        for k in (0, 2, 4, 6):
            shares[k + 1] = swap_dp(shares[k], 1)
        behind = (shares[6], shares[5], shares[3], shares[1], mlp_shares[1])
        mlp_shares.update(gather_z(tie(mlp_shard, *(shares[k] for k in (2, 4, 6)))))
        for k in (2, 4):
            mlp_shares[k + 1] = swap_dp(mlp_shares[k], 1)
        attn_all = place_shares(
            lax.axis_index("dp"),
            [shares[k] for k in range(parts)],
            side_rows,
            assemble(behind) + (mlp_shares[2], mlp_shares[4]),
        )
        early = (mlp_shares[3], mlp_shares[5], mlp_shares[6])
    else:
        attn_all = gather_whole(attn_shard, side_rows)
        assemble((attn_all,))
        early = ()
    input_low, input_high, sequence = blocks
    attn_sib = swap_core(attn_all)
    vectors = attn_all[width:].reshape(parts, side_rows, -1)[:, 0, : 8 * share]
    vectors = vectors.reshape(parts, 8, share).transpose(1, 0, 2).reshape(8, width)
    columns = vectors.astype(F32)
    out_shift, gain_one = columns[1:2], columns[2:3]
    fc_shift_own = columns[6:7]
    fc_shift_sib = attn_sib[width:].reshape(parts, side_rows, -1)[:, 0, 6 * share : 7 * share]
    fc_shift_sib = fc_shift_sib.reshape(1, width).astype(F32)
    qv_shift = (
        columns[7]
        .reshape(parts, share)[:, : share // 2]
        .reshape(parts, 2, share // 4)
        .transpose(1, 0, 2)
        .reshape(2, head_cols)
    )
    qkv_shift = jnp.stack([qv_shift[0], jnp.zeros_like(qv_shift[0]), qv_shift[1]])
    qkv_shift = qkv_shift.reshape(3, pairs, PAIR).transpose(1, 0, 2).reshape(1, qkv_cols)
    proj_both = jnp.concatenate(
        [
            attn_all[:width, qkv_cols : qkv_cols + head_cols],
            attn_sib[:width, qkv_cols : qkv_cols + head_cols],
        ],
        axis=1,
    )

    normed_one, qkv = project(sequence, columns, qkv_shift, attn_all, rows)
    cots = [pick_x(cotangent, cot_x), pick_x(cot_x, cotangent)]

    inputs_two = [input_low, input_high]
    mixed, totals, mixed_own, mixed_sib, parts_two, received_two = [], [], [], [], [], []
    for half in range(2):
        half_mixed, half_totals = attend(
            qkv, half * 2 * rows, 2 * rows, rows, after=tuple(parts_two) + early * half
        )
        mixed.append(half_mixed)
        totals.append(half_totals)
        two = half_mixed.reshape(2, rows, head_cols)
        mine = jnp.where(is_first, two[0], two[1])
        received = swap_core(jnp.where(is_first, two[1], two[0]))
        both = jnp.concatenate([mine, received], axis=1)
        mixed_own.append(mine)
        mixed_sib.append(received)
        part = dot(both, proj_both, NT).astype(BF16)
        parts_two.append(part)
        received_two.append(swap_x(part))
    if parts == 8:
        mlp_shares[7] = swap_dp(mlp_shares[6], 1)
        mlp_all = place_shares(
            lax.axis_index("dp"),
            [mlp_shares[k] for k in range(parts)],
            0,
            (received_two[0], parts_two[1]),
        )
    else:
        mlp_all = gather_whole(mlp_shard, 0)
    mlp_sib = swap_core(mlp_all)
    residuals, normed_two, acts, grads_hidden, backs, out_parts = [], [], [], [], [], []
    fc_bias_sums = 0.0
    for half in range(2):
        residual, normed, act, grad_hidden, back, out_part, sums = feed(
            inputs_two[half],
            parts_two[half],
            received_two[half],
            cots[half],
            columns,
            fc_shift_own,
            fc_shift_sib,
            mlp_all,
            mlp_sib,
            after=(parts_two[1],),
        )
        residuals.append(residual)
        normed_two.append(normed)
        acts.append(act)
        grads_hidden.append(grad_hidden)
        backs.append(back)
        out_parts.append(out_part)
        fc_bias_sums = fc_bias_sums + sums[0]
    back_recv = [swap_x(back) for back in backs]

    sib_grads = feed_grads(
        normed_two, cots, grads_hidden, acts, hidden_cols, None, after=(back_recv[0],)
    )
    grad_mlp = feed_grads(normed_two, cots, grads_hidden, acts, 0, swap_core(sib_grads))
    mlp_sum = lax.psum_scatter(grad_mlp, "dp", scatter_dimension=0, tiled=True)

    grad_residuals, branches, grads_mixed = [], [], []
    for half in range(2):
        grad_residual, branch, grad_both, sums_two = norm_two(
            backs[half],
            back_recv[half],
            residuals[half],
            cots[half],
            columns,
            proj_both,
            after=(sib_grads,) if half == 0 else (grad_mlp, low_grads),
        )
        grad_residuals.append(grad_residual)
        branches.append(branch)
        mine = grad_both[:, :head_cols]
        received = swap_core(grad_both[:, head_cols:])
        grads_mixed.append(
            jnp.concatenate(
                [jnp.where(is_first, mine, received), jnp.where(is_first, received, mine)], axis=0
            )
        )
        vec_two = sums_two if half == 0 else vec_two + sums_two
        if half == 0:
            low_grads, _ = attend_back(
                qkv,
                mixed[0],
                grads_mixed[0],
                totals[0],
                None,
                0,
                rows,
                0,
                pairs,
                after=(grad_mlp,),
            )
    proj_sib = dot(branches[0], mixed_sib[0], TN) + dot(branches[1], mixed_sib[1], TN)
    proj_received = swap_core(proj_sib.astype(BF16))

    out_sent = tie(pick_x(out_parts[1], out_parts[0]), low_grads)
    out_recv = swap_x(out_sent)

    y = lax.axis_index("dp") % 2 if parts == 8 else jnp.zeros((), jnp.int32)
    place_ids = jnp.stack([place // 2, core]).astype(jnp.int32)
    full_grads, grads_received, side_sums, exchanges = [], [], [], []
    after = ()
    for pair in range(pairs):
        grad_pair, pair_sums, grad_sent = attend_back(
            qkv,
            mixed[1],
            grads_mixed[1],
            totals[1],
            low_grads,
            2 * rows,
            rows,
            pair,
            1,
            after=after,
            core=core,
        )
        full_grads.append(grad_pair)
        side_sums.append(pair_sums)
        if pair > 0 and parts == 8:
            grad_sent = tie(grad_sent, exchanges[-1][2])
        grads_received.append(swap_core(grad_sent))
        proj = (branches, mixed_own, proj_received) if pair == 0 else None
        if pair == 0:
            out_recv = tie(out_recv, grad_pair)
        kept, sent = weight_grads(y, normed_one, grad_pair, proj)
        received = scatter_y(sent, parts) if pair < pairs - 1 else None
        exchanges.append((kept, sent, received))
        after = (sent, out_recv)

    z_own, z_sent, vec_one = norm_one(
        place_ids,
        input_low,
        input_high,
        full_grads,
        grads_received,
        attn_all,
        attn_sib,
        after=(exchanges[-1][1],),
    )
    first_terms = scatter_z(*exchanges[0], side=None, parts=parts)
    z_recv = swap_x(z_sent)
    vec_two = vec_two + swap_core(vec_two)
    fc_bias_grad = fc_bias_sums[:hidden_cols] + swap_core(fc_bias_sums[hidden_cols:])

    vec_grads = jnp.concatenate(
        [
            vec_two[:2],
            vec_one[:2],
            vec_two[2:4],
            fc_bias_grad[None],
            jnp.zeros((1, width), F32),
        ],
        axis=0,
    )
    vec_blocks = vec_grads.reshape(8, parts, share).transpose(1, 0, 2)
    vec_blocks = jnp.pad(vec_blocks, ((0, 0), (0, 0), (0, 3 * PAIR - share)))
    pair_rows = jnp.pad(jnp.concatenate(side_sums, axis=0), ((0, 8 - pairs), (0, 0)))
    side = jnp.concatenate(
        [vec_blocks, jnp.broadcast_to(pair_rows[None], (parts, 8, 3 * PAIR))], axis=1
    )
    if parts == 8:
        views = side.reshape((parts // 2, 2) + side.shape[1:])
        side_kept = lax.dynamic_index_in_dim(views, y, 1, keepdims=False)
        side_sent = lax.dynamic_index_in_dim(views, 1 - y, 1, keepdims=False)
        side = side_kept + swap_dp(side_sent, 1)
    terms = [first_terms]
    for pair in range(1, pairs):
        kept, sent, received = exchanges[pair]
        last = pair == pairs - 1
        if last:
            received = scatter_y(tie(sent, z_sent), parts)
        terms.append(scatter_z(kept, sent, received, side if last else None, parts))

    qkv_out, proj_out, six, fc_out, out_out = finish(
        terms, mlp_sum, share, head_cols, side_rows, after=(z_sent,)
    )
    out_recv = tie(out_recv, six)
    out_mine = pick_x(out_parts[0], out_parts[1])
    outputs = (
        pick_x(residuals[0], residuals[1])
        + out_mine.astype(F32)
        + out_recv.astype(F32)
        + out_shift
    ).astype(BF16)

    unit, factor = normalize(inputs.astype(F32))
    z_own = z_own + tie(z_recv, six).astype(F32)
    grad_inputs = (
        pick_x(grad_residuals[0], grad_residuals[1]) + norm_back(unit, factor, gain_one, z_own)
    ).astype(BF16)
    one = six[2:4, :share]
    far = lax.ppermute(one, "tensor", [(i, i ^ 3) for i in range(4)])
    two = one + swap_core(one) + swap_x(one) + far
    piece = share // 4
    start = lax.axis_index("dp") * piece
    mine = lax.dynamic_index_in_dim(six[8 : 8 + pairs], start // PAIR, 0, keepdims=False)
    qv_out = lax.dynamic_slice_in_dim(mine.reshape(3, PAIR), start % PAIR, piece, 1)[0::2]
    return (
        outputs,
        grad_inputs,
        qkv_out,
        qv_out,
        proj_out,
        six[0, :share],
        fc_out,
        six[6, :share],
        out_out,
        six[1, :share],
        two[0],
        two[1],
        six[4, :share],
        six[5, :share],
    )


def solution(mesh):
    rows = P(("dp", "tensor"), None)
    vector = P("dp")
    wide = P(("tensor", "dp"))
    weights = (
        P(None, "dp", "tensor"),
        P(None, ("tensor", "dp")),
        P("tensor", "dp"),
        vector,
        P("dp", "tensor"),
        wide,
        P("tensor", "dp"),
        vector,
        vector,
        vector,
        vector,
        vector,
    )
    return jax.shard_map(
        local,
        mesh=mesh,
        in_specs=(rows, *weights, rows),
        out_specs=(rows, rows, *weights),
        check_vma=False,
    )
```

profile of v0, /device:TPU:0, one launch (start us, length us, event | category | flops | bytes accessed | tf_op | source)
XLA Modules:
  0.0 399.2 jit_solution(6923643727026199778)
XLA Ops:
  7.2 3.0 collective-permute-start
  14.0 3.7 collective-permute-start.1
  21.2 4.7 %collective-permute-done.1.rest_0_.rest_2_.refs_6_ = bf16[144,1024]{1,0:T(8,128)(2,1)S(1)} collective-permute-done((bf16[144,1024]{1,0:T(8,128)(2,1)S(1)}, bf16[144,1024]{1,0:T(8,128)(2,1)S(1)}, u32[]{:S(2)}, u32[]{:S(2)}) %collective-permute-start.1) | collective-permute-done | bytes 294944 | tf_op jit(solution)/shard_map/ppermute | solution.py:766
  27.4 15.1 %collective-permute-done.2.rest_1_.refs_4_ = bf16[144,1024]{1,0:T(8,128)(2,1)S(1)} collective-permute-done((bf16[144,1024]{1,0:T(8,128)(2,1)S(1)}, bf16[144,1024]{1,0:T(8,128)(2,1)S(1)}, u32[]{:S(2)}, u32[]{:S(2)}) %collective-permute-start.2) | collective-permute-done | bytes 294944 | tf_op jit(solution)/shard_map/ppermute | solution.py:766
  44.6 7.9 %collective-permute-done.3.rest_1_.refs_5_ = bf16[144,1024]{1,0:T(8,128)(2,1)S(1)} collective-permute-done((bf16[144,1024]{1,0:T(8,128)(2,1)S(1)}, bf16[144,1024]{1,0:T(8,128)(2,1)S(1)}, u32[]{:S(2)}, u32[]{:S(2)}) %collective-permute-start.3) | collective-permute-done | bytes 294944 | tf_op jit(solution)/shard_map/ppermute | solution.py:766
  52.5 4.4 %collective-permute-done.5.rest_2_.refs_3_ = bf16[144,1024]{1,0:T(8,128)(2,1)S(1)} collective-permute-done((bf16[144,1024]{1,0:T(8,128)(2,1)S(1)}, bf16[144,1024]{1,0:T(8,128)(2,1)S(1)}, u32[]{:S(2)}, u32[]{:S(2)}) %collective-permute-start.5) | collective-permute-done | bytes 294944 | tf_op jit(solution)/shard_map/ppermute | solution.py:766
  70.1 14.4 %collective-permute-done.12.refs_10_.refs_2_ = bf16[128,2048]{1,0:T(8,128)(2,1)} collective-permute-done((bf16[128,2048]{1,0:T(8,128)(2,1)}, bf16[128,2048]{1,0:T(8,128)(2,1)}, u32[]{:S(2)}, u32[]{:S(2)}) %collective-permute-start.12) | collective-permute-done | bytes 524320 | tf_op jit(solution)/shard_map/ppermute | solution.py:766
  96.2 6.1 %project.1 = (bf16[2048,1024]{1,0:T(8,128)(2,1)S(1)}, bf16[2048,768]{1,0:T(8,128)(2,1)S(1)}) custom-call(bf16[2048,1024]{1,0:T(8,128)(2,1)S(1)} %copy-done.6, f32[8,1024]{1,0:T(8,128)S(1)} %bitcast.99, f32[1,768]{1,0:T(1,128)S(1)} %reshape.159.shift_ref, bf16[1152,1024]{1,0:T(8,128)(2,1)S(1)} %place_shares.2.weight_ref.refs_4_.refs_5_), custom_call_target="tpu_custom_call" | custom-call | flops 1650000000 | bytes 1500000 | tf_op jit(solution)/shard_map/project/pallas_call | solution.py:617
  102.3 5.7 %attend_0.1 = (bf16[1024,256]{1,0:T(8,128)(2,1)S(1)}, f32[2,2,1024]{2,1,0:T(2,128)S(1)}) custom-call(bf16[2048,768]{1,0:T(8,128)(2,1)S(1)} %get-tuple-element.61.qkv_ref), custom_call_target="tpu_custom_call" | custom-call | flops 1650000000 | bytes 1500000 | tf_op jit(solution)/shard_map/attend_0/pallas_call | solution.py:136
  113.5 3.8 collective-permute-done.18.rest_2_.refs_5_
  117.3 15.5 %attend_1024.1 = (bf16[1024,256]{1,0:T(8,128)(2,1)S(1)}, f32[2,2,1024]{2,1,0:T(2,128)S(1)}) custom-call(bf16[2048,768]{1,0:T(8,128)(2,1)S(1)} %get-tuple-element.61.qkv_ref, bf16[512,1024]{1,0:T(8,128)(2,1)S(1)} %convolution_convert_fusion.1.rest_0_.part_ref, bf16[128,2048]{1,0:T(8,128)(2,1)} %collective-permute-done.17.rest_1_.refs_3_, ...), custom_call_target="tpu_custom_call" | custom-call | flops 4400000000 | bytes 4000000 | tf_op jit(solution)/shard_map/attend_1024/pallas_call | solution.py:136
  142.1 4.4 %collective-permute-done.22.fc_sib_ref.out_sib_ref = bf16[1024,2048]{1,0:T(8,128)(2,1)S(1)} collective-permute-done((bf16[1024,2048]{1,0:T(8,128)(2,1)S(1)}, bf16[1024,2048]{1,0:T(8,128)(2,1)S(1)}, u32[]{:S(2)}, u32[]{:S(2)}) %collective-permute-start.22) | collective-permute-done | bytes 4194336 | tf_op jit(solution)/shard_map/ppermute | solution.py:40
  148.5 15.5 %feed.2 = (f32[512,1024]{1,0:T(8,128)S(1)}, bf16[512,1024]{1,0:T(8,128)(2,1)S(1)}, bf16[512,2048]{1,0:T(8,128)(2,1)S(1)}, bf16[512,2048]{1,0:T(8,128)(2,1)S(1)},...) custom-call(bf16[512,1024]{1,0:T(8,128)(2,1)S(1)} %copy-done.12, ...), custom_call_target="tpu_custom_call" | custom-call | flops 4400000000 | bytes 4000000 | tf_op jit(solution)/shard_map/feed/pallas_call | solution.py:720
  173.7 14.7 %feed.3 = (f32[512,1024]{1,0:T(8,128)S(1)}, bf16[512,1024]{1,0:T(8,128)(2,1)S(1)}, bf16[512,2048]{1,0:T(8,128)(2,1)S(1)}, bf16[512,2048]{1,0:T(8,128)(2,1)S(1)},...) custom-call(bf16[512,1024]{1,0:T(8,128)(2,1)S(1)} %copy-done.15, ...), custom_call_target="tpu_custom_call" | custom-call | flops 4400000000 | bytes 4000000 | tf_op jit(solution)/shard_map/feed/pallas_call | solution.py:720
  188.4 4.6 %collective-permute-done.24.refs_8_.recv_ref = bf16[512,1024]{1,0:T(8,128)(2,1)S(1)} collective-permute-done((bf16[512,1024]{1,0:T(8,128)(2,1)S(1)}, bf16[512,1024]{1,0:T(8,128)(2,1)S(1)}, u32[]{:S(2)}, u32[]{:S(2)}) %collective-permute-start.24) | collective-permute-done | bytes 1048608 | tf_op jit(solution)/shard_map/ppermute | solution.py:36
  193.0 5.9 %feed_grads.2.rest_0_ = bf16[1024,2048]{1,0:T(8,128)(2,1)S(1)} custom-call(bf16[512,1024]{1,0:T(8,128)(2,1)S(1)} %get-tuple-element.69.refs_0_, bf16[512,1024]{1,0:T(8,128)(2,1)S(1)} %get-tuple-element.70.refs_1_, bf16[512,1024]{1,0:T(8,128)(2,1)S(1)} %get-tuple-element.116.cot_ref.refs_2_, bf16[512,1024]{1,0:T(8,128)(2,1)S(1)} %get-tuple-element.117.cot_ref.refs_3_, ...), custom_call_target="tpu_custom_call" | custom-call | flops 1650000000 | bytes 1500000 | tf_op jit(solution)/shard_map/feed_grads/pallas_call | solution.py:488
  201.1 5.1 %collective-permute-done.26.refs_8_ = bf16[1024,2048]{1,0:T(8,128)(2,1)S(1)} collective-permute-done((bf16[1024,2048]{1,0:T(8,128)(2,1)S(1)}, bf16[1024,2048]{1,0:T(8,128)(2,1)S(1)}, u32[]{:S(2)}, u32[]{:S(2)}) %collective-permute-start.26) | collective-permute-done | bytes 4194336 | tf_op jit(solution)/shard_map/ppermute | solution.py:40
  207.8 6.5 %feed_grads.3.rest_0_ = bf16[1024,2048]{1,0:T(8,128)(2,1)S(1)} custom-call(bf16[512,1024]{1,0:T(8,128)(2,1)S(1)} %get-tuple-element.69.refs_0_, bf16[512,1024]{1,0:T(8,128)(2,1)S(1)} %get-tuple-element.70.refs_1_, bf16[512,1024]{1,0:T(8,128)(2,1)S(1)} %get-tuple-element.116.cot_ref.refs_2_, bf16[512,1024]{1,0:T(8,128)(2,1)S(1)} %get-tuple-element.117.cot_ref.refs_3_, ...), custom_call_target="tpu_custom_call" | custom-call | flops 1650000000 | bytes 1500000 | tf_op jit(solution)/shard_map/feed_grads/pallas_call | solution.py:488
  228.2 3.0 norm_two.2
  236.5 10.9 %attend_back_0_0.1 = (f32[1024,768]{1,0:T(8,128)S(1)}, f32[1,768]{1,0:T(1,128)}) custom-call(s32[1]{0:T(128)} %constant.110.clone.1.core_ref, bf16[2048,768]{1,0:T(8,128)(2,1)S(1)} %copy-done.99, bf16[1024,256]{1,0:T(8,128)(2,1)S(1)} %copy-done.94, bf16[1024,256]{1,0:T(8,128)(2,1)S(1)} %pad_maximum_fusion.3.grad_ref, ...), custom_call_target="tpu_custom_call" | custom-call | flops 3024999936 | bytes 2750000 | tf_op jit(solution)/shard_map/attend_back_0_0/pallas_call | solution.py:259
  258.6 4.1 %norm_two.3 = (f32[512,1024]{1,0:T(8,128)S(1)}, bf16[512,1024]{1,0:T(8,128)(2,1)S(1)}, bf16[512,512]{1,0:T(8,128)(2,1)S(1)}, f32[8,1024]{1,0:T(8,128)S(1)}) custom-call(bf16[512,1024]{1,0:T(8,128)(2,1)S(1)} %copy-done.84, bf16[512,1024]{1,0:T(8,128)(2,1)} %collective-permute-done.28.recv_ref, f32[512,1024]{1,0:T(8,128)S(1)} %copy-done.38, ...), custom_call_target="tpu_custom_call" | custom-call | flops 1100000000 | bytes 1000000 | tf_op jit(solution)/shard_map/norm_two/pallas_call | solution.py:316
  267.0 13.1 %attend_back_1024_0.1 = (bf16[2048,384]{1,0:T(8,128)(2,1)S(1)}, f32[1,384]{1,0:T(1,128)S(1)}, bf16[1024,384]{1,0:T(8,128)(2,1)S(1)}) custom-call(s32[1]{0:T(128)} %bitcast.27.core_ref, bf16[2048,768]{1,0:T(8,128)(2,1)S(1)} %copy-done.100, bf16[1024,256]{1,0:T(8,128)(2,1)S(1)} %copy-done.91, bf16[1024,256]{1,0:T(8,128)(2,1)S(1)} %pad_maximum_fusion.4.grad_ref, ...), custom_call_target="tpu_custom_call" | custom-call | flops 3575000064 | bytes 3250000 | tf_op jit(solution)/shard_map/attend_back_1024_0/pallas_call | solution.py:259
  280.1 5.2 %weight_grads.2 = (f32[4,128,640]{2,1,0:T(8,128)S(1)}, bf16[4,128,640]{2,1,0:T(8,128)(2,1)}) custom-call(s32[1]{0:T(128)} %bitcast.28.y_ref, bf16[2048,1024]{1,0:T(8,128)(2,1)S(1)} %copy-done.18, bf16[2048,384]{1,0:T(8,128)(2,1)S(1)} %get-tuple-element.81.rest_0_.grad_ref.refs_0_, bf16[512,1024]{1,0:T(8,128)(2,1)S(1)} %copy-done.45, ...), custom_call_target="tpu_custom_call" | custom-call | flops 1100000000 | bytes 1000000 | tf_op jit(solution)/shard_map/weight_grads/pallas_call | solution.py:540
  295.0 13.1 %attend_back_1024_1.1 = (bf16[2048,384]{1,0:T(8,128)(2,1)S(1)}, f32[1,384]{1,0:T(1,128)S(1)}, bf16[1024,384]{1,0:T(8,128)(2,1)S(1)}) custom-call(s32[1]{0:T(128)} %bitcast.27.core_ref, bf16[2048,768]{1,0:T(8,128)(2,1)S(1)} %copy-done.101, bf16[1024,256]{1,0:T(8,128)(2,1)S(1)} %copy-done.92, bf16[1024,256]{1,0:T(8,128)(2,1)S(1)} %copy-done.89, ...), custom_call_target="tpu_custom_call" | custom-call | flops 3575000064 | bytes 3250000 | tf_op jit(solution)/shard_map/attend_back_1024_1/pallas_call | solution.py:259
  314.8 3.6 weight_grads.3
  323.0 6.3 %collective-permute-start.33 = (bf16[128,640]{1,0:T(8,128)(2,1)}, bf16[128,640]{1,0:T(8,128)(2,1)}, u32[]{:S(2)}, u32[]{:S(2)}) collective-permute-start(bf16[128,640]{1,0:T(8,128)(2,1)} %get-tuple-element.121), channel_id=1, source_target_pairs={{0,16},{4,20},{8,24},{12,28},{16,0},{20,4},{24,8},{28,12},{1,17},{... | collective-permute-start | bytes 491528 | tf_op jit(solution)/shard_map/ppermute | solution.py:766
  329.5 9.9 %norm_one.1 = (f32[512,1024]{1,0:T(8,128)S(1)}, bf16[512,1024]{1,0:T(8,128)(2,1)}, f32[8,1024]{1,0:T(8,128)S(1)}) custom-call(s32[2]{0:T(128)S(1)} %pad_add_fusion.place_ref, bf16[512,1024]{1,0:T(8,128)(2,1)S(1)} %copy-done.13, bf16[512,1024]{1,0:T(8,128)(2,1)S(1)} %copy-done.16, bf16[2048,384]{1,0:T(8,128)(2,1)S(1)} %copy-done.21, ...), custom_call_target="tpu_custom_call" | custom-call | flops 2200000000 | bytes 2000000 | tf_op jit(solution)/shard_map/norm_one/pallas_call | solution.py:382
  346.7 7.9 %collective-permute-done.40 = f32[4,16,384]{2,1,0:T(8,128)S(1)} collective-permute-done((f32[4,16,384]{2,1,0:T(8,128)S(1)}, f32[4,16,384]{2,1,0:T(8,128)S(1)}, u32[]{:S(2)}, u32[]{:S(2)}) %collective-permute-start.40) | collective-permute-done | bytes 98336 | tf_op jit(solution)/shard_map/ppermute | solution.py:766
  360.8 2.6 collective-permute-done.41.refs_5_
  364.0 3.1 collective-permute-done.42.refs_6_
  378.8 3.1 add_convert_fusion
  386.3 3.6 fusion.8
  (427 shorter events, 152.9 us)
Async XLA Ops:
  7.2 361.2 %reduce-scatter.2.cloned.1.call-start = ((), (), s32[]{:S(2)}) async-start(), calls=%async_computation.1 | async-start | bytes 4718592 | tf_op jit(solution)/shard_map/reduce_scatter | solution.py:986
  7.2 49.6 %collective-permute-start = (bf16[512,1024]{1,0:T(8,128)(2,1)}, bf16[512,1024]{1,0:T(8,128)(2,1)}, u32[]{:S(2)}, u32[]{:S(2)}) collective-permute-start(bf16[512,1024]{1,0:T(8,128)(2,1)} %param.14), channel_id=1, source_target_pairs={{0,2},{2,0},{1,3},{3,1},{4,6},{6,4},{5,7},{7,5},{8,10},{10,8},{9,1... | collective-permute-start | bytes 3145736 | tf_op jit(solution)/shard_map/ppermute | solution.py:36
  17.7 24.8 %collective-permute-start.2 = (bf16[144,1024]{1,0:T(8,128)(2,1)S(1)}, bf16[144,1024]{1,0:T(8,128)(2,1)S(1)}, u32[]{:S(2)}, u32[]{:S(2)}) collective-permute-start(bf16[144,1024]{1,0:T(8,128)(2,1)S(1)} %fusion.19.refs_0_), channel_id=1, source_target_pairs={{0,16},{4,20},{8,24},{12,28},{16,0},{20,4},{24,8},{28,12},{1,17},{... | collective-permute-start | bytes 884744 | tf_op jit(solution)/shard_map/ppermute | solution.py:766
  17.7 26.4 %collective-permute-start.4 = (bf16[144,1024]{1,0:T(8,128)(2,1)S(1)}, bf16[144,1024]{1,0:T(8,128)(2,1)S(1)}, u32[]{:S(2)}, u32[]{:S(2)}) collective-permute-start(bf16[144,1024]{1,0:T(8,128)(2,1)S(1)} %fusion.19.refs_0_), channel_id=1, source_target_pairs={{0,8},{4,12},{8,0},{12,4},{16,24},{20,28},{24,16},{28,20},{1,9},{5... | collective-permute-start | bytes 884744 | tf_op jit(solution)/shard_map/ppermute | solution.py:766
  19.6 25.0 %collective-permute-start.7 = (bf16[128,2048]{1,0:T(8,128)(2,1)S(1)}, bf16[128,2048]{1,0:T(8,128)(2,1)S(1)}, u32[]{:S(2)}, u32[]{:S(2)}) collective-permute-start(bf16[128,2048]{1,0:T(8,128)(2,1)S(1)} %pad_maximum_fusion.2.refs_0_), channel_id=1, source_target_pairs={{0,4},{4,0},{8,12},{12,8},{16,20},{20,16},{24,28},{28,24},{1,5},{5... | collective-permute-start | bytes 1572872 | tf_op jit(solution)/shard_map/ppermute | solution.py:766
  25.9 18.7 %collective-permute-start.6 = (bf16[144,1024]{1,0:T(8,128)(2,1)S(1)}, bf16[144,1024]{1,0:T(8,128)(2,1)S(1)}, u32[]{:S(2)}, u32[]{:S(2)}) collective-permute-start(bf16[144,1024]{1,0:T(8,128)(2,1)S(1)} %fusion.19.refs_0_), channel_id=1, source_target_pairs={{0,4},{4,0},{8,12},{12,8},{16,20},{20,16},{24,28},{28,24},{1,5},{5... | collective-permute-start | bytes 884744 | tf_op jit(solution)/shard_map/ppermute | solution.py:766
  44.6 16.9 %collective-permute-start.8 = (bf16[512,1024]{1,0:T(8,128)(2,1)}, bf16[512,1024]{1,0:T(8,128)(2,1)}, u32[]{:S(2)}, u32[]{:S(2)}) collective-permute-start(bf16[512,1024]{1,0:T(8,128)(2,1)} %param.14), channel_id=1, source_target_pairs={{0,1},{1,0},{2,3},{3,2},{4,5},{5,4},{6,7},{7,6},{8,9},{9,8},{10,11... | collective-permute-start | bytes 3145736 | tf_op jit(solution)/shard_map/ppermute | solution.py:40
  57.6 28.3 %collective-permute-start.11 = (bf16[512,1024]{1,0:T(8,128)(2,1)}, bf16[512,1024]{1,0:T(8,128)(2,1)S(1)}, u32[]{:S(2)}, u32[]{:S(2)}) collective-permute-start(bf16[512,1024]{1,0:T(8,128)(2,1)} %param.27), channel_id=1, source_target_pairs={{0,2},{2,0},{1,3},{3,1},{4,6},{6,4},{5,7},{7,5},{8,10},{10,8},{9,1... | collective-permute-start | bytes 3145736 | tf_op jit(solution)/shard_map/ppermute | solution.py:36
  58.9 25.6 %collective-permute-start.12 = (bf16[128,2048]{1,0:T(8,128)(2,1)}, bf16[128,2048]{1,0:T(8,128)(2,1)}, u32[]{:S(2)}, u32[]{:S(2)}) collective-permute-start(bf16[128,2048]{1,0:T(8,128)(2,1)} %tie.9), channel_id=1, source_target_pairs={{0,8},{4,12},{8,0},{12,4},{16,24},{20,28},{24,16},{28,20},{1,9},{5... | collective-permute-start | bytes 1572872 | tf_op jit(solution)/shard_map/ppermute | solution.py:766
  59.6 26.3 %collective-permute-start.13 = (bf16[128,2048]{1,0:T(8,128)(2,1)}, bf16[128,2048]{1,0:T(8,128)(2,1)}, u32[]{:S(2)}, u32[]{:S(2)}) collective-permute-start(bf16[128,2048]{1,0:T(8,128)(2,1)} %tie.9), channel_id=1, source_target_pairs={{0,16},{4,20},{8,24},{12,28},{16,0},{20,4},{24,8},{28,12},{1,17},{... | collective-permute-start | bytes 1572872 | tf_op jit(solution)/shard_map/ppermute | solution.py:766
  88.3 21.6 %collective-permute-start.15 = (bf16[1152,1024]{1,0:T(8,128)(2,1)S(1)}, bf16[1152,1024]{1,0:T(8,128)(2,1)}, u32[]{:S(2)}, u32[]{:S(2)}) collective-permute-start(bf16[1152,1024]{1,0:T(8,128)(2,1)S(1)} %place_shares.2.weight_ref.refs_4_.refs_5_), channel_id=1, source_target_pairs={{0,1},{1,0},{2,3},{3,2},{4,5},{5,4},{6,7},{7,6},{8,9},{9,8},{10,11... | collective-permute-start | bytes 7077896 | tf_op jit(solution)/shard_map/ppermute | solution.py:40
  88.4 19.8 %collective-permute-start.19 = (bf16[128,2048]{1,0:T(8,128)(2,1)}, bf16[128,2048]{1,0:T(8,128)(2,1)}, u32[]{:S(2)}, u32[]{:S(2)}) collective-permute-start(bf16[128,2048]{1,0:T(8,128)(2,1)} %tie.9), channel_id=1, source_target_pairs={{0,24},{4,28},{8,16},{12,20},{16,8},{20,12},{24,0},{28,4},{1,25},{... | collective-permute-start | bytes 1572872 | tf_op jit(solution)/shard_map/ppermute | solution.py:766
  91.0 22.5 %collective-permute-start.17 = (bf16[128,2048]{1,0:T(8,128)(2,1)}, bf16[128,2048]{1,0:T(8,128)(2,1)}, u32[]{:S(2)}, u32[]{:S(2)}) collective-permute-start(bf16[128,2048]{1,0:T(8,128)(2,1)} %collective-permute-done.12.refs_10_.refs_2_), channel_id=1, source_target_pairs={{0,4},{4,0},{8,12},{12,8},{16,20},{20,16},{24,28},{28,24},{1,5},{5... | collective-permute-start | bytes 1572872 | tf_op jit(solution)/shard_map/ppermute | solution.py:766
  92.5 24.8 %collective-permute-start.18 = (bf16[128,2048]{1,0:T(8,128)(2,1)}, bf16[128,2048]{1,0:T(8,128)(2,1)}, u32[]{:S(2)}, u32[]{:S(2)}) collective-permute-start(bf16[128,2048]{1,0:T(8,128)(2,1)} %collective-permute-done.13.refs_11_.refs_4_), channel_id=1, source_target_pairs={{0,4},{4,0},{8,12},{12,8},{16,20},{20,16},{24,28},{28,24},{1,5},{5... | collective-permute-start | bytes 1572872 | tf_op jit(solution)/shard_map/ppermute | solution.py:766
  108.2 27.1 %collective-permute-start.20 = (bf16[128,2048]{1,0:T(8,128)(2,1)}, bf16[128,2048]{1,0:T(8,128)(2,1)S(1)}, u32[]{:S(2)}, u32[]{:S(2)}) collective-permute-start(bf16[128,2048]{1,0:T(8,128)(2,1)} %collective-permute-done.19.rest_3_.refs_6_), channel_id=1, source_target_pairs={{0,4},{4,0},{8,12},{12,8},{16,20},{20,16},{24,28},{28,24},{1,5},{5... | collective-permute-start | bytes 1572872 | tf_op jit(solution)/shard_map/ppermute | solution.py:766
  111.9 25.3 %collective-permute-start.16 = (bf16[512,1024]{1,0:T(8,128)(2,1)S(1)}, bf16[512,1024]{1,0:T(8,128)(2,1)S(1)}, u32[]{:S(2)}, u32[]{:S(2)}) collective-permute-start(bf16[512,1024]{1,0:T(8,128)(2,1)S(1)} %convolution_convert_fusion.1.rest_0_.part_ref), channel_id=1, source_target_pairs={{0,2},{2,0},{1,3},{3,1},{4,6},{6,4},{5,7},{7,5},{8,10},{10,8},{9,1... | collective-permute-start | bytes 3145736 | tf_op jit(solution)/shard_map/ppermute | solution.py:36
  140.5 28.8 %collective-permute-start.23 = (bf16[512,1024]{1,0:T(8,128)(2,1)S(1)}, bf16[512,1024]{1,0:T(8,128)(2,1)S(1)}, u32[]{:S(2)}, u32[]{:S(2)}) collective-permute-start(bf16[512,1024]{1,0:T(8,128)(2,1)S(1)} %convolution_convert_fusion.refs_9_.rest_0_.part_ref), channel_id=1, source_target_pairs={{0,2},{2,0},{1,3},{3,1},{4,6},{6,4},{5,7},{7,5},{8,10},{10,8},{9,1... | collective-permute-start | bytes 3145736 | tf_op jit(solution)/shard_map/ppermute | solution.py:36
  167.8 25.2 %collective-permute-start.24 = (bf16[512,1024]{1,0:T(8,128)(2,1)S(1)}, bf16[512,1024]{1,0:T(8,128)(2,1)S(1)}, u32[]{:S(2)}, u32[]{:S(2)}) collective-permute-start(bf16[512,1024]{1,0:T(8,128)(2,1)S(1)} %get-tuple-element.68.back_ref), channel_id=1, source_target_pairs={{0,2},{2,0},{1,3},{3,1},{4,6},{6,4},{5,7},{7,5},{8,10},{10,8},{9,1... | collective-permute-start | bytes 3145736 | tf_op jit(solution)/shard_map/ppermute | solution.py:36
  222.6 27.1 %collective-permute-start.28 = (bf16[512,1024]{1,0:T(8,128)(2,1)}, bf16[512,1024]{1,0:T(8,128)(2,1)}, u32[]{:S(2)}, u32[]{:S(2)}) collective-permute-start(bf16[512,1024]{1,0:T(8,128)(2,1)} %copy-done.83), channel_id=1, source_target_pairs={{0,2},{2,0},{1,3},{3,1},{4,6},{6,4},{5,7},{7,5},{8,10},{10,8},{9,1... | collective-permute-start | bytes 3145736 | tf_op jit(solution)/shard_map/ppermute | solution.py:36
  249.1 39.9 %collective-permute-start.27 = (bf16[512,1024]{1,0:T(8,128)(2,1)}, bf16[512,1024]{1,0:T(8,128)(2,1)}, u32[]{:S(2)}, u32[]{:S(2)}) collective-permute-start(bf16[512,1024]{1,0:T(8,128)(2,1)} %tie.10), channel_id=1, source_target_pairs={{0,2},{2,0},{1,3},{3,1},{4,6},{6,4},{5,7},{7,5},{8,10},{10,8},{9,1... | collective-permute-start | bytes 3145736 | tf_op jit(solution)/shard_map/ppermute | solution.py:36
  265.2 14.9 %collective-permute-start.30 = (bf16[1024,256]{1,0:T(8,128)(2,1)S(1)}, bf16[1024,256]{1,0:T(8,128)(2,1)S(1)}, u32[]{:S(2)}, u32[]{:S(2)}) collective-permute-start(bf16[1024,256]{1,0:T(8,128)(2,1)S(1)} %fusion.10), channel_id=1, source_target_pairs={{0,1},{1,0},{2,3},{3,2},{4,5},{5,4},{6,7},{7,6},{8,9},{9,8},{10,11... | collective-permute-start | bytes 1572872 | tf_op jit(solution)/shard_map/ppermute | solution.py:40
  286.4 23.9 %collective-permute-start.31 = (bf16[4,128,640]{2,1,0:T(8,128)(2,1)}, bf16[4,128,640]{2,1,0:T(8,128)(2,1)}, u32[]{:S(2)}, u32[]{:S(2)}) collective-permute-start(bf16[4,128,640]{2,1,0:T(8,128)(2,1)} %get-tuple-element.86.rest_1_), channel_id=1, source_target_pairs={{0,4},{4,0},{8,12},{12,8},{16,20},{20,16},{24,28},{28,24},{1,5},{5... | collective-permute-start | bytes 1966088 | tf_op jit(solution)/shard_map/ppermute | solution.py:766
  288.8 40.6 %collective-permute-start.35 = (bf16[1024,384]{1,0:T(8,128)(2,1)}, bf16[1024,384]{1,0:T(8,128)(2,1)S(1)}, u32[]{:S(2)}, u32[]{:S(2)}) collective-permute-start(bf16[1024,384]{1,0:T(8,128)(2,1)} %copy-done.102), channel_id=1, source_target_pairs={{0,1},{1,0},{2,3},{3,2},{4,5},{5,4},{6,7},{7,6},{8,9},{9,8},{10,11... | collective-permute-start | bytes 2359304 | tf_op jit(solution)/shard_map/ppermute | solution.py:40
  310.3 19.1 %collective-permute-start.36 = (bf16[1024,384]{1,0:T(8,128)(2,1)}, bf16[1024,384]{1,0:T(8,128)(2,1)S(1)}, u32[]{:S(2)}, u32[]{:S(2)}) collective-permute-start(bf16[1024,384]{1,0:T(8,128)(2,1)} %tie.12), channel_id=1, source_target_pairs={{0,1},{1,0},{2,3},{3,2},{4,5},{5,4},{6,7},{7,6},{8,9},{9,8},{10,11... | collective-permute-start | bytes 2359304 | tf_op jit(solution)/shard_map/ppermute | solution.py:40
  322.2 34.9 %collective-permute-start.32 = (bf16[128,640]{1,0:T(8,128)(2,1)}, bf16[128,640]{1,0:T(8,128)(2,1)}, u32[]{:S(2)}, u32[]{:S(2)}) collective-permute-start(bf16[128,640]{1,0:T(8,128)(2,1)} %get-tuple-element.122), channel_id=1, source_target_pairs={{0,24},{4,28},{8,16},{12,20},{16,8},{20,12},{24,0},{28,4},{1,25},{... | collective-permute-start | bytes 491528 | tf_op jit(solution)/shard_map/ppermute | solution.py:766
  323.0 35.8 %collective-permute-start.33 = (bf16[128,640]{1,0:T(8,128)(2,1)}, bf16[128,640]{1,0:T(8,128)(2,1)}, u32[]{:S(2)}, u32[]{:S(2)}) collective-permute-start(bf16[128,640]{1,0:T(8,128)(2,1)} %get-tuple-element.121), channel_id=1, source_target_pairs={{0,16},{4,20},{8,24},{12,28},{16,0},{20,4},{24,8},{28,12},{1,17},{... | collective-permute-start | bytes 491528 | tf_op jit(solution)/shard_map/ppermute | solution.py:766
  329.4 31.4 %collective-permute-start.34 = (bf16[128,640]{1,0:T(8,128)(2,1)}, bf16[128,640]{1,0:T(8,128)(2,1)}, u32[]{:S(2)}, u32[]{:S(2)}) collective-permute-start(bf16[128,640]{1,0:T(8,128)(2,1)} %get-tuple-element.120), channel_id=1, source_target_pairs={{0,8},{4,12},{8,0},{12,4},{16,24},{20,28},{24,16},{28,20},{1,9},{5... | collective-permute-start | bytes 491528 | tf_op jit(solution)/shard_map/ppermute | solution.py:766
  341.3 14.1 %collective-permute-start.37 = (bf16[4,128,384]{2,1,0:T(8,128)(2,1)}, bf16[4,128,384]{2,1,0:T(8,128)(2,1)S(1)}, u32[]{:S(2)}, u32[]{:S(2)}) collective-permute-start(bf16[4,128,384]{2,1,0:T(8,128)(2,1)} %tie.13), channel_id=1, source_target_pairs={{0,4},{4,0},{8,12},{12,8},{16,20},{20,16},{24,28},{28,24},{1,5},{5... | collective-permute-start | bytes 1179656 | tf_op jit(solution)/shard_map/ppermute | solution.py:766
  354.6 27.3 %collective-permute-start.44 = (bf16[512,1024]{1,0:T(8,128)(2,1)}, bf16[512,1024]{1,0:T(8,128)(2,1)}, u32[]{:S(2)}, u32[]{:S(2)}) collective-permute-start(bf16[512,1024]{1,0:T(8,128)(2,1)} %get-tuple-element.92.rest_0_.refs_9_), channel_id=1, source_target_pairs={{0,2},{2,0},{1,3},{3,1},{4,6},{6,4},{5,7},{7,5},{8,10},{10,8},{9,1... | collective-permute-start | bytes 3145736 | tf_op jit(solution)/shard_map/ppermute | solution.py:36
  375.5 15.1 %collective-permute-start.47 = (f32[2,128]{1,0:T(2,128)S(1)}, f32[2,128]{1,0:T(2,128)S(1)}, u32[]{:S(2)}, u32[]{:S(2)}) collective-permute-start(f32[2,128]{1,0:T(2,128)S(1)} %slice.164), channel_id=1, source_target_pairs={{0,3},{1,2},{2,1},{3,0},{4,7},{5,6},{6,5},{7,4},{8,11},{9,10},{10,... | collective-permute-start | bytes 3080 | tf_op jit(solution)/shard_map/ppermute | solution.py:1121
  375.5 15.1 %collective-permute-start.46 = (f32[2,128]{1,0:T(2,128)S(1)}, f32[2,128]{1,0:T(2,128)S(1)}, u32[]{:S(2)}, u32[]{:S(2)}) collective-permute-start(f32[2,128]{1,0:T(2,128)S(1)} %slice.164), channel_id=1, source_target_pairs={{0,2},{2,0},{1,3},{3,1},{4,6},{6,4},{5,7},{7,5},{8,10},{10,8},{9,1... | collective-permute-start | bytes 3080 | tf_op jit(solution)/shard_map/ppermute | solution.py:36
  376.9 13.7 %collective-permute-start.45 = (f32[2,128]{1,0:T(2,128)S(1)}, f32[2,128]{1,0:T(2,128)S(1)}, u32[]{:S(2)}, u32[]{:S(2)}) collective-permute-start(f32[2,128]{1,0:T(2,128)S(1)} %slice.164), channel_id=1, source_target_pairs={{0,1},{1,0},{2,3},{3,2},{4,5},{5,4},{6,7},{7,6},{8,9},{9,8},{10,11... | collective-permute-start | bytes 3080 | tf_op jit(solution)/shard_map/ppermute | solution.py:40
  (143 other events, 1069.4 us)
Sparse Core Ops, SparseCore 0:
  217.5 93.8 reduce-scatter.1
where the time goes:
time: 403 us; the launch traced here: 399 us
  Pallas kernels  137 us (34%)
  waiting for transfers between devices  85 us (21%)
  local copies, waits for them, and re-layouts  82.8 us (21%)
  starting transfers between devices  50 us (12%)
  other arithmetic  25.8 us (6%)
  between operations  15.9 us (4%)
    unnamed x257, local copies, waits for them, and re-layouts  70.5 us
    ppermute x23, waiting for transfers between devices, swap_dp(): return lax.ppermute(value, 'dp', [(i, i ^ mask) for i in range(size)])  66.5 us
    pallas_call x3, Pallas kernels, attend_back(): pl.pallas_call(functools.partial(attend_back_kernel, row0=row0, block=blo...  37.2 us
    ppermute x23, starting transfers between devices, swap_dp(): return lax.ppermute(value, 'dp', [(i, i ^ mask) for i in range(size)])  34.2 us
    pallas_call x2, Pallas kernels, feed(): pl.pallas_call(functools.partial(feed_kernel, tiles=tiles), grid=(2 * til...  30.1 us
    pallas_call x2, Pallas kernels, attend(): pl.pallas_call(functools.partial(attend_kernel, row0=row0, block=block),...  21.3 us
    ppermute x9, starting transfers between devices, swap_x(): return lax.ppermute(value, 'tensor', [(0, 2), (2, 0), (1, 3), (3, 1)])  12.5 us
    pallas_call x2, Pallas kernels, feed_grads(): pl.pallas_call(functools.partial(feed_grads_kernel, tiles=tiles, received...  12.4 us
  transfers between devices with their start and end apart: 49, of which 18 were waited for; matrix products, arithmetic and copies ran while one was open for 11% of the time, Pallas kernels for 31%

commit v1 on v0

--- a/solution.py
+++ b/solution.py
@@ -411,6 +411,33 @@
     )
 
 
+def norm_one_back_kernel(
+    place_ref, input_ref, own_ref, recv_ref, low_ref, high_ref, vec_ref, out_ref
+):
+    unit, factor = normalize(input_ref[...].astype(F32))
+    z = own_ref[...] + recv_ref[...].astype(F32)
+    residual = jnp.where(place_ref[0] == 0, low_ref[...], high_ref[...])
+    out_ref[...] = (residual + norm_back(unit, factor, vec_ref[2:3, :], z)).astype(BF16)
+
+
+def norm_one_back(places, inputs, z_own, z_recv, residual_grads, vectors):
+    rows, width = inputs.shape
+    steps = 4
+    strip = pl.BlockSpec((rows // steps, width), lambda i: (i, 0))
+    return pl.pallas_call(
+        norm_one_back_kernel,
+        grid=(steps,),
+        in_specs=[SCALARS]
+        + [strip] * 5
+        + [pl.BlockSpec(vectors.shape, lambda i: (0, 0))],
+        out_specs=strip,
+        out_shape=jax.ShapeDtypeStruct((rows, width), BF16),
+        compiler_params=params(12),
+        cost_estimate=cost(4),
+        name="norm_one_back",
+    )(places, inputs, z_own, z_recv, *residual_grads, vectors)
+
+
 def tie_kernel(value_ref, *rest):
     pass
 
@@ -598,7 +625,7 @@
             jax.ShapeDtypeStruct((share, hidden_cols), F32),
             jax.ShapeDtypeStruct((hidden_cols, share), F32),
         ],
-        compiler_params=params(12),
+        compiler_params=params(60),
         cost_estimate=cost(3),
         name="finish",
     )(*flat, feed_sum, *after)
@@ -790,8 +817,6 @@
             whole = jnp.concatenate([whole, side], axis=1)
         return [lax.psum_scatter(whole.astype(BF16), "dp", scatter_dimension=0)]
     sums = kept + received.astype(F32)
-    if side is not None:
-        sums = jnp.concatenate([sums, side], axis=1)
     z = lax.axis_index("dp") // 2
     terms = [lax.dynamic_index_in_dim(sums, z, 0, keepdims=False)]
     for k in (3, 2, 1):
@@ -883,15 +908,15 @@
         mlp_shares = {0: mlp_shard, 1: swap_dp(mlp_shard, 1)}
         for k in (0, 2, 4, 6):
             shares[k + 1] = swap_dp(shares[k], 1)
-        behind = (shares[6], shares[5], shares[3], shares[1], mlp_shares[1])
         mlp_shares.update(gather_z(tie(mlp_shard, *(shares[k] for k in (2, 4, 6)))))
+        behind = tuple(shares[k] for k in (6, 5, 3, 1)) + (mlp_shares[1], mlp_shares[4])
         for k in (2, 4):
             mlp_shares[k + 1] = swap_dp(mlp_shares[k], 1)
         attn_all = place_shares(
             lax.axis_index("dp"),
             [shares[k] for k in range(parts)],
             side_rows,
-            assemble(behind) + (mlp_shares[2], mlp_shares[4]),
+            assemble(behind),
         )
         early = (mlp_shares[3], mlp_shares[5], mlp_shares[6])
     else:
@@ -982,8 +1007,7 @@
     sib_grads = feed_grads(
         normed_two, cots, grads_hidden, acts, hidden_cols, None, after=(back_recv[0],)
     )
-    grad_mlp = feed_grads(normed_two, cots, grads_hidden, acts, 0, swap_core(sib_grads))
-    mlp_sum = lax.psum_scatter(grad_mlp, "dp", scatter_dimension=0, tiled=True)
+    sib_received = swap_core(sib_grads)
 
     grad_residuals, branches, grads_mixed = [], [], []
     for half in range(2):
@@ -994,7 +1018,7 @@
             cots[half],
             columns,
             proj_both,
-            after=(sib_grads,) if half == 0 else (grad_mlp, low_grads),
+            after=(sib_grads,) if half == 0 else (low_grads,),
         )
         grad_residuals.append(grad_residual)
         branches.append(branch)
@@ -1007,6 +1031,10 @@
         )
         vec_two = sums_two if half == 0 else vec_two + sums_two
         if half == 0:
+            grad_mlp = feed_grads(
+                normed_two, cots, grads_hidden, acts, 0, sib_received, after=(branch,)
+            )
+            mlp_sum = lax.psum_scatter(grad_mlp, "dp", scatter_dimension=0, tiled=True)
             low_grads, _ = attend_back(
                 qkv,
                 mixed[0],
@@ -1087,23 +1115,20 @@
     side = jnp.concatenate(
         [vec_blocks, jnp.broadcast_to(pair_rows[None], (parts, 8, 3 * PAIR))], axis=1
     )
-    if parts == 8:
-        views = side.reshape((parts // 2, 2) + side.shape[1:])
-        side_kept = lax.dynamic_index_in_dim(views, y, 1, keepdims=False)
-        side_sent = lax.dynamic_index_in_dim(views, 1 - y, 1, keepdims=False)
-        side = side_kept + swap_dp(side_sent, 1)
+    views = side.reshape((-1, 2) + side.shape[1:])
+    side_kept = lax.dynamic_index_in_dim(views, y, 1, keepdims=False)
+    side_sent = lax.dynamic_index_in_dim(views, 1 - y, 1, keepdims=False)
     terms = [first_terms]
     for pair in range(1, pairs):
         kept, sent, received = exchanges[pair]
         last = pair == pairs - 1
-        if last:
-            received = scatter_y(tie(sent, z_sent), parts)
+        if last and parts == 8:
+            kept = jnp.concatenate([kept, side_kept], axis=1)
+            sent = jnp.concatenate([sent, side_sent.astype(BF16)], axis=1)
+            received = tie(scatter_y(sent, parts), *first_terms[1:])
         terms.append(scatter_z(kept, sent, received, side if last else None, parts))
 
-    qkv_out, proj_out, six, fc_out, out_out = finish(
-        terms, mlp_sum, share, head_cols, side_rows, after=(z_sent,)
-    )
-    out_recv = tie(out_recv, six)
+    out_recv = tie(out_recv, *terms[-1][1:])
     out_mine = pick_x(out_parts[0], out_parts[1])
     outputs = (
         pick_x(residuals[0], residuals[1])
@@ -1112,11 +1137,12 @@
         + out_shift
     ).astype(BF16)
 
-    unit, factor = normalize(inputs.astype(F32))
-    z_own = z_own + tie(z_recv, six).astype(F32)
-    grad_inputs = (
-        pick_x(grad_residuals[0], grad_residuals[1]) + norm_back(unit, factor, gain_one, z_own)
-    ).astype(BF16)
+    qkv_out, proj_out, six, fc_out, out_out = finish(
+        terms, mlp_sum, share, head_cols, side_rows, after=(outputs, z_recv)
+    )
+    grad_inputs = norm_one_back(
+        place_ids, inputs, z_own, tie(z_recv, six), grad_residuals, columns
+    )
     one = six[2:4, :share]
     far = lax.ppermute(one, "tensor", [(i, i ^ 3) for i in range(4)])
     two = one + swap_core(one) + swap_x(one) + far

time: 403 us -> 407 us (level)
  waiting for transfers between devices: 85 us -> 110 us
  local copies, waits for them, and re-layouts: 82.8 us -> 72.4 us
  starting transfers between devices: 50 us -> 39.7 us
  other arithmetic: 25.8 us -> 17.6 us
  Pallas kernels: 137 us -> 145 us
    ppermute x9, waiting for transfers between devices: 6.49 us -> 30.6 us  [swap_x(): return lax.ppermute(value, 'tensor', [(0, 2), (2, 0), (1, 3), (3, 1)])]
    unnamed x257 -> x223, local copies, waits for them, and re-layouts: 70.5 us -> 60.7 us
    reduce_sum x3 -> x0, other arithmetic: 5.71 us -> none  [the longest x1 2.48 us: norm_back(): jnp.mean(scaled, axis=-1, keepdims=True)]
    ppermute x23 -> x22, starting transfers between devices: 34.2 us -> 28.7 us  [swap_dp(): return lax.ppermute(value, 'dp', [(i, i ^ mask) for i in range(size)])]
    ppermute x23 -> x22, waiting for transfers between devices: 66.5 us -> 71.4 us  [swap_dp(): return lax.ppermute(value, 'dp', [(i, i ^ mask) for i in range(size)])]
    ppermute x15, waiting for transfers between devices: 12 us -> 7.55 us  [swap_core(): return lax.ppermute(value, 'tensor', [(0, 1), (1, 0), (2, 3), (3, 2)])]
  transfers between devices with their start and end apart: 49 -> 48, of which waited for: 18 -> 23; matrix products, arithmetic and copies ran while one was open for 11% -> 8% of each run, Pallas kernels for 31% -> 32%
where the time goes in v1:
time: 407 us; the launch traced here: 403 us
  Pallas kernels  145 us (36%)
  waiting for transfers between devices  110 us (27%)
  local copies, waits for them, and re-layouts  72.4 us (18%)
  starting transfers between devices  39.7 us (10%)
  other arithmetic  17.6 us (4%)
  between operations  15.8 us (4%)
    ppermute x22, waiting for transfers between devices, swap_dp(): return lax.ppermute(value, 'dp', [(i, i ^ mask) for i in range(size)])  71.4 us
    unnamed x223, local copies, waits for them, and re-layouts  60.7 us
    pallas_call x3, Pallas kernels, attend_back(): pl.pallas_call(functools.partial(attend_back_kernel, row0=row0, block=blo...  37.9 us
    pallas_call x2, Pallas kernels, feed(): pl.pallas_call(functools.partial(feed_kernel, tiles=tiles), grid=(2 * til...  31.1 us
    ppermute x9, waiting for transfers between devices, swap_x(): return lax.ppermute(value, 'tensor', [(0, 2), (2, 0), (1, 3), (3, 1)])  30.6 us
    ppermute x22, starting transfers between devices, swap_dp(): return lax.ppermute(value, 'dp', [(i, i ^ mask) for i in range(size)])  28.7 us
    pallas_call x2, Pallas kernels, attend(): pl.pallas_call(functools.partial(attend_kernel, row0=row0, block=block),...  21.3 us
    pallas_call x2, Pallas kernels, feed_grads(): pl.pallas_call(functools.partial(feed_grads_kernel, tiles=tiles, received...  12.4 us
  transfers between devices with their start and end apart: 48, of which 23 were waited for; matrix products, arithmetic and copies ran while one was open for 8% of the time, Pallas kernels for 32%

profile of v1, /device:TPU:0, one launch (start us, length us, event | category | flops | bytes accessed | tf_op | source)
XLA Modules:
  0.0 403.0 jit_solution(10202712717453663285)
XLA Ops:
  7.2 3.0 collective-permute-start
  14.0 3.7 collective-permute-start.1
  22.0 4.0 collective-permute-done.1.rest_2_.rest_0_.refs_6_
  27.4 15.1 %collective-permute-done.2.rest_1_.refs_4_ = bf16[144,1024]{1,0:T(8,128)(2,1)S(1)} collective-permute-done((bf16[144,1024]{1,0:T(8,128)(2,1)S(1)}, bf16[144,1024]{1,0:T(8,128)(2,1)S(1)}, u32[]{:S(2)}, u32[]{:S(2)}) %collective-permute-start.2) | collective-permute-done | bytes 294944 | tf_op jit(solution)/shard_map/ppermute | solution.py:793
  45.5 8.0 %collective-permute-done.3.rest_1_.refs_5_ = bf16[144,1024]{1,0:T(8,128)(2,1)S(1)} collective-permute-done((bf16[144,1024]{1,0:T(8,128)(2,1)}, bf16[144,1024]{1,0:T(8,128)(2,1)S(1)}, u32[]{:S(2)}, u32[]{:S(2)}) %collective-permute-start.3) | collective-permute-done | bytes 294944 | tf_op jit(solution)/shard_map/ppermute | solution.py:793
  53.5 4.4 %collective-permute-done.5.rest_2_.refs_3_ = bf16[144,1024]{1,0:T(8,128)(2,1)S(1)} collective-permute-done((bf16[144,1024]{1,0:T(8,128)(2,1)}, bf16[144,1024]{1,0:T(8,128)(2,1)S(1)}, u32[]{:S(2)}, u32[]{:S(2)}) %collective-permute-start.5) | collective-permute-done | bytes 294944 | tf_op jit(solution)/shard_map/ppermute | solution.py:793
  57.9 10.1 %collective-permute-done.8.rest_5_.refs_4_ = bf16[128,2048]{1,0:T(8,128)(2,1)} collective-permute-done((bf16[128,2048]{1,0:T(8,128)(2,1)}, bf16[128,2048]{1,0:T(8,128)(2,1)}, u32[]{:S(2)}, u32[]{:S(2)}) %collective-permute-start.8) | collective-permute-done | bytes 524320 | tf_op jit(solution)/shard_map/ppermute | solution.py:793
  77.8 16.2 %collective-permute-done.12.refs_9_ = bf16[512,1024]{1,0:T(8,128)(2,1)} collective-permute-done((bf16[512,1024]{1,0:T(8,128)(2,1)}, bf16[512,1024]{1,0:T(8,128)(2,1)}, u32[]{:S(2)}, u32[]{:S(2)}) %collective-permute-start.12) | collective-permute-done | bytes 1048608 | tf_op jit(solution)/shard_map/ppermute | solution.py:36
  98.8 11.4 %collective-permute-done.16.refs_2_ = bf16[128,2048]{1,0:T(8,128)(2,1)} collective-permute-done((bf16[128,2048]{1,0:T(8,128)(2,1)}, bf16[128,2048]{1,0:T(8,128)(2,1)}, u32[]{:S(2)}, u32[]{:S(2)}) %collective-permute-start.16) | collective-permute-done | bytes 524320 | tf_op jit(solution)/shard_map/ppermute | solution.py:793
  114.8 6.1 %project.1 = (bf16[2048,1024]{1,0:T(8,128)(2,1)S(1)}, bf16[2048,768]{1,0:T(8,128)(2,1)S(1)}) custom-call(bf16[2048,1024]{1,0:T(8,128)(2,1)S(1)} %copy-done.3, f32[8,1024]{1,0:T(8,128)S(1)} %bitcast.102, f32[1,768]{1,0:T(1,128)S(1)} %reshape.138.shift_ref, bf16[1152,1024]{1,0:T(8,128)(2,1)S(1)} %place_shares.2.weight_ref.refs_4_.refs_5_), custom_call_target="tpu_custom_call" | custom-call | flops 1650000000 | bytes 1500000 | tf_op jit(solution)/shard_map/project/pallas_call | solution.py:644
  120.9 5.7 %attend_0.1 = (bf16[1024,256]{1,0:T(8,128)(2,1)S(1)}, f32[2,2,1024]{2,1,0:T(2,128)S(1)}) custom-call(bf16[2048,768]{1,0:T(8,128)(2,1)S(1)} %get-tuple-element.61.qkv_ref), custom_call_target="tpu_custom_call" | custom-call | flops 1650000000 | bytes 1500000 | tf_op jit(solution)/shard_map/attend_0/pallas_call | solution.py:136
  130.2 15.6 %attend_1024.1 = (bf16[1024,256]{1,0:T(8,128)(2,1)S(1)}, f32[2,2,1024]{2,1,0:T(2,128)S(1)}) custom-call(bf16[2048,768]{1,0:T(8,128)(2,1)S(1)} %get-tuple-element.61.qkv_ref, bf16[512,1024]{1,0:T(8,128)(2,1)S(1)} %convolution_convert_fusion.1.rest_0_.part_ref, bf16[128,2048]{1,0:T(8,128)(2,1)} %collective-permute-done.17.rest_1_.refs_3_, ...), custom_call_target="tpu_custom_call" | custom-call | flops 4400000000 | bytes 4000000 | tf_op jit(solution)/shard_map/attend_1024/pallas_call | solution.py:136
  148.9 5.9 %collective-permute-done.15.refs_8_.recv_ref = bf16[512,1024]{1,0:T(8,128)(2,1)S(1)} collective-permute-done((bf16[512,1024]{1,0:T(8,128)(2,1)S(1)}, bf16[512,1024]{1,0:T(8,128)(2,1)S(1)}, u32[]{:S(2)}, u32[]{:S(2)}) %collective-permute-start.15) | collective-permute-done | bytes 1048608 | tf_op jit(solution)/shard_map/ppermute | solution.py:36
  160.9 3.1 collective-permute-done.22.fc_sib_ref.out_sib_ref
  166.1 16.4 %feed.2 = (f32[512,1024]{1,0:T(8,128)S(1)}, bf16[512,1024]{1,0:T(8,128)(2,1)S(1)}, bf16[512,2048]{1,0:T(8,128)(2,1)S(1)}, bf16[512,2048]{1,0:T(8,128)(2,1)S(1)},...) custom-call(bf16[512,1024]{1,0:T(8,128)(2,1)S(1)} %copy-done.10, ...), custom_call_target="tpu_custom_call" | custom-call | flops 4400000000 | bytes 4000000 | tf_op jit(solution)/shard_map/feed/pallas_call | solution.py:747
  193.1 14.7 %feed.3 = (f32[512,1024]{1,0:T(8,128)S(1)}, bf16[512,1024]{1,0:T(8,128)(2,1)S(1)}, bf16[512,2048]{1,0:T(8,128)(2,1)S(1)}, bf16[512,2048]{1,0:T(8,128)(2,1)S(1)},...) custom-call(bf16[512,1024]{1,0:T(8,128)(2,1)S(1)} %copy-done.13, ...), custom_call_target="tpu_custom_call" | custom-call | flops 4400000000 | bytes 4000000 | tf_op jit(solution)/shard_map/feed/pallas_call | solution.py:747
  211.3 5.9 %feed_grads.2.rest_0_ = bf16[1024,2048]{1,0:T(8,128)(2,1)S(1)} custom-call(bf16[512,1024]{1,0:T(8,128)(2,1)S(1)} %copy-done.46, bf16[512,1024]{1,0:T(8,128)(2,1)S(1)} %get-tuple-element.70.refs_1_, bf16[512,1024]{1,0:T(8,128)(2,1)S(1)} %copy-done.8, bf16[512,1024]{1,0:T(8,128)(2,1)S(1)} %copy-done.5, bf16[512,2048]{1,0:T(8,128)(2,1)S(1)} %get-tuple-element.71.refs_4_, ...), custom_call_target="tpu_custom_call" | custom-call | flops 1650000000 | bytes 1500000 | tf_op jit(solution)/shard_map/feed_grads/pallas_call | solution.py:515
  217.5 4.3 %norm_two.2 = (f32[512,1024]{1,0:T(8,128)S(1)}, bf16[512,1024]{1,0:T(8,128)(2,1)S(1)}, bf16[512,512]{1,0:T(8,128)(2,1)S(1)}, f32[8,1024]{1,0:T(8,128)S(1)}) custom-call(bf16[512,1024]{1,0:T(8,128)(2,1)} %get-tuple-element.68.back_ref, bf16[512,1024]{1,0:T(8,128)(2,1)} %collective-permute-done.24.refs_8_.recv_ref, ...), custom_call_target="tpu_custom_call" | custom-call | flops 1100000000 | bytes 1000000 | tf_op jit(solution)/shard_map/norm_two/pallas_call | solution.py:316
  224.5 6.4 %feed_grads.3.rest_0_ = bf16[1024,2048]{1,0:T(8,128)(2,1)S(1)} custom-call(bf16[512,1024]{1,0:T(8,128)(2,1)S(1)} %copy-done.47, bf16[512,1024]{1,0:T(8,128)(2,1)S(1)} %get-tuple-element.70.refs_1_, bf16[512,1024]{1,0:T(8,128)(2,1)S(1)} %copy-done.8, bf16[512,1024]{1,0:T(8,128)(2,1)S(1)} %copy-done.5, bf16[512,2048]{1,0:T(8,128)(2,1)S(1)} %copy-done.37, ...), custom_call_target="tpu_custom_call" | custom-call | flops 1650000000 | bytes 1500000 | tf_op jit(solution)/shard_map/feed_grads/pallas_call | solution.py:515
  241.0 10.9 %attend_back_0_0.1 = (f32[1024,768]{1,0:T(8,128)S(1)}, f32[1,768]{1,0:T(1,128)}) custom-call(s32[1]{0:T(128)} %constant.103.clone.1.core_ref, bf16[2048,768]{1,0:T(8,128)(2,1)S(1)} %copy-done.88, bf16[1024,256]{1,0:T(8,128)(2,1)S(1)} %copy-done.84, bf16[1024,256]{1,0:T(8,128)(2,1)S(1)} %pad_maximum_fusion.3.grad_ref, ...), custom_call_target="tpu_custom_call" | custom-call | flops 3024999936 | bytes 2750000 | tf_op jit(solution)/shard_map/attend_back_0_0/pallas_call | solution.py:259
  255.1 5.4 %collective-permute-done.28.recv_ref = bf16[512,1024]{1,0:T(8,128)(2,1)} collective-permute-done((bf16[512,1024]{1,0:T(8,128)(2,1)}, bf16[512,1024]{1,0:T(8,128)(2,1)}, u32[]{:S(2)}, u32[]{:S(2)}) %collective-permute-start.28) | collective-permute-done | bytes 1048608 | tf_op jit(solution)/shard_map/ppermute | solution.py:36
  266.5 4.3 %norm_two.3 = (f32[512,1024]{1,0:T(8,128)S(1)}, bf16[512,1024]{1,0:T(8,128)(2,1)S(1)}, bf16[512,512]{1,0:T(8,128)(2,1)S(1)}, f32[8,1024]{1,0:T(8,128)S(1)}) custom-call(bf16[512,1024]{1,0:T(8,128)(2,1)S(1)} %copy-done.71, bf16[512,1024]{1,0:T(8,128)(2,1)} %collective-permute-done.28.recv_ref, f32[512,1024]{1,0:T(8,128)S(1)} %copy-done.35, ...), custom_call_target="tpu_custom_call" | custom-call | flops 1100000000 | bytes 1000000 | tf_op jit(solution)/shard_map/norm_two/pallas_call | solution.py:316
  275.0 13.8 %attend_back_1024_0.1 = (bf16[2048,384]{1,0:T(8,128)(2,1)S(1)}, f32[1,384]{1,0:T(1,128)S(1)}, bf16[1024,384]{1,0:T(8,128)(2,1)}) custom-call(s32[1]{0:T(128)} %bitcast.27.core_ref, bf16[2048,768]{1,0:T(8,128)(2,1)S(1)} %copy-done.89, bf16[1024,256]{1,0:T(8,128)(2,1)S(1)} %copy-done.82, bf16[1024,256]{1,0:T(8,128)(2,1)S(1)} %pad_maximum_fusion.4.grad_ref, ...), custom_call_target="tpu_custom_call" | custom-call | flops 3575000064 | bytes 3250000 | tf_op jit(solution)/shard_map/attend_back_1024_0/pallas_call | solution.py:259
  288.8 5.1 %weight_grads.2 = (f32[4,128,640]{2,1,0:T(8,128)S(1)}, bf16[4,128,640]{2,1,0:T(8,128)(2,1)}) custom-call(s32[1]{0:T(128)} %bitcast.28.y_ref, bf16[2048,1024]{1,0:T(8,128)(2,1)S(1)} %copy-done.16, bf16[2048,384]{1,0:T(8,128)(2,1)S(1)} %get-tuple-element.82.rest_0_.grad_ref.refs_0_, bf16[512,1024]{1,0:T(8,128)(2,1)S(1)} %copy-done.31, ...), custom_call_target="tpu_custom_call" | custom-call | flops 1100000000 | bytes 1000000 | tf_op jit(solution)/shard_map/weight_grads/pallas_call | solution.py:567
  300.4 13.2 %attend_back_1024_1.1 = (bf16[2048,384]{1,0:T(8,128)(2,1)S(1)}, f32[1,384]{1,0:T(1,128)S(1)}, bf16[1024,384]{1,0:T(8,128)(2,1)S(1)}) custom-call(s32[1]{0:T(128)} %bitcast.27.core_ref, bf16[2048,768]{1,0:T(8,128)(2,1)S(1)} %copy-done.90, bf16[1024,256]{1,0:T(8,128)(2,1)S(1)} %copy-done.82, bf16[1024,256]{1,0:T(8,128)(2,1)S(1)} %pad_maximum_fusion.4.grad_ref, ...), custom_call_target="tpu_custom_call" | custom-call | flops 3575000064 | bytes 3250000 | tf_op jit(solution)/shard_map/attend_back_1024_1/pallas_call | solution.py:259
  323.0 3.6 weight_grads.3
  327.6 10.0 %norm_one.1 = (f32[512,1024]{1,0:T(8,128)S(1)}, bf16[512,1024]{1,0:T(8,128)(2,1)}, f32[8,1024]{1,0:T(8,128)S(1)}) custom-call(s32[2]{0:T(128)S(1)} %pad_add_fusion.place_ref, bf16[512,1024]{1,0:T(8,128)(2,1)S(1)} %copy-done.11, bf16[512,1024]{1,0:T(8,128)(2,1)S(1)} %copy-done.14, bf16[2048,384]{1,0:T(8,128)(2,1)S(1)} %copy-done.23, ...), custom_call_target="tpu_custom_call" | custom-call | flops 2200000000 | bytes 2000000 | tf_op jit(solution)/shard_map/norm_one/pallas_call | solution.py:382
  347.6 3.4 collective-permute-done.37.rest_0_.refs_1_
  351.0 7.2 %collective-permute-done.38.rest_1_.refs_2_ = bf16[128,640]{1,0:T(8,128)(2,1)S(1)} collective-permute-done((bf16[128,640]{1,0:T(8,128)(2,1)S(1)}, bf16[128,640]{1,0:T(8,128)(2,1)S(1)}, u32[]{:S(2)}, u32[]{:S(2)}) %collective-permute-start.38) | collective-permute-done | bytes 163872 | tf_op jit(solution)/shard_map/ppermute | solution.py:793
  372.8 3.4 add_convert_fusion.refs_9_
  377.2 2.9 finish.1
  390.4 3.4 norm_one_back.1
  (386 shorter events, 140.6 us)
Async XLA Ops:
  7.2 369.1 %reduce-scatter.2.cloned.1.call-start = ((), (), s32[]{:S(2)}) async-start(), calls=%async_computation.1 | async-start | bytes 4718592 | tf_op jit(solution)/shard_map/reduce_scatter | solution.py:1037
  7.2 60.8 %collective-permute-start = (bf16[512,1024]{1,0:T(8,128)(2,1)}, bf16[512,1024]{1,0:T(8,128)(2,1)}, u32[]{:S(2)}, u32[]{:S(2)}) collective-permute-start(bf16[512,1024]{1,0:T(8,128)(2,1)} %input_ref.1), channel_id=1, source_target_pairs={{0,2},{2,0},{1,3},{3,1},{4,6},{6,4},{5,7},{7,5},{8,10},{10,8},{9,1... | collective-permute-start | bytes 3145736 | tf_op jit(solution)/shard_map/ppermute | solution.py:36
  14.0 11.9 %collective-permute-start.1 = (bf16[144,1024]{1,0:T(8,128)(2,1)S(1)}, bf16[144,1024]{1,0:T(8,128)(2,1)S(1)}, u32[]{:S(2)}, u32[]{:S(2)}) collective-permute-start(bf16[144,1024]{1,0:T(8,128)(2,1)S(1)} %fusion.8.refs_0_), channel_id=1, source_target_pairs={{0,24},{4,28},{8,16},{12,20},{16,8},{20,12},{24,0},{28,4},{1,25},{... | collective-permute-start | bytes 884744 | tf_op jit(solution)/shard_map/ppermute | solution.py:793
  17.7 24.8 %collective-permute-start.2 = (bf16[144,1024]{1,0:T(8,128)(2,1)S(1)}, bf16[144,1024]{1,0:T(8,128)(2,1)S(1)}, u32[]{:S(2)}, u32[]{:S(2)}) collective-permute-start(bf16[144,1024]{1,0:T(8,128)(2,1)S(1)} %fusion.8.refs_0_), channel_id=1, source_target_pairs={{0,16},{4,20},{8,24},{12,28},{16,0},{20,4},{24,8},{28,12},{1,17},{... | collective-permute-start | bytes 884744 | tf_op jit(solution)/shard_map/ppermute | solution.py:793
  17.7 24.8 %collective-permute-start.4 = (bf16[144,1024]{1,0:T(8,128)(2,1)S(1)}, bf16[144,1024]{1,0:T(8,128)(2,1)}, u32[]{:S(2)}, u32[]{:S(2)}) collective-permute-start(bf16[144,1024]{1,0:T(8,128)(2,1)S(1)} %fusion.8.refs_0_), channel_id=1, source_target_pairs={{0,8},{4,12},{8,0},{12,4},{16,24},{20,28},{24,16},{28,20},{1,9},{5... | collective-permute-start | bytes 884744 | tf_op jit(solution)/shard_map/ppermute | solution.py:793
  18.5 26.4 %collective-permute-start.6 = (bf16[144,1024]{1,0:T(8,128)(2,1)S(1)}, bf16[144,1024]{1,0:T(8,128)(2,1)S(1)}, u32[]{:S(2)}, u32[]{:S(2)}) collective-permute-start(bf16[144,1024]{1,0:T(8,128)(2,1)S(1)} %fusion.8.refs_0_), channel_id=1, source_target_pairs={{0,4},{4,0},{8,12},{12,8},{16,20},{20,16},{24,28},{28,24},{1,5},{5... | collective-permute-start | bytes 884744 | tf_op jit(solution)/shard_map/ppermute | solution.py:793
  25.9 19.4 %collective-permute-start.7 = (bf16[128,2048]{1,0:T(8,128)(2,1)S(1)}, bf16[128,2048]{1,0:T(8,128)(2,1)S(1)}, u32[]{:S(2)}, u32[]{:S(2)}) collective-permute-start(bf16[128,2048]{1,0:T(8,128)(2,1)S(1)} %pad_maximum_fusion.2.refs_0_), channel_id=1, source_target_pairs={{0,4},{4,0},{8,12},{12,8},{16,20},{20,16},{24,28},{28,24},{1,5},{5... | collective-permute-start | bytes 1572872 | tf_op jit(solution)/shard_map/ppermute | solution.py:793
  43.2 24.8 %collective-permute-start.8 = (bf16[128,2048]{1,0:T(8,128)(2,1)}, bf16[128,2048]{1,0:T(8,128)(2,1)}, u32[]{:S(2)}, u32[]{:S(2)}) collective-permute-start(bf16[128,2048]{1,0:T(8,128)(2,1)} %tie.8), channel_id=1, source_target_pairs={{0,16},{4,20},{8,24},{12,28},{16,0},{20,4},{24,8},{28,12},{1,17},{... | collective-permute-start | bytes 1572872 | tf_op jit(solution)/shard_map/ppermute | solution.py:793
  44.8 13.0 %collective-permute-start.5 = (bf16[144,1024]{1,0:T(8,128)(2,1)}, bf16[144,1024]{1,0:T(8,128)(2,1)S(1)}, u32[]{:S(2)}, u32[]{:S(2)}) collective-permute-start(bf16[144,1024]{1,0:T(8,128)(2,1)} %collective-permute-done.4.rest_0_.refs_2_), channel_id=1, source_target_pairs={{0,4},{4,0},{8,12},{12,8},{16,20},{20,16},{24,28},{28,24},{1,5},{5... | collective-permute-start | bytes 884744 | tf_op jit(solution)/shard_map/ppermute | solution.py:793
  45.4 24.9 %collective-permute-start.9 = (bf16[512,1024]{1,0:T(8,128)(2,1)S(1)}, bf16[512,1024]{1,0:T(8,128)(2,1)}, u32[]{:S(2)}, u32[]{:S(2)}) collective-permute-start(bf16[512,1024]{1,0:T(8,128)(2,1)S(1)} %copy-done.41), channel_id=1, source_target_pairs={{0,1},{1,0},{2,3},{3,2},{4,5},{5,4},{6,7},{7,6},{8,9},{9,8},{10,11... | collective-permute-start | bytes 3145736 | tf_op jit(solution)/shard_map/ppermute | solution.py:40
  68.1 25.9 %collective-permute-start.12 = (bf16[512,1024]{1,0:T(8,128)(2,1)}, bf16[512,1024]{1,0:T(8,128)(2,1)}, u32[]{:S(2)}, u32[]{:S(2)}) collective-permute-start(bf16[512,1024]{1,0:T(8,128)(2,1)} %param.27), channel_id=1, source_target_pairs={{0,2},{2,0},{1,3},{3,1},{4,6},{6,4},{5,7},{7,5},{8,10},{10,8},{9,1... | collective-permute-start | bytes 3145736 | tf_op jit(solution)/shard_map/ppermute | solution.py:36
  95.2 32.3 %collective-permute-start.14 = (bf16[1152,1024]{1,0:T(8,128)(2,1)S(1)}, bf16[1152,1024]{1,0:T(8,128)(2,1)}, u32[]{:S(2)}, u32[]{:S(2)}) collective-permute-start(bf16[1152,1024]{1,0:T(8,128)(2,1)S(1)} %place_shares.2.weight_ref.refs_4_.refs_5_), channel_id=1, source_target_pairs={{0,1},{1,0},{2,3},{3,2},{4,5},{5,4},{6,7},{7,6},{8,9},{9,8},{10,11... | collective-permute-start | bytes 7077896 | tf_op jit(solution)/shard_map/ppermute | solution.py:40
  95.3 14.9 %collective-permute-start.16 = (bf16[128,2048]{1,0:T(8,128)(2,1)}, bf16[128,2048]{1,0:T(8,128)(2,1)}, u32[]{:S(2)}, u32[]{:S(2)}) collective-permute-start(bf16[128,2048]{1,0:T(8,128)(2,1)} %tie.8), channel_id=1, source_target_pairs={{0,8},{4,12},{8,0},{12,4},{16,24},{20,28},{24,16},{28,20},{1,9},{5... | collective-permute-start | bytes 1572872 | tf_op jit(solution)/shard_map/ppermute | solution.py:793
  95.4 31.4 %collective-permute-start.19 = (bf16[128,2048]{1,0:T(8,128)(2,1)}, bf16[128,2048]{1,0:T(8,128)(2,1)}, u32[]{:S(2)}, u32[]{:S(2)}) collective-permute-start(bf16[128,2048]{1,0:T(8,128)(2,1)} %tie.8), channel_id=1, source_target_pairs={{0,24},{4,28},{8,16},{12,20},{16,8},{20,12},{24,0},{28,4},{1,25},{... | collective-permute-start | bytes 1572872 | tf_op jit(solution)/shard_map/ppermute | solution.py:793
  97.2 32.9 %collective-permute-start.18 = (bf16[128,2048]{1,0:T(8,128)(2,1)}, bf16[128,2048]{1,0:T(8,128)(2,1)}, u32[]{:S(2)}, u32[]{:S(2)}) collective-permute-start(bf16[128,2048]{1,0:T(8,128)(2,1)} %collective-permute-done.8.rest_5_.refs_4_), channel_id=1, source_target_pairs={{0,4},{4,0},{8,12},{12,8},{16,20},{20,16},{24,28},{28,24},{1,5},{5... | collective-permute-start | bytes 1572872 | tf_op jit(solution)/shard_map/ppermute | solution.py:793
  110.1 20.1 %collective-permute-start.17 = (bf16[128,2048]{1,0:T(8,128)(2,1)}, bf16[128,2048]{1,0:T(8,128)(2,1)}, u32[]{:S(2)}, u32[]{:S(2)}) collective-permute-start(bf16[128,2048]{1,0:T(8,128)(2,1)} %collective-permute-done.16.refs_2_), channel_id=1, source_target_pairs={{0,4},{4,0},{8,12},{12,8},{16,20},{20,16},{24,28},{28,24},{1,5},{5... | collective-permute-start | bytes 1572872 | tf_op jit(solution)/shard_map/ppermute | solution.py:793
  126.8 22.1 %collective-permute-start.20 = (bf16[128,2048]{1,0:T(8,128)(2,1)}, bf16[128,2048]{1,0:T(8,128)(2,1)S(1)}, u32[]{:S(2)}, u32[]{:S(2)}) collective-permute-start(bf16[128,2048]{1,0:T(8,128)(2,1)} %collective-permute-done.19.rest_3_.refs_6_), channel_id=1, source_target_pairs={{0,4},{4,0},{8,12},{12,8},{16,20},{20,16},{24,28},{28,24},{1,5},{5... | collective-permute-start | bytes 1572872 | tf_op jit(solution)/shard_map/ppermute | solution.py:793
  129.6 25.3 %collective-permute-start.15 = (bf16[512,1024]{1,0:T(8,128)(2,1)S(1)}, bf16[512,1024]{1,0:T(8,128)(2,1)S(1)}, u32[]{:S(2)}, u32[]{:S(2)}) collective-permute-start(bf16[512,1024]{1,0:T(8,128)(2,1)S(1)} %convolution_convert_fusion.1.rest_0_.part_ref), channel_id=1, source_target_pairs={{0,2},{2,0},{1,3},{3,1},{4,6},{6,4},{5,7},{7,5},{8,10},{10,8},{9,1... | collective-permute-start | bytes 3145736 | tf_op jit(solution)/shard_map/ppermute | solution.py:36
  160.3 25.6 %collective-permute-start.23 = (bf16[512,1024]{1,0:T(8,128)(2,1)S(1)}, bf16[512,1024]{1,0:T(8,128)(2,1)S(1)}, u32[]{:S(2)}, u32[]{:S(2)}) collective-permute-start(bf16[512,1024]{1,0:T(8,128)(2,1)S(1)} %convolution_convert_fusion.refs_9_.rest_0_.part_ref), channel_id=1, source_target_pairs={{0,2},{2,0},{1,3},{3,1},{4,6},{6,4},{5,7},{7,5},{8,10},{10,8},{9,1... | collective-permute-start | bytes 3145736 | tf_op jit(solution)/shard_map/ppermute | solution.py:36
  184.6 25.5 %collective-permute-start.24 = (bf16[512,1024]{1,0:T(8,128)(2,1)}, bf16[512,1024]{1,0:T(8,128)(2,1)}, u32[]{:S(2)}, u32[]{:S(2)}) collective-permute-start(bf16[512,1024]{1,0:T(8,128)(2,1)} %get-tuple-element.68.back_ref), channel_id=1, source_target_pairs={{0,2},{2,0},{1,3},{3,1},{4,6},{6,4},{5,7},{7,5},{8,10},{10,8},{9,1... | collective-permute-start | bytes 3145736 | tf_op jit(solution)/shard_map/ppermute | solution.py:36
  234.1 26.4 %collective-permute-start.28 = (bf16[512,1024]{1,0:T(8,128)(2,1)}, bf16[512,1024]{1,0:T(8,128)(2,1)}, u32[]{:S(2)}, u32[]{:S(2)}) collective-permute-start(bf16[512,1024]{1,0:T(8,128)(2,1)} %copy-done.70), channel_id=1, source_target_pairs={{0,2},{2,0},{1,3},{3,1},{4,6},{6,4},{5,7},{7,5},{8,10},{10,8},{9,1... | collective-permute-start | bytes 3145736 | tf_op jit(solution)/shard_map/ppermute | solution.py:36
  253.6 43.0 %collective-permute-start.27 = (bf16[512,1024]{1,0:T(8,128)(2,1)}, bf16[512,1024]{1,0:T(8,128)(2,1)}, u32[]{:S(2)}, u32[]{:S(2)}) collective-permute-start(bf16[512,1024]{1,0:T(8,128)(2,1)} %tie.10), channel_id=1, source_target_pairs={{0,2},{2,0},{1,3},{3,1},{4,6},{6,4},{5,7},{7,5},{8,10},{10,8},{9,1... | collective-permute-start | bytes 3145736 | tf_op jit(solution)/shard_map/ppermute | solution.py:36
  273.3 15.5 %collective-permute-start.30 = (bf16[1024,256]{1,0:T(8,128)(2,1)S(1)}, bf16[1024,256]{1,0:T(8,128)(2,1)S(1)}, u32[]{:S(2)}, u32[]{:S(2)}) collective-permute-start(bf16[1024,256]{1,0:T(8,128)(2,1)S(1)} %fusion), channel_id=1, source_target_pairs={{0,1},{1,0},{2,3},{3,2},{4,5},{5,4},{6,7},{7,6},{8,9},{9,8},{10,11... | collective-permute-start | bytes 1572872 | tf_op jit(solution)/shard_map/ppermute | solution.py:40
  295.0 22.0 %collective-permute-start.33 = (bf16[4,128,640]{2,1,0:T(8,128)(2,1)}, bf16[4,128,640]{2,1,0:T(8,128)(2,1)}, u32[]{:S(2)}, u32[]{:S(2)}) collective-permute-start(bf16[4,128,640]{2,1,0:T(8,128)(2,1)} %get-tuple-element.85.rest_1_), channel_id=1, source_target_pairs={{0,4},{4,0},{8,12},{12,8},{16,20},{20,16},{24,28},{28,24},{1,5},{5... | collective-permute-start | bytes 1966088 | tf_op jit(solution)/shard_map/ppermute | solution.py:793
  296.6 30.9 %collective-permute-start.32 = (bf16[1024,384]{1,0:T(8,128)(2,1)}, bf16[1024,384]{1,0:T(8,128)(2,1)}, u32[]{:S(2)}, u32[]{:S(2)}) collective-permute-start(bf16[1024,384]{1,0:T(8,128)(2,1)} %get-tuple-element.90), channel_id=1, source_target_pairs={{0,1},{1,0},{2,3},{3,2},{4,5},{5,4},{6,7},{7,6},{8,9},{9,8},{10,11... | collective-permute-start | bytes 2359304 | tf_op jit(solution)/shard_map/ppermute | solution.py:40
  317.1 10.4 %collective-permute-start.34 = (bf16[1024,384]{1,0:T(8,128)(2,1)}, bf16[1024,384]{1,0:T(8,128)(2,1)}, u32[]{:S(2)}, u32[]{:S(2)}) collective-permute-start(bf16[1024,384]{1,0:T(8,128)(2,1)} %tie.12), channel_id=1, source_target_pairs={{0,1},{1,0},{2,3},{3,2},{4,5},{5,4},{6,7},{7,6},{8,9},{9,8},{10,11... | collective-permute-start | bytes 2359304 | tf_op jit(solution)/shard_map/ppermute | solution.py:40
  339.1 19.2 %collective-permute-start.36 = (bf16[4,144,384]{2,1,0:T(8,128)(2,1)S(1)}, bf16[4,144,384]{2,1,0:T(8,128)(2,1)S(1)}, u32[]{:S(2)}, u32[]{:S(2)}) collective-permute-start(bf16[4,144,384]{2,1,0:T(8,128)(2,1)S(1)} %pad_maximum_fusion.5), channel_id=1, source_target_pairs={{0,4},{4,0},{8,12},{12,8},{16,20},{20,16},{24,28},{28,24},{1,5},{5... | collective-permute-start | bytes 1327112 | tf_op jit(solution)/shard_map/ppermute | solution.py:793
  343.7 14.6 %collective-permute-start.38 = (bf16[128,640]{1,0:T(8,128)(2,1)S(1)}, bf16[128,640]{1,0:T(8,128)(2,1)S(1)}, u32[]{:S(2)}, u32[]{:S(2)}) collective-permute-start(bf16[128,640]{1,0:T(8,128)(2,1)S(1)} %get-tuple-element.119), channel_id=1, source_target_pairs={{0,16},{4,20},{8,24},{12,28},{16,0},{20,4},{24,8},{28,12},{1,17},{... | collective-permute-start | bytes 491528 | tf_op jit(solution)/shard_map/ppermute | solution.py:793
  343.8 14.5 %collective-permute-start.39 = (bf16[128,640]{1,0:T(8,128)(2,1)S(1)}, bf16[128,640]{1,0:T(8,128)(2,1)S(1)}, u32[]{:S(2)}, u32[]{:S(2)}) collective-permute-start(bf16[128,640]{1,0:T(8,128)(2,1)S(1)} %get-tuple-element.118), channel_id=1, source_target_pairs={{0,8},{4,12},{8,0},{12,4},{16,24},{20,28},{24,16},{28,20},{1,9},{5... | collective-permute-start | bytes 491528 | tf_op jit(solution)/shard_map/ppermute | solution.py:793
  347.2 29.0 %collective-permute-start.43 = (bf16[512,1024]{1,0:T(8,128)(2,1)}, bf16[512,1024]{1,0:T(8,128)(2,1)S(1)}, u32[]{:S(2)}, u32[]{:S(2)}) collective-permute-start(bf16[512,1024]{1,0:T(8,128)(2,1)} %get-tuple-element.100), channel_id=1, source_target_pairs={{0,2},{2,0},{1,3},{3,1},{4,6},{6,4},{5,7},{7,5},{8,10},{10,8},{9,1... | collective-permute-start | bytes 3145736 | tf_op jit(solution)/shard_map/ppermute | solution.py:36
  382.8 11.6 %collective-permute-start.46 = (f32[2,128]{1,0:T(2,128)S(1)}, f32[2,128]{1,0:T(2,128)S(1)}, u32[]{:S(2)}, u32[]{:S(2)}) collective-permute-start(f32[2,128]{1,0:T(2,128)S(1)} %slice.159), channel_id=1, source_target_pairs={{0,3},{1,2},{2,1},{3,0},{4,7},{5,6},{6,5},{7,4},{8,11},{9,10},{10,... | collective-permute-start | bytes 3080 | tf_op jit(solution)/shard_map/ppermute | solution.py:1147
  383.7 10.7 %collective-permute-start.45 = (f32[2,128]{1,0:T(2,128)S(1)}, f32[2,128]{1,0:T(2,128)S(1)}, u32[]{:S(2)}, u32[]{:S(2)}) collective-permute-start(f32[2,128]{1,0:T(2,128)S(1)} %slice.159), channel_id=1, source_target_pairs={{0,2},{2,0},{1,3},{3,1},{4,6},{6,4},{5,7},{7,5},{8,10},{10,8},{9,1... | collective-permute-start | bytes 3080 | tf_op jit(solution)/shard_map/ppermute | solution.py:36
  (125 other events, 905.0 us)
Sparse Core Ops, SparseCore 0:
  234.2 91.0 reduce-scatter.1

commit v2 on v1

--- a/solution.py
+++ b/solution.py
@@ -432,7 +432,7 @@
         + [pl.BlockSpec(vectors.shape, lambda i: (0, 0))],
         out_specs=strip,
         out_shape=jax.ShapeDtypeStruct((rows, width), BF16),
-        compiler_params=params(12),
+        compiler_params=params(60),
         cost_estimate=cost(4),
         name="norm_one_back",
     )(places, inputs, z_own, z_recv, *residual_grads, vectors)
@@ -901,7 +901,7 @@
             axis=0,
         )
         blocks.extend([low, high, sequence])
-        return (sequence, cot_x)
+        return (sequence,)
 
     if parts == 8:
         shares = {0: attn_shard, **gather_z(attn_shard)}
@@ -909,7 +909,8 @@
         for k in (0, 2, 4, 6):
             shares[k + 1] = swap_dp(shares[k], 1)
         mlp_shares.update(gather_z(tie(mlp_shard, *(shares[k] for k in (2, 4, 6)))))
-        behind = tuple(shares[k] for k in (6, 5, 3, 1)) + (mlp_shares[1], mlp_shares[4])
+        behind = tuple(shares[k] for k in (6, 5, 3, 1))
+        behind += (mlp_shares[1], mlp_shares[2], cot_x)
         for k in (2, 4):
             mlp_shares[k + 1] = swap_dp(mlp_shares[k], 1)
         attn_all = place_shares(
@@ -918,7 +919,7 @@
             side_rows,
             assemble(behind),
         )
-        early = (mlp_shares[3], mlp_shares[5], mlp_shares[6])
+        early = (mlp_shares[3], mlp_shares[4], mlp_shares[6])
     else:
         attn_all = gather_whole(attn_shard, side_rows)
         assemble((attn_all,))
@@ -1128,7 +1129,7 @@
             received = tie(scatter_y(sent, parts), *first_terms[1:])
         terms.append(scatter_z(kept, sent, received, side if last else None, parts))
 
-    out_recv = tie(out_recv, *terms[-1][1:])
+    out_recv = tie(out_recv, z_sent)
     out_mine = pick_x(out_parts[0], out_parts[1])
     outputs = (
         pick_x(residuals[0], residuals[1])

time: 407 us -> 399 us (0.980)
  waiting for transfers between devices: 110 us -> 88.2 us
  starting transfers between devices: 39.7 us -> 56.4 us
  local copies, waits for them, and re-layouts: 72.4 us -> 66.7 us
    ppermute x9, waiting for transfers between devices: 30.6 us -> 12.5 us  [swap_x(): return lax.ppermute(value, 'tensor', [(0, 2), (2, 0), (1, 3), (3, 1)])]
    ppermute x22, starting transfers between devices: 28.7 us -> 42.5 us  [swap_dp(): return lax.ppermute(value, 'dp', [(i, i ^ mask) for i in range(size)])]
    unnamed x223 -> x215, local copies, waits for them, and re-layouts: 60.7 us -> 54.9 us
  transfers between devices with their start and end apart: 48 -> 48, of which waited for: 23 -> 21; matrix products, arithmetic and copies ran while one was open for 8% -> 8% of each run, Pallas kernels for 32% -> 33%
where the time goes in v2:
time: 399 us; the launch traced here: 395 us
  Pallas kernels  146 us (37%)
  waiting for transfers between devices  88.2 us (22%)
  local copies, waits for them, and re-layouts  66.7 us (17%)
  starting transfers between devices  56.4 us (14%)
  other arithmetic  19.6 us (5%)
  between operations  15.9 us (4%)
    ppermute x22, waiting for transfers between devices, swap_dp(): return lax.ppermute(value, 'dp', [(i, i ^ mask) for i in range(size)])  69.3 us
    unnamed x215, local copies, waits for them, and re-layouts  54.9 us
    ppermute x22, starting transfers between devices, swap_dp(): return lax.ppermute(value, 'dp', [(i, i ^ mask) for i in range(size)])  42.5 us
    pallas_call x3, Pallas kernels, attend_back(): pl.pallas_call(functools.partial(attend_back_kernel, row0=row0, block=blo...  36.7 us
    pallas_call x2, Pallas kernels, feed(): pl.pallas_call(functools.partial(feed_kernel, tiles=tiles), grid=(2 * til...  31.1 us
    pallas_call x2, Pallas kernels, attend(): pl.pallas_call(functools.partial(attend_kernel, row0=row0, block=block),...  21.3 us
    ppermute x9, waiting for transfers between devices, swap_x(): return lax.ppermute(value, 'tensor', [(0, 2), (2, 0), (1, 3), (3, 1)])  12.5 us
    pallas_call x2, Pallas kernels, feed_grads(): pl.pallas_call(functools.partial(feed_grads_kernel, tiles=tiles, received...  12.4 us
  transfers between devices with their start and end apart: 48, of which 21 were waited for; matrix products, arithmetic and copies ran while one was open for 8% of the time, Pallas kernels for 33%

profile of v2, /device:TPU:0, one launch (start us, length us, event | category | flops | bytes accessed | tf_op | source)
XLA Modules:
  0.0 395.0 jit_solution(16661673543401808507)
XLA Ops:
  11.0 5.1 %collective-permute-start.1 = (bf16[144,1024]{1,0:T(8,128)(2,1)S(1)}, bf16[144,1024]{1,0:T(8,128)(2,1)S(1)}, u32[]{:S(2)}, u32[]{:S(2)}) collective-permute-start(bf16[144,1024]{1,0:T(8,128)(2,1)S(1)} %fusion.8.refs_0_), channel_id=1, source_target_pairs={{0,24},{4,28},{8,16},{12,20},{16,8},{20,12},{24,0},{28,4},{1,25},{... | collective-permute-start | bytes 884744 | tf_op jit(solution)/shard_map/ppermute | solution.py:793
  20.0 4.2 %collective-permute-done.1.rest_2_.rest_0_.refs_6_ = bf16[144,1024]{1,0:T(8,128)(2,1)S(1)} collective-permute-done((bf16[144,1024]{1,0:T(8,128)(2,1)S(1)}, bf16[144,1024]{1,0:T(8,128)(2,1)S(1)}, u32[]{:S(2)}, u32[]{:S(2)}) %collective-permute-start.1) | collective-permute-done | bytes 294944 | tf_op jit(solution)/shard_map/ppermute | solution.py:793
  25.9 15.4 %collective-permute-done.2.rest_1_.refs_4_ = bf16[144,1024]{1,0:T(8,128)(2,1)S(1)} collective-permute-done((bf16[144,1024]{1,0:T(8,128)(2,1)S(1)}, bf16[144,1024]{1,0:T(8,128)(2,1)S(1)}, u32[]{:S(2)}, u32[]{:S(2)}) %collective-permute-start.2) | collective-permute-done | bytes 294944 | tf_op jit(solution)/shard_map/ppermute | solution.py:793
  44.4 5.0 %collective-permute-done.6.rest_3_.refs_1_ = bf16[144,1024]{1,0:T(8,128)(2,1)S(1)} collective-permute-done((bf16[144,1024]{1,0:T(8,128)(2,1)S(1)}, bf16[144,1024]{1,0:T(8,128)(2,1)S(1)}, u32[]{:S(2)}, u32[]{:S(2)}) %collective-permute-start.6) | collective-permute-done | bytes 294944 | tf_op jit(solution)/shard_map/ppermute | solution.py:793
  51.4 8.1 %collective-permute-done.3.rest_1_.refs_5_ = bf16[144,1024]{1,0:T(8,128)(2,1)S(1)} collective-permute-done((bf16[144,1024]{1,0:T(8,128)(2,1)}, bf16[144,1024]{1,0:T(8,128)(2,1)S(1)}, u32[]{:S(2)}, u32[]{:S(2)}) %collective-permute-start.3) | collective-permute-done | bytes 294944 | tf_op jit(solution)/shard_map/ppermute | solution.py:793
  59.5 3.6 collective-permute-done.5.rest_2_.refs_3_
  75.1 5.1 %collective-permute-start.17 = (bf16[128,2048]{1,0:T(8,128)(2,1)}, bf16[128,2048]{1,0:T(8,128)(2,1)}, u32[]{:S(2)}, u32[]{:S(2)}) collective-permute-start(bf16[128,2048]{1,0:T(8,128)(2,1)} %tie.8), channel_id=1, source_target_pairs={{0,16},{4,20},{8,24},{12,28},{16,0},{20,4},{24,8},{28,12},{1,17},{... | collective-permute-start | bytes 1572872 | tf_op jit(solution)/shard_map/ppermute | solution.py:793
  86.2 6.1 %project.1 = (bf16[2048,1024]{1,0:T(8,128)(2,1)S(1)}, bf16[2048,768]{1,0:T(8,128)(2,1)S(1)}) custom-call(bf16[2048,1024]{1,0:T(8,128)(2,1)S(1)} %copy-done.3, f32[8,1024]{1,0:T(8,128)S(1)} %bitcast.102, f32[1,768]{1,0:T(1,128)S(1)} %reshape.138.shift_ref, bf16[1152,1024]{1,0:T(8,128)(2,1)S(1)} %place_shares.2.weight_ref.refs_4_.refs_5_), custom_call_target="tpu_custom_call" | custom-call | flops 1650000000 | bytes 1500000 | tf_op jit(solution)/shard_map/project/pallas_call | solution.py:644
  92.3 5.7 %attend_0.1 = (bf16[1024,256]{1,0:T(8,128)(2,1)S(1)}, f32[2,2,1024]{2,1,0:T(2,128)S(1)}) custom-call(bf16[2048,768]{1,0:T(8,128)(2,1)S(1)} %get-tuple-element.61.qkv_ref), custom_call_target="tpu_custom_call" | custom-call | flops 1650000000 | bytes 1500000 | tf_op jit(solution)/shard_map/attend_0/pallas_call | solution.py:136
  98.2 17.6 %collective-permute-done.17.rest_2_.refs_4_ = bf16[128,2048]{1,0:T(8,128)(2,1)} collective-permute-done((bf16[128,2048]{1,0:T(8,128)(2,1)}, bf16[128,2048]{1,0:T(8,128)(2,1)}, u32[]{:S(2)}, u32[]{:S(2)}) %collective-permute-start.17) | collective-permute-done | bytes 524320 | tf_op jit(solution)/shard_map/ppermute | solution.py:793
  121.5 15.6 %attend_1024.1 = (bf16[1024,256]{1,0:T(8,128)(2,1)S(1)}, f32[2,2,1024]{2,1,0:T(2,128)S(1)}) custom-call(bf16[2048,768]{1,0:T(8,128)(2,1)S(1)} %get-tuple-element.61.qkv_ref, bf16[512,1024]{1,0:T(8,128)(2,1)S(1)} %convolution_convert_fusion.1.rest_0_.part_ref, bf16[128,2048]{1,0:T(8,128)(2,1)} %collective-permute-done.16.rest_1_.refs_3_, ...), custom_call_target="tpu_custom_call" | custom-call | flops 4400000000 | bytes 4000000 | tf_op jit(solution)/shard_map/attend_1024/pallas_call | solution.py:136
  140.5 3.5 collective-permute-done.15.refs_8_.recv_ref
  155.1 16.5 %feed.2 = (f32[512,1024]{1,0:T(8,128)S(1)}, bf16[512,1024]{1,0:T(8,128)(2,1)S(1)}, bf16[512,2048]{1,0:T(8,128)(2,1)S(1)}, bf16[512,2048]{1,0:T(8,128)(2,1)S(1)},...) custom-call(bf16[512,1024]{1,0:T(8,128)(2,1)S(1)} %copy-done.10, ...), custom_call_target="tpu_custom_call" | custom-call | flops 4400000000 | bytes 4000000 | tf_op jit(solution)/shard_map/feed/pallas_call | solution.py:747
  182.9 14.7 %feed.3 = (f32[512,1024]{1,0:T(8,128)S(1)}, bf16[512,1024]{1,0:T(8,128)(2,1)S(1)}, bf16[512,2048]{1,0:T(8,128)(2,1)S(1)}, bf16[512,2048]{1,0:T(8,128)(2,1)S(1)},...) custom-call(bf16[512,1024]{1,0:T(8,128)(2,1)S(1)} %copy-done.13, ...), custom_call_target="tpu_custom_call" | custom-call | flops 4400000000 | bytes 4000000 | tf_op jit(solution)/shard_map/feed/pallas_call | solution.py:747
  201.3 5.9 %feed_grads.2.rest_0_ = bf16[1024,2048]{1,0:T(8,128)(2,1)S(1)} custom-call(bf16[512,1024]{1,0:T(8,128)(2,1)S(1)} %copy-done.43, bf16[512,1024]{1,0:T(8,128)(2,1)S(1)} %get-tuple-element.70.refs_1_, bf16[512,1024]{1,0:T(8,128)(2,1)S(1)} %copy-done.8, bf16[512,1024]{1,0:T(8,128)(2,1)S(1)} %copy-done.5, bf16[512,2048]{1,0:T(8,128)(2,1)S(1)} %get-tuple-element.71.refs_4_, ...), custom_call_target="tpu_custom_call" | custom-call | flops 1650000000 | bytes 1500000 | tf_op jit(solution)/shard_map/feed_grads/pallas_call | solution.py:515
  207.5 4.3 %norm_two.2 = (f32[512,1024]{1,0:T(8,128)S(1)}, bf16[512,1024]{1,0:T(8,128)(2,1)S(1)}, bf16[512,512]{1,0:T(8,128)(2,1)S(1)}, f32[8,1024]{1,0:T(8,128)S(1)}) custom-call(bf16[512,1024]{1,0:T(8,128)(2,1)} %get-tuple-element.68.back_ref, bf16[512,1024]{1,0:T(8,128)(2,1)} %collective-permute-done.24.refs_8_.recv_ref, ...), custom_call_target="tpu_custom_call" | custom-call | flops 1100000000 | bytes 1000000 | tf_op jit(solution)/shard_map/norm_two/pallas_call | solution.py:316
  214.5 6.4 %feed_grads.3.rest_0_ = bf16[1024,2048]{1,0:T(8,128)(2,1)S(1)} custom-call(bf16[512,1024]{1,0:T(8,128)(2,1)S(1)} %copy-done.44, bf16[512,1024]{1,0:T(8,128)(2,1)S(1)} %get-tuple-element.70.refs_1_, bf16[512,1024]{1,0:T(8,128)(2,1)S(1)} %copy-done.8, bf16[512,1024]{1,0:T(8,128)(2,1)S(1)} %copy-done.5, bf16[512,2048]{1,0:T(8,128)(2,1)S(1)} %copy-done.35, ...), custom_call_target="tpu_custom_call" | custom-call | flops 1650000000 | bytes 1500000 | tf_op jit(solution)/shard_map/feed_grads/pallas_call | solution.py:515
  231.6 10.9 %attend_back_0_0.1 = (f32[1024,768]{1,0:T(8,128)S(1)}, f32[1,768]{1,0:T(1,128)}) custom-call(s32[1]{0:T(128)} %constant.103.clone.1.core_ref, bf16[2048,768]{1,0:T(8,128)(2,1)S(1)} %copy-done.88, bf16[1024,256]{1,0:T(8,128)(2,1)S(1)} %copy-done.83, bf16[1024,256]{1,0:T(8,128)(2,1)S(1)} %pad_maximum_fusion.3.grad_ref, ...), custom_call_target="tpu_custom_call" | custom-call | flops 3024999936 | bytes 2750000 | tf_op jit(solution)/shard_map/attend_back_0_0/pallas_call | solution.py:259
  244.6 5.8 %collective-permute-done.28.recv_ref = bf16[512,1024]{1,0:T(8,128)(2,1)} collective-permute-done((bf16[512,1024]{1,0:T(8,128)(2,1)}, bf16[512,1024]{1,0:T(8,128)(2,1)}, u32[]{:S(2)}, u32[]{:S(2)}) %collective-permute-start.28) | collective-permute-done | bytes 1048608 | tf_op jit(solution)/shard_map/ppermute | solution.py:36
  256.4 4.3 %norm_two.3 = (f32[512,1024]{1,0:T(8,128)S(1)}, bf16[512,1024]{1,0:T(8,128)(2,1)S(1)}, bf16[512,512]{1,0:T(8,128)(2,1)S(1)}, f32[8,1024]{1,0:T(8,128)S(1)}) custom-call(bf16[512,1024]{1,0:T(8,128)(2,1)S(1)} %copy-done.67, bf16[512,1024]{1,0:T(8,128)(2,1)} %collective-permute-done.28.recv_ref, f32[512,1024]{1,0:T(8,128)S(1)} %copy-done.33, ...), custom_call_target="tpu_custom_call" | custom-call | flops 1100000000 | bytes 1000000 | tf_op jit(solution)/shard_map/norm_two/pallas_call | solution.py:316
  265.7 12.9 %attend_back_1024_0.1 = (bf16[2048,384]{1,0:T(8,128)(2,1)S(1)}, f32[1,384]{1,0:T(1,128)S(1)}, bf16[1024,384]{1,0:T(8,128)(2,1)S(1)}) custom-call(s32[1]{0:T(128)} %bitcast.27.core_ref, bf16[2048,768]{1,0:T(8,128)(2,1)S(1)} %copy-done.89, bf16[1024,256]{1,0:T(8,128)(2,1)S(1)} %copy-done.80, bf16[1024,256]{1,0:T(8,128)(2,1)S(1)} %pad_maximum_fusion.4.grad_ref, ...), custom_call_target="tpu_custom_call" | custom-call | flops 3575000064 | bytes 3250000 | tf_op jit(solution)/shard_map/attend_back_1024_0/pallas_call | solution.py:259
  278.7 5.4 %weight_grads.2 = (f32[4,128,640]{2,1,0:T(8,128)S(1)}, bf16[4,128,640]{2,1,0:T(8,128)(2,1)}) custom-call(s32[1]{0:T(128)} %bitcast.29.y_ref, bf16[2048,1024]{1,0:T(8,128)(2,1)S(1)} %copy-done.16, bf16[2048,384]{1,0:T(8,128)(2,1)S(1)} %get-tuple-element.82.rest_0_.grad_ref.refs_0_, bf16[512,1024]{1,0:T(8,128)(2,1)S(1)} %copy-done.29, ...), custom_call_target="tpu_custom_call" | custom-call | flops 1100000000 | bytes 1000000 | tf_op jit(solution)/shard_map/weight_grads/pallas_call | solution.py:567
  294.3 12.9 %attend_back_1024_1.1 = (bf16[2048,384]{1,0:T(8,128)(2,1)S(1)}, f32[1,384]{1,0:T(1,128)S(1)}, bf16[1024,384]{1,0:T(8,128)(2,1)S(1)}) custom-call(s32[1]{0:T(128)} %bitcast.27.core_ref, bf16[2048,768]{1,0:T(8,128)(2,1)S(1)} %copy-done.90, bf16[1024,256]{1,0:T(8,128)(2,1)S(1)} %copy-done.81, bf16[1024,256]{1,0:T(8,128)(2,1)S(1)} %copy-done.78, ...), custom_call_target="tpu_custom_call" | custom-call | flops 3575000064 | bytes 3250000 | tf_op jit(solution)/shard_map/attend_back_1024_1/pallas_call | solution.py:259
  313.2 3.6 weight_grads.3
  321.1 10.2 %collective-permute-start.36 = (bf16[128,640]{1,0:T(8,128)(2,1)}, bf16[128,640]{1,0:T(8,128)(2,1)}, u32[]{:S(2)}, u32[]{:S(2)}) collective-permute-start(bf16[128,640]{1,0:T(8,128)(2,1)} %get-tuple-element.119), channel_id=1, source_target_pairs={{0,16},{4,20},{8,24},{12,28},{16,0},{20,4},{24,8},{28,12},{1,17},{... | collective-permute-start | bytes 491528 | tf_op jit(solution)/shard_map/ppermute | solution.py:793
  332.2 9.9 %norm_one.1 = (f32[512,1024]{1,0:T(8,128)S(1)}, bf16[512,1024]{1,0:T(8,128)(2,1)}, f32[8,1024]{1,0:T(8,128)S(1)}) custom-call(s32[2]{0:T(128)S(1)} %pad_add_fusion.place_ref, bf16[512,1024]{1,0:T(8,128)(2,1)S(1)} %copy-done.11, bf16[512,1024]{1,0:T(8,128)(2,1)S(1)} %copy-done.14, bf16[2048,384]{1,0:T(8,128)(2,1)S(1)} %copy-done.23, ...), custom_call_target="tpu_custom_call" | custom-call | flops 2200000000 | bytes 2000000 | tf_op jit(solution)/shard_map/norm_one/pallas_call | solution.py:382
  348.5 3.1 add_convert_fusion.refs_9_
  351.6 7.3 %collective-permute-done.40.value_ref = bf16[4,144,384]{2,1,0:T(8,128)(2,1)} collective-permute-done((bf16[4,144,384]{2,1,0:T(8,128)(2,1)}, bf16[4,144,384]{2,1,0:T(8,128)(2,1)}, u32[]{:S(2)}, u32[]{:S(2)}) %collective-permute-start.40) | collective-permute-done | bytes 442400 | tf_op jit(solution)/shard_map/ppermute | solution.py:793
  365.3 2.7 collective-permute-done.41.refs_5_
  367.9 3.8 collective-permute-done.42.refs_6_
  372.4 2.9 finish.1
  380.0 5.9 %norm_one_back.1 = bf16[512,1024]{1,0:T(8,128)(2,1)} custom-call(s32[2]{0:T(128)} %copy-done.86, bf16[512,1024]{1,0:T(8,128)(2,1)} %input_ref.1, f32[512,1024]{1,0:T(8,128)} %copy-done.49, bf16[512,1024]{1,0:T(8,128)(2,1)} %tie.15.recv_ref, f32[512,1024]{1,0:T(8,128)} %copy-done.47, f32[512,1024]{1,0:T(8,128)} %copy-done.48, f32[8,1024]{1,0:T(8,128)} %bitcast.107), custom_call_target="tpu_custom_call" | custom-call | flops 1100000000 | bytes 1000000 | tf_op jit(solution)/shard_map/norm_one_back/pallas_call | solution.py:427
  (378 shorter events, 134.9 us)
Async XLA Ops:
  7.2 364.6 %reduce-scatter.2.cloned.1.call-start = ((), (), s32[]{:S(2)}) async-start(), calls=%async_computation.1 | async-start | bytes 4718592 | tf_op jit(solution)/shard_map/reduce_scatter | solution.py:1038
  11.0 13.1 %collective-permute-start.1 = (bf16[144,1024]{1,0:T(8,128)(2,1)S(1)}, bf16[144,1024]{1,0:T(8,128)(2,1)S(1)}, u32[]{:S(2)}, u32[]{:S(2)}) collective-permute-start(bf16[144,1024]{1,0:T(8,128)(2,1)S(1)} %fusion.8.refs_0_), channel_id=1, source_target_pairs={{0,24},{4,28},{8,16},{12,20},{16,8},{20,12},{24,0},{28,4},{1,25},{... | collective-permute-start | bytes 884744 | tf_op jit(solution)/shard_map/ppermute | solution.py:793
  16.2 25.1 %collective-permute-start.2 = (bf16[144,1024]{1,0:T(8,128)(2,1)S(1)}, bf16[144,1024]{1,0:T(8,128)(2,1)S(1)}, u32[]{:S(2)}, u32[]{:S(2)}) collective-permute-start(bf16[144,1024]{1,0:T(8,128)(2,1)S(1)} %fusion.8.refs_0_), channel_id=1, source_target_pairs={{0,16},{4,20},{8,24},{12,28},{16,0},{20,4},{24,8},{28,12},{1,17},{... | collective-permute-start | bytes 884744 | tf_op jit(solution)/shard_map/ppermute | solution.py:793
  16.2 27.4 %collective-permute-start.4 = (bf16[144,1024]{1,0:T(8,128)(2,1)S(1)}, bf16[144,1024]{1,0:T(8,128)(2,1)S(1)}, u32[]{:S(2)}, u32[]{:S(2)}) collective-permute-start(bf16[144,1024]{1,0:T(8,128)(2,1)S(1)} %fusion.8.refs_0_), channel_id=1, source_target_pairs={{0,8},{4,12},{8,0},{12,4},{16,24},{20,28},{24,16},{28,20},{1,9},{5... | collective-permute-start | bytes 884744 | tf_op jit(solution)/shard_map/ppermute | solution.py:793
  16.8 46.3 %collective-permute-start = (bf16[512,1024]{1,0:T(8,128)(2,1)}, bf16[512,1024]{1,0:T(8,128)(2,1)}, u32[]{:S(2)}, u32[]{:S(2)}) collective-permute-start(bf16[512,1024]{1,0:T(8,128)(2,1)} %input_ref.1), channel_id=1, source_target_pairs={{0,2},{2,0},{1,3},{3,1},{4,6},{6,4},{5,7},{7,5},{8,10},{10,8},{9,1... | collective-permute-start | bytes 3145736 | tf_op jit(solution)/shard_map/ppermute | solution.py:36
  18.4 45.5 %collective-permute-start.9 = (bf16[512,1024]{1,0:T(8,128)(2,1)}, bf16[512,1024]{1,0:T(8,128)(2,1)}, u32[]{:S(2)}, u32[]{:S(2)}) collective-permute-start(bf16[512,1024]{1,0:T(8,128)(2,1)} %param.27), channel_id=1, source_target_pairs={{0,2},{2,0},{1,3},{3,1},{4,6},{6,4},{5,7},{7,5},{8,10},{10,8},{9,1... | collective-permute-start | bytes 3145736 | tf_op jit(solution)/shard_map/ppermute | solution.py:36
  24.1 26.7 %collective-permute-start.7 = (bf16[128,2048]{1,0:T(8,128)(2,1)S(1)}, bf16[128,2048]{1,0:T(8,128)(2,1)S(1)}, u32[]{:S(2)}, u32[]{:S(2)}) collective-permute-start(bf16[128,2048]{1,0:T(8,128)(2,1)S(1)} %pad_maximum_fusion.2.refs_0_), channel_id=1, source_target_pairs={{0,4},{4,0},{8,12},{12,8},{16,20},{20,16},{24,28},{28,24},{1,5},{5... | collective-permute-start | bytes 1572872 | tf_op jit(solution)/shard_map/ppermute | solution.py:793
  44.3 18.8 %collective-permute-start.8 = (bf16[128,2048]{1,0:T(8,128)(2,1)}, bf16[128,2048]{1,0:T(8,128)(2,1)}, u32[]{:S(2)}, u32[]{:S(2)}) collective-permute-start(bf16[128,2048]{1,0:T(8,128)(2,1)} %tie.8), channel_id=1, source_target_pairs={{0,8},{4,12},{8,0},{12,4},{16,24},{20,28},{24,16},{28,20},{1,9},{5... | collective-permute-start | bytes 1572872 | tf_op jit(solution)/shard_map/ppermute | solution.py:793
  49.3 10.2 %collective-permute-start.3 = (bf16[144,1024]{1,0:T(8,128)(2,1)}, bf16[144,1024]{1,0:T(8,128)(2,1)S(1)}, u32[]{:S(2)}, u32[]{:S(2)}) collective-permute-start(bf16[144,1024]{1,0:T(8,128)(2,1)} %copy-done.56), channel_id=1, source_target_pairs={{0,4},{4,0},{8,12},{12,8},{16,20},{20,16},{24,28},{28,24},{1,5},{5... | collective-permute-start | bytes 884744 | tf_op jit(solution)/shard_map/ppermute | solution.py:793
  50.9 12.3 %collective-permute-start.5 = (bf16[144,1024]{1,0:T(8,128)(2,1)}, bf16[144,1024]{1,0:T(8,128)(2,1)S(1)}, u32[]{:S(2)}, u32[]{:S(2)}) collective-permute-start(bf16[144,1024]{1,0:T(8,128)(2,1)} %copy-done.58), channel_id=1, source_target_pairs={{0,4},{4,0},{8,12},{12,8},{16,20},{20,16},{24,28},{28,24},{1,5},{5... | collective-permute-start | bytes 884744 | tf_op jit(solution)/shard_map/ppermute | solution.py:793
  74.9 43.0 %collective-permute-start.14 = (bf16[1152,1024]{1,0:T(8,128)(2,1)S(1)}, bf16[1152,1024]{1,0:T(8,128)(2,1)}, u32[]{:S(2)}, u32[]{:S(2)}) collective-permute-start(bf16[1152,1024]{1,0:T(8,128)(2,1)S(1)} %place_shares.2.weight_ref.refs_4_.refs_5_), channel_id=1, source_target_pairs={{0,1},{1,0},{2,3},{3,2},{4,5},{5,4},{6,7},{7,6},{8,9},{9,8},{10,11... | collective-permute-start | bytes 7077896 | tf_op jit(solution)/shard_map/ppermute | solution.py:40
  75.1 40.6 %collective-permute-start.17 = (bf16[128,2048]{1,0:T(8,128)(2,1)}, bf16[128,2048]{1,0:T(8,128)(2,1)}, u32[]{:S(2)}, u32[]{:S(2)}) collective-permute-start(bf16[128,2048]{1,0:T(8,128)(2,1)} %tie.8), channel_id=1, source_target_pairs={{0,16},{4,20},{8,24},{12,28},{16,0},{20,4},{24,8},{28,12},{1,17},{... | collective-permute-start | bytes 1572872 | tf_op jit(solution)/shard_map/ppermute | solution.py:793
  80.2 37.1 %collective-permute-start.19 = (bf16[128,2048]{1,0:T(8,128)(2,1)}, bf16[128,2048]{1,0:T(8,128)(2,1)}, u32[]{:S(2)}, u32[]{:S(2)}) collective-permute-start(bf16[128,2048]{1,0:T(8,128)(2,1)} %tie.8), channel_id=1, source_target_pairs={{0,24},{4,28},{8,16},{12,20},{16,8},{20,12},{24,0},{28,4},{1,25},{... | collective-permute-start | bytes 1572872 | tf_op jit(solution)/shard_map/ppermute | solution.py:793
  82.0 39.5 %collective-permute-start.16 = (bf16[128,2048]{1,0:T(8,128)(2,1)}, bf16[128,2048]{1,0:T(8,128)(2,1)}, u32[]{:S(2)}, u32[]{:S(2)}) collective-permute-start(bf16[128,2048]{1,0:T(8,128)(2,1)} %collective-permute-done.8.rest_5_.refs_2_), channel_id=1, source_target_pairs={{0,4},{4,0},{8,12},{12,8},{16,20},{20,16},{24,28},{28,24},{1,5},{5... | collective-permute-start | bytes 1572872 | tf_op jit(solution)/shard_map/ppermute | solution.py:793
  98.1 21.1 %collective-permute-start.13 = (bf16[512,256]{1,0:T(8,128)(2,1)S(1)}, bf16[512,256]{1,0:T(8,128)(2,1)S(1)}, u32[]{:S(2)}, u32[]{:S(2)}) collective-permute-start(bf16[512,256]{1,0:T(8,128)(2,1)S(1)} %get-tuple-element.131), channel_id=1, source_target_pairs={{0,1},{1,0},{2,3},{3,2},{4,5},{5,4},{6,7},{7,6},{8,9},{9,8},{10,11... | collective-permute-start | bytes 786440 | tf_op jit(solution)/shard_map/ppermute | solution.py:40
  115.8 23.8 %collective-permute-start.18 = (bf16[128,2048]{1,0:T(8,128)(2,1)}, bf16[128,2048]{1,0:T(8,128)(2,1)S(1)}, u32[]{:S(2)}, u32[]{:S(2)}) collective-permute-start(bf16[128,2048]{1,0:T(8,128)(2,1)} %collective-permute-done.17.rest_2_.refs_4_), channel_id=1, source_target_pairs={{0,4},{4,0},{8,12},{12,8},{16,20},{20,16},{24,28},{28,24},{1,5},{5... | collective-permute-start | bytes 1572872 | tf_op jit(solution)/shard_map/ppermute | solution.py:793
  117.3 23.2 %collective-permute-start.20 = (bf16[128,2048]{1,0:T(8,128)(2,1)}, bf16[128,2048]{1,0:T(8,128)(2,1)S(1)}, u32[]{:S(2)}, u32[]{:S(2)}) collective-permute-start(bf16[128,2048]{1,0:T(8,128)(2,1)} %collective-permute-done.19.rest_3_.refs_6_), channel_id=1, source_target_pairs={{0,4},{4,0},{8,12},{12,8},{16,20},{20,16},{24,28},{28,24},{1,5},{5... | collective-permute-start | bytes 1572872 | tf_op jit(solution)/shard_map/ppermute | solution.py:793
  119.9 24.1 %collective-permute-start.15 = (bf16[512,1024]{1,0:T(8,128)(2,1)S(1)}, bf16[512,1024]{1,0:T(8,128)(2,1)S(1)}, u32[]{:S(2)}, u32[]{:S(2)}) collective-permute-start(bf16[512,1024]{1,0:T(8,128)(2,1)S(1)} %convolution_convert_fusion.1.rest_0_.part_ref), channel_id=1, source_target_pairs={{0,2},{2,0},{1,3},{3,1},{4,6},{6,4},{5,7},{7,5},{8,10},{10,8},{9,1... | collective-permute-start | bytes 3145736 | tf_op jit(solution)/shard_map/ppermute | solution.py:36
  149.3 26.7 %collective-permute-start.23 = (bf16[512,1024]{1,0:T(8,128)(2,1)S(1)}, bf16[512,1024]{1,0:T(8,128)(2,1)S(1)}, u32[]{:S(2)}, u32[]{:S(2)}) collective-permute-start(bf16[512,1024]{1,0:T(8,128)(2,1)S(1)} %convolution_convert_fusion.refs_9_.rest_0_.part_ref), channel_id=1, source_target_pairs={{0,2},{2,0},{1,3},{3,1},{4,6},{6,4},{5,7},{7,5},{8,10},{10,8},{9,1... | collective-permute-start | bytes 3145736 | tf_op jit(solution)/shard_map/ppermute | solution.py:36
  174.5 25.5 %collective-permute-start.24 = (bf16[512,1024]{1,0:T(8,128)(2,1)}, bf16[512,1024]{1,0:T(8,128)(2,1)}, u32[]{:S(2)}, u32[]{:S(2)}) collective-permute-start(bf16[512,1024]{1,0:T(8,128)(2,1)} %get-tuple-element.68.back_ref), channel_id=1, source_target_pairs={{0,2},{2,0},{1,3},{3,1},{4,6},{6,4},{5,7},{7,5},{8,10},{10,8},{9,1... | collective-permute-start | bytes 3145736 | tf_op jit(solution)/shard_map/ppermute | solution.py:36
  224.0 26.4 %collective-permute-start.28 = (bf16[512,1024]{1,0:T(8,128)(2,1)}, bf16[512,1024]{1,0:T(8,128)(2,1)}, u32[]{:S(2)}, u32[]{:S(2)}) collective-permute-start(bf16[512,1024]{1,0:T(8,128)(2,1)} %copy-done.66), channel_id=1, source_target_pairs={{0,2},{2,0},{1,3},{3,1},{4,6},{6,4},{5,7},{7,5},{8,10},{10,8},{9,1... | collective-permute-start | bytes 3145736 | tf_op jit(solution)/shard_map/ppermute | solution.py:36
  244.1 44.3 %collective-permute-start.27 = (bf16[512,1024]{1,0:T(8,128)(2,1)}, bf16[512,1024]{1,0:T(8,128)(2,1)}, u32[]{:S(2)}, u32[]{:S(2)}) collective-permute-start(bf16[512,1024]{1,0:T(8,128)(2,1)} %tie.10), channel_id=1, source_target_pairs={{0,2},{2,0},{1,3},{3,1},{4,6},{6,4},{5,7},{7,5},{8,10},{10,8},{9,1... | collective-permute-start | bytes 3145736 | tf_op jit(solution)/shard_map/ppermute | solution.py:36
  263.8 14.9 %collective-permute-start.30 = (bf16[1024,256]{1,0:T(8,128)(2,1)S(1)}, bf16[1024,256]{1,0:T(8,128)(2,1)S(1)}, u32[]{:S(2)}, u32[]{:S(2)}) collective-permute-start(bf16[1024,256]{1,0:T(8,128)(2,1)S(1)} %fusion), channel_id=1, source_target_pairs={{0,1},{1,0},{2,3},{3,2},{4,5},{5,4},{6,7},{7,6},{8,9},{9,8},{10,11... | collective-permute-start | bytes 1572872 | tf_op jit(solution)/shard_map/ppermute | solution.py:40
  285.2 24.1 %collective-permute-start.32 = (bf16[4,128,640]{2,1,0:T(8,128)(2,1)}, bf16[4,128,640]{2,1,0:T(8,128)(2,1)}, u32[]{:S(2)}, u32[]{:S(2)}) collective-permute-start(bf16[4,128,640]{2,1,0:T(8,128)(2,1)} %get-tuple-element.85.rest_1_), channel_id=1, source_target_pairs={{0,4},{4,0},{8,12},{12,8},{16,20},{20,16},{24,28},{28,24},{1,5},{5... | collective-permute-start | bytes 1966088 | tf_op jit(solution)/shard_map/ppermute | solution.py:793
  288.1 44.0 %collective-permute-start.31 = (bf16[1024,384]{1,0:T(8,128)(2,1)}, bf16[1024,384]{1,0:T(8,128)(2,1)S(1)}, u32[]{:S(2)}, u32[]{:S(2)}) collective-permute-start(bf16[1024,384]{1,0:T(8,128)(2,1)} %copy-done.91), channel_id=1, source_target_pairs={{0,1},{1,0},{2,3},{3,2},{4,5},{5,4},{6,7},{7,6},{8,9},{9,8},{10,11... | collective-permute-start | bytes 2359304 | tf_op jit(solution)/shard_map/ppermute | solution.py:40
  309.3 22.8 %collective-permute-start.33 = (bf16[1024,384]{1,0:T(8,128)(2,1)}, bf16[1024,384]{1,0:T(8,128)(2,1)S(1)}, u32[]{:S(2)}, u32[]{:S(2)}) collective-permute-start(bf16[1024,384]{1,0:T(8,128)(2,1)} %tie.12), channel_id=1, source_target_pairs={{0,1},{1,0},{2,3},{3,2},{4,5},{5,4},{6,7},{7,6},{8,9},{9,8},{10,11... | collective-permute-start | bytes 2359304 | tf_op jit(solution)/shard_map/ppermute | solution.py:40
  319.3 32.3 %collective-permute-start.35 = (bf16[128,640]{1,0:T(8,128)(2,1)}, bf16[128,640]{1,0:T(8,128)(2,1)}, u32[]{:S(2)}, u32[]{:S(2)}) collective-permute-start(bf16[128,640]{1,0:T(8,128)(2,1)} %get-tuple-element.120), channel_id=1, source_target_pairs={{0,24},{4,28},{8,16},{12,20},{16,8},{20,12},{24,0},{28,4},{1,25},{... | collective-permute-start | bytes 491528 | tf_op jit(solution)/shard_map/ppermute | solution.py:793
  321.1 30.5 %collective-permute-start.36 = (bf16[128,640]{1,0:T(8,128)(2,1)}, bf16[128,640]{1,0:T(8,128)(2,1)}, u32[]{:S(2)}, u32[]{:S(2)}) collective-permute-start(bf16[128,640]{1,0:T(8,128)(2,1)} %get-tuple-element.119), channel_id=1, source_target_pairs={{0,16},{4,20},{8,24},{12,28},{16,0},{20,4},{24,8},{28,12},{1,17},{... | collective-permute-start | bytes 491528 | tf_op jit(solution)/shard_map/ppermute | solution.py:793
  331.4 20.3 %collective-permute-start.37 = (bf16[128,640]{1,0:T(8,128)(2,1)}, bf16[128,640]{1,0:T(8,128)(2,1)}, u32[]{:S(2)}, u32[]{:S(2)}) collective-permute-start(bf16[128,640]{1,0:T(8,128)(2,1)} %get-tuple-element.118), channel_id=1, source_target_pairs={{0,8},{4,12},{8,0},{12,4},{16,24},{20,28},{24,16},{28,20},{1,9},{5... | collective-permute-start | bytes 491528 | tf_op jit(solution)/shard_map/ppermute | solution.py:793
  343.4 28.3 %collective-permute-start.34 = (bf16[512,1024]{1,0:T(8,128)(2,1)}, bf16[512,1024]{1,0:T(8,128)(2,1)}, u32[]{:S(2)}, u32[]{:S(2)}) collective-permute-start(bf16[512,1024]{1,0:T(8,128)(2,1)} %get-tuple-element.90.rest_0_), channel_id=1, source_target_pairs={{0,2},{2,0},{1,3},{3,1},{4,6},{6,4},{5,7},{7,5},{8,10},{10,8},{9,1... | collective-permute-start | bytes 3145736 | tf_op jit(solution)/shard_map/ppermute | solution.py:36
  347.0 11.9 %collective-permute-start.40 = (bf16[4,144,384]{2,1,0:T(8,128)(2,1)}, bf16[4,144,384]{2,1,0:T(8,128)(2,1)}, u32[]{:S(2)}, u32[]{:S(2)}) collective-permute-start(bf16[4,144,384]{2,1,0:T(8,128)(2,1)} %pad_maximum_fusion.5), channel_id=1, source_target_pairs={{0,4},{4,0},{8,12},{12,8},{16,20},{20,16},{24,28},{28,24},{1,5},{5... | collective-permute-start | bytes 1327112 | tf_op jit(solution)/shard_map/ppermute | solution.py:793
  361.9 9.8 %collective-permute-start.42 = (bf16[144,384]{1,0:T(8,128)(2,1)S(1)}, bf16[144,384]{1,0:T(8,128)(2,1)S(1)}, u32[]{:S(2)}, u32[]{:S(2)}) collective-permute-start(bf16[144,384]{1,0:T(8,128)(2,1)S(1)} %get-tuple-element.122), channel_id=1, source_target_pairs={{0,16},{4,20},{8,24},{12,28},{16,0},{20,4},{24,8},{28,12},{1,17},{... | collective-permute-start | bytes 331784 | tf_op jit(solution)/shard_map/ppermute | solution.py:793
  (121 other events, 1005.6 us)
Sparse Core Ops, SparseCore 0:
  224.1 107.7 reduce-scatter.1

commit v3 on v2

--- a/solution.py
+++ b/solution.py
@@ -151,7 +151,7 @@
             pltpu.VMEM((2, block, PAIR), F32),
         ],
         compiler_params=params(16),
-        cost_estimate=cost(16 if row0 else 6),
+        cost_estimate=cost(0.01),
         name="attend_%d" % row0,
     )(qkv, *after)
 
@@ -660,7 +660,7 @@
             jax.ShapeDtypeStruct((length, cols), BF16),
         ],
         compiler_params=params(16),
-        cost_estimate=cost(6),
+        cost_estimate=cost(0.01),
         name="project",
     )(sequence, vectors, shift, weights, *after)
 
@@ -919,7 +919,7 @@
             side_rows,
             assemble(behind),
         )
-        early = (mlp_shares[3], mlp_shares[4], mlp_shares[6])
+        early = (mlp_shares[3],)
     else:
         attn_all = gather_whole(attn_shard, side_rows)
         assemble((attn_all,))

time: 399 us -> 405 us (1.015)
  waiting for transfers between devices: 88.2 us -> 97.7 us
    ppermute x22, waiting for transfers between devices: 69.3 us -> 82.3 us  [swap_dp(): return lax.ppermute(value, 'dp', [(i, i ^ mask) for i in range(size)])]
    unnamed x215 -> x221, local copies, waits for them, and re-layouts: 54.9 us -> 56.7 us
  transfers between devices with their start and end apart: 48 -> 48, of which waited for: 21 -> 20; matrix products, arithmetic and copies ran while one was open for 8% -> 7% of each run, Pallas kernels for 33% -> 32%
where the time goes in v3:
time: 405 us; the launch traced here: 401 us
  Pallas kernels  144 us (36%)
  waiting for transfers between devices  97.7 us (24%)
  local copies, waits for them, and re-layouts  68.5 us (17%)
  starting transfers between devices  52.7 us (13%)
  other arithmetic  19.6 us (5%)
  between operations  15.8 us (4%)
    ppermute x22, waiting for transfers between devices, swap_dp(): return lax.ppermute(value, 'dp', [(i, i ^ mask) for i in range(size)])  82.3 us
    unnamed x221, local copies, waits for them, and re-layouts  56.7 us
    ppermute x22, starting transfers between devices, swap_dp(): return lax.ppermute(value, 'dp', [(i, i ^ mask) for i in range(size)])  38.7 us
    pallas_call x3, Pallas kernels, attend_back(): pl.pallas_call(functools.partial(attend_back_kernel, row0=row0, block=blo...  36.7 us
    pallas_call x2, Pallas kernels, feed(): pl.pallas_call(functools.partial(feed_kernel, tiles=tiles), grid=(2 * til...  31.1 us
    pallas_call x2, Pallas kernels, attend(): pl.pallas_call(functools.partial(attend_kernel, row0=row0, block=block),...  21.3 us
    pallas_call x2, Pallas kernels, feed_grads(): pl.pallas_call(functools.partial(feed_grads_kernel, tiles=tiles, received...  12.4 us
    ppermute x9, starting transfers between devices, swap_x(): return lax.ppermute(value, 'tensor', [(0, 2), (2, 0), (1, 3), (3, 1)])  10.9 us
  transfers between devices with their start and end apart: 48, of which 20 were waited for; matrix products, arithmetic and copies ran while one was open for 7% of the time, Pallas kernels for 32%

profile of v3, /device:TPU:0, one launch (start us, length us, event | category | flops | bytes accessed | tf_op | source)
XLA Modules:
  0.0 401.0 jit_solution(10455286414258793371)
XLA Ops:
  11.0 5.1 %collective-permute-start.1 = (bf16[144,1024]{1,0:T(8,128)(2,1)S(1)}, bf16[144,1024]{1,0:T(8,128)(2,1)S(1)}, u32[]{:S(2)}, u32[]{:S(2)}) collective-permute-start(bf16[144,1024]{1,0:T(8,128)(2,1)S(1)} %fusion.8.refs_0_), channel_id=1, source_target_pairs={{0,24},{4,28},{8,16},{12,20},{16,8},{20,12},{24,0},{28,4},{1,25},{... | collective-permute-start | bytes 884744 | tf_op jit(solution)/shard_map/ppermute | solution.py:793
  20.0 4.2 %collective-permute-done.1.rest_2_.rest_0_.refs_6_ = bf16[144,1024]{1,0:T(8,128)(2,1)S(1)} collective-permute-done((bf16[144,1024]{1,0:T(8,128)(2,1)S(1)}, bf16[144,1024]{1,0:T(8,128)(2,1)S(1)}, u32[]{:S(2)}, u32[]{:S(2)}) %collective-permute-start.1) | collective-permute-done | bytes 294944 | tf_op jit(solution)/shard_map/ppermute | solution.py:793
  25.9 15.4 %collective-permute-done.2.rest_1_.refs_4_ = bf16[144,1024]{1,0:T(8,128)(2,1)S(1)} collective-permute-done((bf16[144,1024]{1,0:T(8,128)(2,1)S(1)}, bf16[144,1024]{1,0:T(8,128)(2,1)S(1)}, u32[]{:S(2)}, u32[]{:S(2)}) %collective-permute-start.2) | collective-permute-done | bytes 294944 | tf_op jit(solution)/shard_map/ppermute | solution.py:793
  44.3 5.0 %collective-permute-done.6.rest_3_.refs_1_ = bf16[144,1024]{1,0:T(8,128)(2,1)S(1)} collective-permute-done((bf16[144,1024]{1,0:T(8,128)(2,1)S(1)}, bf16[144,1024]{1,0:T(8,128)(2,1)S(1)}, u32[]{:S(2)}, u32[]{:S(2)}) %collective-permute-start.6) | collective-permute-done | bytes 294944 | tf_op jit(solution)/shard_map/ppermute | solution.py:793
  51.4 8.1 %collective-permute-done.3.rest_1_.refs_5_ = bf16[144,1024]{1,0:T(8,128)(2,1)S(1)} collective-permute-done((bf16[144,1024]{1,0:T(8,128)(2,1)}, bf16[144,1024]{1,0:T(8,128)(2,1)S(1)}, u32[]{:S(2)}, u32[]{:S(2)}) %collective-permute-start.3) | collective-permute-done | bytes 294944 | tf_op jit(solution)/shard_map/ppermute | solution.py:793
  59.5 3.6 collective-permute-done.5.rest_2_.refs_3_
  77.7 6.1 %project.1 = (bf16[2048,1024]{1,0:T(8,128)(2,1)S(1)}, bf16[2048,768]{1,0:T(8,128)(2,1)S(1)}) custom-call(bf16[2048,1024]{1,0:T(8,128)(2,1)S(1)} %copy-done.3, f32[8,1024]{1,0:T(8,128)S(1)} %bitcast.102, f32[1,768]{1,0:T(1,128)S(1)} %reshape.138.shift_ref, bf16[1152,1024]{1,0:T(8,128)(2,1)S(1)} %place_shares.2.weight_ref.refs_4_.refs_5_), custom_call_target="tpu_custom_call" | custom-call | flops 2750000 | bytes 2500 | tf_op jit(solution)/shard_map/project/pallas_call | solution.py:644
  83.9 5.7 %attend_0.1 = (bf16[1024,256]{1,0:T(8,128)(2,1)S(1)}, f32[2,2,1024]{2,1,0:T(2,128)S(1)}) custom-call(bf16[2048,768]{1,0:T(8,128)(2,1)S(1)} %get-tuple-element.61.qkv_ref), custom_call_target="tpu_custom_call" | custom-call | flops 2750000 | bytes 2500 | tf_op jit(solution)/shard_map/attend_0/pallas_call | solution.py:136
  90.8 5.2 %collective-permute-start.17 = (bf16[128,2048]{1,0:T(8,128)(2,1)S(1)}, bf16[128,2048]{1,0:T(8,128)(2,1)S(1)}, u32[]{:S(2)}, u32[]{:S(2)}) collective-permute-start(bf16[128,2048]{1,0:T(8,128)(2,1)S(1)} %copy-done.98), channel_id=1, source_target_pairs={{0,16},{4,20},{8,24},{12,28},{16,0},{20,4},{24,8},{28,12},{1,17},{... | collective-permute-start | bytes 1572872 | tf_op jit(solution)/shard_map/ppermute | solution.py:793
  103.1 28.1 %collective-permute-done.17.refs_4_ = bf16[128,2048]{1,0:T(8,128)(2,1)S(1)} collective-permute-done((bf16[128,2048]{1,0:T(8,128)(2,1)S(1)}, bf16[128,2048]{1,0:T(8,128)(2,1)S(1)}, u32[]{:S(2)}, u32[]{:S(2)}) %collective-permute-start.17) | collective-permute-done | bytes 524320 | tf_op jit(solution)/shard_map/ppermute | solution.py:793
  133.3 15.6 %attend_1024.1 = (bf16[1024,256]{1,0:T(8,128)(2,1)S(1)}, f32[2,2,1024]{2,1,0:T(2,128)S(1)}) custom-call(bf16[2048,768]{1,0:T(8,128)(2,1)S(1)} %get-tuple-element.61.qkv_ref, bf16[512,1024]{1,0:T(8,128)(2,1)S(1)} %convolution_convert_fusion.1.rest_0_.part_ref, bf16[128,2048]{1,0:T(8,128)(2,1)S(1)} %collective-permute-done.16.rest_1_.refs_3_), custom_call_target="tpu_custom_call" | custom-call | flops 2750000 | bytes 2500 | tf_op jit(solution)/shard_map/attend_1024/pallas_call | solution.py:136
  152.0 3.4 collective-permute-done.20.refs_7_
  165.1 16.4 %feed.2 = (f32[512,1024]{1,0:T(8,128)S(1)}, bf16[512,1024]{1,0:T(8,128)(2,1)S(1)}, bf16[512,2048]{1,0:T(8,128)(2,1)S(1)}, bf16[512,2048]{1,0:T(8,128)(2,1)S(1)},...) custom-call(bf16[512,1024]{1,0:T(8,128)(2,1)S(1)} %copy-done.10, ...), custom_call_target="tpu_custom_call" | custom-call | flops 4400000000 | bytes 4000000 | tf_op jit(solution)/shard_map/feed/pallas_call | solution.py:747
  192.8 14.6 %feed.3 = (f32[512,1024]{1,0:T(8,128)S(1)}, bf16[512,1024]{1,0:T(8,128)(2,1)S(1)}, bf16[512,2048]{1,0:T(8,128)(2,1)S(1)}, bf16[512,2048]{1,0:T(8,128)(2,1)S(1)},...) custom-call(bf16[512,1024]{1,0:T(8,128)(2,1)S(1)} %copy-done.13, ...), custom_call_target="tpu_custom_call" | custom-call | flops 4400000000 | bytes 4000000 | tf_op jit(solution)/shard_map/feed/pallas_call | solution.py:747
  211.2 5.9 %feed_grads.2.rest_0_ = bf16[1024,2048]{1,0:T(8,128)(2,1)S(1)} custom-call(bf16[512,1024]{1,0:T(8,128)(2,1)S(1)} %copy-done.47, bf16[512,1024]{1,0:T(8,128)(2,1)S(1)} %get-tuple-element.70.refs_1_, bf16[512,1024]{1,0:T(8,128)(2,1)S(1)} %copy-done.8, bf16[512,1024]{1,0:T(8,128)(2,1)S(1)} %copy-done.5, bf16[512,2048]{1,0:T(8,128)(2,1)S(1)} %get-tuple-element.71.refs_4_, ...), custom_call_target="tpu_custom_call" | custom-call | flops 1650000000 | bytes 1500000 | tf_op jit(solution)/shard_map/feed_grads/pallas_call | solution.py:515
  217.4 4.3 %norm_two.2 = (f32[512,1024]{1,0:T(8,128)S(1)}, bf16[512,1024]{1,0:T(8,128)(2,1)S(1)}, bf16[512,512]{1,0:T(8,128)(2,1)S(1)}, f32[8,1024]{1,0:T(8,128)S(1)}) custom-call(bf16[512,1024]{1,0:T(8,128)(2,1)} %get-tuple-element.68.back_ref, bf16[512,1024]{1,0:T(8,128)(2,1)} %collective-permute-done.24.refs_8_.recv_ref, ...), custom_call_target="tpu_custom_call" | custom-call | flops 1100000000 | bytes 1000000 | tf_op jit(solution)/shard_map/norm_two/pallas_call | solution.py:316
  224.4 6.4 %feed_grads.3.rest_0_ = bf16[1024,2048]{1,0:T(8,128)(2,1)S(1)} custom-call(bf16[512,1024]{1,0:T(8,128)(2,1)S(1)} %copy-done.48, bf16[512,1024]{1,0:T(8,128)(2,1)S(1)} %get-tuple-element.70.refs_1_, bf16[512,1024]{1,0:T(8,128)(2,1)S(1)} %copy-done.8, bf16[512,1024]{1,0:T(8,128)(2,1)S(1)} %copy-done.5, bf16[512,2048]{1,0:T(8,128)(2,1)S(1)} %copy-done.39, ...), custom_call_target="tpu_custom_call" | custom-call | flops 1650000000 | bytes 1500000 | tf_op jit(solution)/shard_map/feed_grads/pallas_call | solution.py:515
  241.5 10.9 %attend_back_0_0.1 = (f32[1024,768]{1,0:T(8,128)S(1)}, f32[1,768]{1,0:T(1,128)}) custom-call(s32[1]{0:T(128)} %constant.103.clone.1.core_ref, bf16[2048,768]{1,0:T(8,128)(2,1)S(1)} %copy-done.25, bf16[1024,256]{1,0:T(8,128)(2,1)S(1)} %copy-done.89, bf16[1024,256]{1,0:T(8,128)(2,1)S(1)} %pad_maximum_fusion.3.grad_ref, ...), custom_call_target="tpu_custom_call" | custom-call | flops 3024999936 | bytes 2750000 | tf_op jit(solution)/shard_map/attend_back_0_0/pallas_call | solution.py:259
  254.6 5.8 %collective-permute-done.28.recv_ref = bf16[512,1024]{1,0:T(8,128)(2,1)} collective-permute-done((bf16[512,1024]{1,0:T(8,128)(2,1)}, bf16[512,1024]{1,0:T(8,128)(2,1)}, u32[]{:S(2)}, u32[]{:S(2)}) %collective-permute-start.28) | collective-permute-done | bytes 1048608 | tf_op jit(solution)/shard_map/ppermute | solution.py:36
  266.4 4.3 %norm_two.3 = (f32[512,1024]{1,0:T(8,128)S(1)}, bf16[512,1024]{1,0:T(8,128)(2,1)S(1)}, bf16[512,512]{1,0:T(8,128)(2,1)S(1)}, f32[8,1024]{1,0:T(8,128)S(1)}) custom-call(bf16[512,1024]{1,0:T(8,128)(2,1)S(1)} %copy-done.73, bf16[512,1024]{1,0:T(8,128)(2,1)} %collective-permute-done.28.recv_ref, f32[512,1024]{1,0:T(8,128)S(1)} %copy-done.37, ...), custom_call_target="tpu_custom_call" | custom-call | flops 1100000000 | bytes 1000000 | tf_op jit(solution)/shard_map/norm_two/pallas_call | solution.py:316
  275.8 12.9 %attend_back_1024_0.1 = (bf16[2048,384]{1,0:T(8,128)(2,1)S(1)}, f32[1,384]{1,0:T(1,128)S(1)}, bf16[1024,384]{1,0:T(8,128)(2,1)S(1)}) custom-call(s32[1]{0:T(128)} %bitcast.27.core_ref, bf16[2048,768]{1,0:T(8,128)(2,1)S(1)} %copy-done.26, bf16[1024,256]{1,0:T(8,128)(2,1)S(1)} %copy-done.86, bf16[1024,256]{1,0:T(8,128)(2,1)S(1)} %pad_maximum_fusion.4.grad_ref, ...), custom_call_target="tpu_custom_call" | custom-call | flops 3575000064 | bytes 3250000 | tf_op jit(solution)/shard_map/attend_back_1024_0/pallas_call | solution.py:259
  288.8 5.4 %weight_grads.2 = (f32[4,128,640]{2,1,0:T(8,128)S(1)}, bf16[4,128,640]{2,1,0:T(8,128)(2,1)}) custom-call(s32[1]{0:T(128)} %bitcast.29.y_ref, bf16[2048,1024]{1,0:T(8,128)(2,1)S(1)} %copy-done.16, bf16[2048,384]{1,0:T(8,128)(2,1)S(1)} %get-tuple-element.82.rest_0_.grad_ref.refs_0_, bf16[512,1024]{1,0:T(8,128)(2,1)S(1)} %copy-done.33, ...), custom_call_target="tpu_custom_call" | custom-call | flops 1100000000 | bytes 1000000 | tf_op jit(solution)/shard_map/weight_grads/pallas_call | solution.py:567
  304.5 12.9 %attend_back_1024_1.1 = (bf16[2048,384]{1,0:T(8,128)(2,1)S(1)}, f32[1,384]{1,0:T(1,128)S(1)}, bf16[1024,384]{1,0:T(8,128)(2,1)S(1)}) custom-call(s32[1]{0:T(128)} %bitcast.27.core_ref, bf16[2048,768]{1,0:T(8,128)(2,1)S(1)} %copy-done.27, bf16[1024,256]{1,0:T(8,128)(2,1)S(1)} %copy-done.87, bf16[1024,256]{1,0:T(8,128)(2,1)S(1)} %copy-done.84, ...), custom_call_target="tpu_custom_call" | custom-call | flops 3575000064 | bytes 3250000 | tf_op jit(solution)/shard_map/attend_back_1024_1/pallas_call | solution.py:259
  323.3 3.6 weight_grads.3
  331.2 6.1 %collective-permute-start.36 = (bf16[128,640]{1,0:T(8,128)(2,1)}, bf16[128,640]{1,0:T(8,128)(2,1)}, u32[]{:S(2)}, u32[]{:S(2)}) collective-permute-start(bf16[128,640]{1,0:T(8,128)(2,1)} %get-tuple-element.119), channel_id=1, source_target_pairs={{0,16},{4,20},{8,24},{12,28},{16,0},{20,4},{24,8},{28,12},{1,17},{... | collective-permute-start | bytes 491528 | tf_op jit(solution)/shard_map/ppermute | solution.py:793
  338.1 9.9 %norm_one.1 = (f32[512,1024]{1,0:T(8,128)S(1)}, bf16[512,1024]{1,0:T(8,128)(2,1)}, f32[8,1024]{1,0:T(8,128)S(1)}) custom-call(s32[2]{0:T(128)S(1)} %pad_add_fusion.place_ref, bf16[512,1024]{1,0:T(8,128)(2,1)S(1)} %copy-done.11, bf16[512,1024]{1,0:T(8,128)(2,1)S(1)} %copy-done.14, bf16[2048,384]{1,0:T(8,128)(2,1)S(1)} %copy-done.23, ...), custom_call_target="tpu_custom_call" | custom-call | flops 2200000000 | bytes 2000000 | tf_op jit(solution)/shard_map/norm_one/pallas_call | solution.py:382
  354.6 3.1 add_convert_fusion.refs_9_
  357.7 7.2 %collective-permute-done.40.value_ref = bf16[4,144,384]{2,1,0:T(8,128)(2,1)} collective-permute-done((bf16[4,144,384]{2,1,0:T(8,128)(2,1)}, bf16[4,144,384]{2,1,0:T(8,128)(2,1)}, u32[]{:S(2)}, u32[]{:S(2)}) %collective-permute-start.40) | collective-permute-done | bytes 442400 | tf_op jit(solution)/shard_map/ppermute | solution.py:793
  371.2 2.7 collective-permute-done.41.refs_5_
  373.9 3.8 collective-permute-done.42.refs_6_
  378.5 2.9 finish.1
  386.1 5.8 %norm_one_back.1 = bf16[512,1024]{1,0:T(8,128)(2,1)} custom-call(s32[2]{0:T(128)} %copy-done.92, bf16[512,1024]{1,0:T(8,128)(2,1)} %input_ref.1, f32[512,1024]{1,0:T(8,128)} %copy-done.53, bf16[512,1024]{1,0:T(8,128)(2,1)} %tie.15.recv_ref, f32[512,1024]{1,0:T(8,128)} %copy-done.51, f32[512,1024]{1,0:T(8,128)} %copy-done.52, f32[8,1024]{1,0:T(8,128)} %bitcast.107), custom_call_target="tpu_custom_call" | custom-call | flops 1100000000 | bytes 1000000 | tf_op jit(solution)/shard_map/norm_one_back/pallas_call | solution.py:427
  (384 shorter events, 134.6 us)
Async XLA Ops:
  7.2 370.6 %reduce-scatter.2.cloned.1.call-start = ((), (), s32[]{:S(2)}) async-start(), calls=%async_computation.1 | async-start | bytes 4718592 | tf_op jit(solution)/shard_map/reduce_scatter | solution.py:1038
  11.0 13.1 %collective-permute-start.1 = (bf16[144,1024]{1,0:T(8,128)(2,1)S(1)}, bf16[144,1024]{1,0:T(8,128)(2,1)S(1)}, u32[]{:S(2)}, u32[]{:S(2)}) collective-permute-start(bf16[144,1024]{1,0:T(8,128)(2,1)S(1)} %fusion.8.refs_0_), channel_id=1, source_target_pairs={{0,24},{4,28},{8,16},{12,20},{16,8},{20,12},{24,0},{28,4},{1,25},{... | collective-permute-start | bytes 884744 | tf_op jit(solution)/shard_map/ppermute | solution.py:793
  16.2 25.1 %collective-permute-start.2 = (bf16[144,1024]{1,0:T(8,128)(2,1)S(1)}, bf16[144,1024]{1,0:T(8,128)(2,1)S(1)}, u32[]{:S(2)}, u32[]{:S(2)}) collective-permute-start(bf16[144,1024]{1,0:T(8,128)(2,1)S(1)} %fusion.8.refs_0_), channel_id=1, source_target_pairs={{0,16},{4,20},{8,24},{12,28},{16,0},{20,4},{24,8},{28,12},{1,17},{... | collective-permute-start | bytes 884744 | tf_op jit(solution)/shard_map/ppermute | solution.py:793
  16.2 27.4 %collective-permute-start.4 = (bf16[144,1024]{1,0:T(8,128)(2,1)S(1)}, bf16[144,1024]{1,0:T(8,128)(2,1)S(1)}, u32[]{:S(2)}, u32[]{:S(2)}) collective-permute-start(bf16[144,1024]{1,0:T(8,128)(2,1)S(1)} %fusion.8.refs_0_), channel_id=1, source_target_pairs={{0,8},{4,12},{8,0},{12,4},{16,24},{20,28},{24,16},{28,20},{1,9},{5... | collective-permute-start | bytes 884744 | tf_op jit(solution)/shard_map/ppermute | solution.py:793
  16.8 46.3 %collective-permute-start = (bf16[512,1024]{1,0:T(8,128)(2,1)}, bf16[512,1024]{1,0:T(8,128)(2,1)}, u32[]{:S(2)}, u32[]{:S(2)}) collective-permute-start(bf16[512,1024]{1,0:T(8,128)(2,1)} %input_ref.1), channel_id=1, source_target_pairs={{0,2},{2,0},{1,3},{3,1},{4,6},{6,4},{5,7},{7,5},{8,10},{10,8},{9,1... | collective-permute-start | bytes 3145736 | tf_op jit(solution)/shard_map/ppermute | solution.py:36
  18.4 45.5 %collective-permute-start.9 = (bf16[512,1024]{1,0:T(8,128)(2,1)}, bf16[512,1024]{1,0:T(8,128)(2,1)}, u32[]{:S(2)}, u32[]{:S(2)}) collective-permute-start(bf16[512,1024]{1,0:T(8,128)(2,1)} %param.27), channel_id=1, source_target_pairs={{0,2},{2,0},{1,3},{3,1},{4,6},{6,4},{5,7},{7,5},{8,10},{10,8},{9,1... | collective-permute-start | bytes 3145736 | tf_op jit(solution)/shard_map/ppermute | solution.py:36
  24.1 26.7 %collective-permute-start.7 = (bf16[128,2048]{1,0:T(8,128)(2,1)S(1)}, bf16[128,2048]{1,0:T(8,128)(2,1)S(1)}, u32[]{:S(2)}, u32[]{:S(2)}) collective-permute-start(bf16[128,2048]{1,0:T(8,128)(2,1)S(1)} %pad_maximum_fusion.2.refs_0_), channel_id=1, source_target_pairs={{0,4},{4,0},{8,12},{12,8},{16,20},{20,16},{24,28},{28,24},{1,5},{5... | collective-permute-start | bytes 1572872 | tf_op jit(solution)/shard_map/ppermute | solution.py:793
  44.3 18.8 %collective-permute-start.8 = (bf16[128,2048]{1,0:T(8,128)(2,1)}, bf16[128,2048]{1,0:T(8,128)(2,1)S(1)}, u32[]{:S(2)}, u32[]{:S(2)}) collective-permute-start(bf16[128,2048]{1,0:T(8,128)(2,1)} %tie.8), channel_id=1, source_target_pairs={{0,8},{4,12},{8,0},{12,4},{16,24},{20,28},{24,16},{28,20},{1,9},{5... | collective-permute-start | bytes 1572872 | tf_op jit(solution)/shard_map/ppermute | solution.py:793
  49.3 10.2 %collective-permute-start.3 = (bf16[144,1024]{1,0:T(8,128)(2,1)}, bf16[144,1024]{1,0:T(8,128)(2,1)S(1)}, u32[]{:S(2)}, u32[]{:S(2)}) collective-permute-start(bf16[144,1024]{1,0:T(8,128)(2,1)} %copy-done.62), channel_id=1, source_target_pairs={{0,4},{4,0},{8,12},{12,8},{16,20},{20,16},{24,28},{28,24},{1,5},{5... | collective-permute-start | bytes 884744 | tf_op jit(solution)/shard_map/ppermute | solution.py:793
  50.9 12.3 %collective-permute-start.5 = (bf16[144,1024]{1,0:T(8,128)(2,1)}, bf16[144,1024]{1,0:T(8,128)(2,1)S(1)}, u32[]{:S(2)}, u32[]{:S(2)}) collective-permute-start(bf16[144,1024]{1,0:T(8,128)(2,1)} %copy-done.64), channel_id=1, source_target_pairs={{0,4},{4,0},{8,12},{12,8},{16,20},{20,16},{24,28},{28,24},{1,5},{5... | collective-permute-start | bytes 884744 | tf_op jit(solution)/shard_map/ppermute | solution.py:793
  74.9 24.6 %collective-permute-start.14 = (bf16[1152,1024]{1,0:T(8,128)(2,1)S(1)}, bf16[1152,1024]{1,0:T(8,128)(2,1)}, u32[]{:S(2)}, u32[]{:S(2)}) collective-permute-start(bf16[1152,1024]{1,0:T(8,128)(2,1)S(1)} %place_shares.2.weight_ref.refs_4_.refs_5_), channel_id=1, source_target_pairs={{0,1},{1,0},{2,3},{3,2},{4,5},{5,4},{6,7},{7,6},{8,9},{9,8},{10,11... | collective-permute-start | bytes 7077896 | tf_op jit(solution)/shard_map/ppermute | solution.py:40
  90.5 10.3 %collective-permute-start.13 = (bf16[512,256]{1,0:T(8,128)(2,1)S(1)}, bf16[512,256]{1,0:T(8,128)(2,1)S(1)}, u32[]{:S(2)}, u32[]{:S(2)}) collective-permute-start(bf16[512,256]{1,0:T(8,128)(2,1)S(1)} %get-tuple-element.131), channel_id=1, source_target_pairs={{0,1},{1,0},{2,3},{3,2},{4,5},{5,4},{6,7},{7,6},{8,9},{9,8},{10,11... | collective-permute-start | bytes 786440 | tf_op jit(solution)/shard_map/ppermute | solution.py:40
  90.8 40.4 %collective-permute-start.17 = (bf16[128,2048]{1,0:T(8,128)(2,1)S(1)}, bf16[128,2048]{1,0:T(8,128)(2,1)S(1)}, u32[]{:S(2)}, u32[]{:S(2)}) collective-permute-start(bf16[128,2048]{1,0:T(8,128)(2,1)S(1)} %copy-done.98), channel_id=1, source_target_pairs={{0,16},{4,20},{8,24},{12,28},{16,0},{20,4},{24,8},{28,12},{1,17},{... | collective-permute-start | bytes 1572872 | tf_op jit(solution)/shard_map/ppermute | solution.py:793
  96.1 36.7 %collective-permute-start.19 = (bf16[128,2048]{1,0:T(8,128)(2,1)S(1)}, bf16[128,2048]{1,0:T(8,128)(2,1)S(1)}, u32[]{:S(2)}, u32[]{:S(2)}) collective-permute-start(bf16[128,2048]{1,0:T(8,128)(2,1)S(1)} %copy-done.98), channel_id=1, source_target_pairs={{0,24},{4,28},{8,16},{12,20},{16,8},{20,12},{24,0},{28,4},{1,25},{... | collective-permute-start | bytes 1572872 | tf_op jit(solution)/shard_map/ppermute | solution.py:793
  97.9 35.4 %collective-permute-start.16 = (bf16[128,2048]{1,0:T(8,128)(2,1)S(1)}, bf16[128,2048]{1,0:T(8,128)(2,1)S(1)}, u32[]{:S(2)}, u32[]{:S(2)}) collective-permute-start(bf16[128,2048]{1,0:T(8,128)(2,1)S(1)} %copy-done.57), channel_id=1, source_target_pairs={{0,4},{4,0},{8,12},{12,8},{16,20},{20,16},{24,28},{28,24},{1,5},{5... | collective-permute-start | bytes 1572872 | tf_op jit(solution)/shard_map/ppermute | solution.py:793
  101.6 53.9 %collective-permute-start.15 = (bf16[512,1024]{1,0:T(8,128)(2,1)S(1)}, bf16[512,1024]{1,0:T(8,128)(2,1)S(1)}, u32[]{:S(2)}, u32[]{:S(2)}) collective-permute-start(bf16[512,1024]{1,0:T(8,128)(2,1)S(1)} %convolution_convert_fusion.1.rest_0_.part_ref), channel_id=1, source_target_pairs={{0,2},{2,0},{1,3},{3,1},{4,6},{6,4},{5,7},{7,5},{8,10},{10,8},{9,1... | collective-permute-start | bytes 3145736 | tf_op jit(solution)/shard_map/ppermute | solution.py:36
  131.3 20.8 %collective-permute-start.18 = (bf16[128,2048]{1,0:T(8,128)(2,1)S(1)}, bf16[128,2048]{1,0:T(8,128)(2,1)S(1)}, u32[]{:S(2)}, u32[]{:S(2)}) collective-permute-start(bf16[128,2048]{1,0:T(8,128)(2,1)S(1)} %collective-permute-done.17.refs_4_), channel_id=1, source_target_pairs={{0,4},{4,0},{8,12},{12,8},{16,20},{20,16},{24,28},{28,24},{1,5},{5... | collective-permute-start | bytes 1572872 | tf_op jit(solution)/shard_map/ppermute | solution.py:793
  132.8 22.7 %collective-permute-start.20 = (bf16[128,2048]{1,0:T(8,128)(2,1)S(1)}, bf16[128,2048]{1,0:T(8,128)(2,1)S(1)}, u32[]{:S(2)}, u32[]{:S(2)}) collective-permute-start(bf16[128,2048]{1,0:T(8,128)(2,1)S(1)} %collective-permute-done.19.refs_6_), channel_id=1, source_target_pairs={{0,4},{4,0},{8,12},{12,8},{16,20},{20,16},{24,28},{28,24},{1,5},{5... | collective-permute-start | bytes 1572872 | tf_op jit(solution)/shard_map/ppermute | solution.py:793
  159.3 26.7 %collective-permute-start.23 = (bf16[512,1024]{1,0:T(8,128)(2,1)S(1)}, bf16[512,1024]{1,0:T(8,128)(2,1)S(1)}, u32[]{:S(2)}, u32[]{:S(2)}) collective-permute-start(bf16[512,1024]{1,0:T(8,128)(2,1)S(1)} %convolution_convert_fusion.refs_9_.rest_0_.part_ref), channel_id=1, source_target_pairs={{0,2},{2,0},{1,3},{3,1},{4,6},{6,4},{5,7},{7,5},{8,10},{10,8},{9,1... | collective-permute-start | bytes 3145736 | tf_op jit(solution)/shard_map/ppermute | solution.py:36
  184.4 25.5 %collective-permute-start.24 = (bf16[512,1024]{1,0:T(8,128)(2,1)}, bf16[512,1024]{1,0:T(8,128)(2,1)}, u32[]{:S(2)}, u32[]{:S(2)}) collective-permute-start(bf16[512,1024]{1,0:T(8,128)(2,1)} %get-tuple-element.68.back_ref), channel_id=1, source_target_pairs={{0,2},{2,0},{1,3},{3,1},{4,6},{6,4},{5,7},{7,5},{8,10},{10,8},{9,1... | collective-permute-start | bytes 3145736 | tf_op jit(solution)/shard_map/ppermute | solution.py:36
  233.9 26.4 %collective-permute-start.28 = (bf16[512,1024]{1,0:T(8,128)(2,1)}, bf16[512,1024]{1,0:T(8,128)(2,1)}, u32[]{:S(2)}, u32[]{:S(2)}) collective-permute-start(bf16[512,1024]{1,0:T(8,128)(2,1)} %copy-done.72), channel_id=1, source_target_pairs={{0,2},{2,0},{1,3},{3,1},{4,6},{6,4},{5,7},{7,5},{8,10},{10,8},{9,1... | collective-permute-start | bytes 3145736 | tf_op jit(solution)/shard_map/ppermute | solution.py:36
  254.0 44.5 %collective-permute-start.27 = (bf16[512,1024]{1,0:T(8,128)(2,1)}, bf16[512,1024]{1,0:T(8,128)(2,1)}, u32[]{:S(2)}, u32[]{:S(2)}) collective-permute-start(bf16[512,1024]{1,0:T(8,128)(2,1)} %tie.10), channel_id=1, source_target_pairs={{0,2},{2,0},{1,3},{3,1},{4,6},{6,4},{5,7},{7,5},{8,10},{10,8},{9,1... | collective-permute-start | bytes 3145736 | tf_op jit(solution)/shard_map/ppermute | solution.py:36
  273.8 14.9 %collective-permute-start.30 = (bf16[1024,256]{1,0:T(8,128)(2,1)S(1)}, bf16[1024,256]{1,0:T(8,128)(2,1)S(1)}, u32[]{:S(2)}, u32[]{:S(2)}) collective-permute-start(bf16[1024,256]{1,0:T(8,128)(2,1)S(1)} %fusion), channel_id=1, source_target_pairs={{0,1},{1,0},{2,3},{3,2},{4,5},{5,4},{6,7},{7,6},{8,9},{9,8},{10,11... | collective-permute-start | bytes 1572872 | tf_op jit(solution)/shard_map/ppermute | solution.py:40
  295.3 24.2 %collective-permute-start.32 = (bf16[4,128,640]{2,1,0:T(8,128)(2,1)}, bf16[4,128,640]{2,1,0:T(8,128)(2,1)}, u32[]{:S(2)}, u32[]{:S(2)}) collective-permute-start(bf16[4,128,640]{2,1,0:T(8,128)(2,1)} %get-tuple-element.85.rest_1_), channel_id=1, source_target_pairs={{0,4},{4,0},{8,12},{12,8},{16,20},{20,16},{24,28},{28,24},{1,5},{5... | collective-permute-start | bytes 1966088 | tf_op jit(solution)/shard_map/ppermute | solution.py:793
  298.2 39.8 %collective-permute-start.31 = (bf16[1024,384]{1,0:T(8,128)(2,1)}, bf16[1024,384]{1,0:T(8,128)(2,1)S(1)}, u32[]{:S(2)}, u32[]{:S(2)}) collective-permute-start(bf16[1024,384]{1,0:T(8,128)(2,1)} %copy-done.93), channel_id=1, source_target_pairs={{0,1},{1,0},{2,3},{3,2},{4,5},{5,4},{6,7},{7,6},{8,9},{9,8},{10,11... | collective-permute-start | bytes 2359304 | tf_op jit(solution)/shard_map/ppermute | solution.py:40
  319.5 18.5 %collective-permute-start.33 = (bf16[1024,384]{1,0:T(8,128)(2,1)}, bf16[1024,384]{1,0:T(8,128)(2,1)S(1)}, u32[]{:S(2)}, u32[]{:S(2)}) collective-permute-start(bf16[1024,384]{1,0:T(8,128)(2,1)} %tie.12), channel_id=1, source_target_pairs={{0,1},{1,0},{2,3},{3,2},{4,5},{5,4},{6,7},{7,6},{8,9},{9,8},{10,11... | collective-permute-start | bytes 2359304 | tf_op jit(solution)/shard_map/ppermute | solution.py:40
  329.4 28.2 %collective-permute-start.35 = (bf16[128,640]{1,0:T(8,128)(2,1)}, bf16[128,640]{1,0:T(8,128)(2,1)}, u32[]{:S(2)}, u32[]{:S(2)}) collective-permute-start(bf16[128,640]{1,0:T(8,128)(2,1)} %get-tuple-element.120), channel_id=1, source_target_pairs={{0,24},{4,28},{8,16},{12,20},{16,8},{20,12},{24,0},{28,4},{1,25},{... | collective-permute-start | bytes 491528 | tf_op jit(solution)/shard_map/ppermute | solution.py:793
  331.2 26.5 %collective-permute-start.36 = (bf16[128,640]{1,0:T(8,128)(2,1)}, bf16[128,640]{1,0:T(8,128)(2,1)}, u32[]{:S(2)}, u32[]{:S(2)}) collective-permute-start(bf16[128,640]{1,0:T(8,128)(2,1)} %get-tuple-element.119), channel_id=1, source_target_pairs={{0,16},{4,20},{8,24},{12,28},{16,0},{20,4},{24,8},{28,12},{1,17},{... | collective-permute-start | bytes 491528 | tf_op jit(solution)/shard_map/ppermute | solution.py:793
  337.3 20.4 %collective-permute-start.37 = (bf16[128,640]{1,0:T(8,128)(2,1)}, bf16[128,640]{1,0:T(8,128)(2,1)}, u32[]{:S(2)}, u32[]{:S(2)}) collective-permute-start(bf16[128,640]{1,0:T(8,128)(2,1)} %get-tuple-element.118), channel_id=1, source_target_pairs={{0,8},{4,12},{8,0},{12,4},{16,24},{20,28},{24,16},{28,20},{1,9},{5... | collective-permute-start | bytes 491528 | tf_op jit(solution)/shard_map/ppermute | solution.py:793
  349.3 28.4 %collective-permute-start.34 = (bf16[512,1024]{1,0:T(8,128)(2,1)}, bf16[512,1024]{1,0:T(8,128)(2,1)}, u32[]{:S(2)}, u32[]{:S(2)}) collective-permute-start(bf16[512,1024]{1,0:T(8,128)(2,1)} %get-tuple-element.90.rest_0_), channel_id=1, source_target_pairs={{0,2},{2,0},{1,3},{3,1},{4,6},{6,4},{5,7},{7,5},{8,10},{10,8},{9,1... | collective-permute-start | bytes 3145736 | tf_op jit(solution)/shard_map/ppermute | solution.py:36
  352.9 12.0 %collective-permute-start.40 = (bf16[4,144,384]{2,1,0:T(8,128)(2,1)}, bf16[4,144,384]{2,1,0:T(8,128)(2,1)}, u32[]{:S(2)}, u32[]{:S(2)}) collective-permute-start(bf16[4,144,384]{2,1,0:T(8,128)(2,1)} %pad_maximum_fusion.5), channel_id=1, source_target_pairs={{0,4},{4,0},{8,12},{12,8},{16,20},{20,16},{24,28},{28,24},{1,5},{5... | collective-permute-start | bytes 1327112 | tf_op jit(solution)/shard_map/ppermute | solution.py:793
  367.6 10.1 %collective-permute-start.42 = (bf16[144,384]{1,0:T(8,128)(2,1)S(1)}, bf16[144,384]{1,0:T(8,128)(2,1)S(1)}, u32[]{:S(2)}, u32[]{:S(2)}) collective-permute-start(bf16[144,384]{1,0:T(8,128)(2,1)S(1)} %get-tuple-element.122), channel_id=1, source_target_pairs={{0,16},{4,20},{8,24},{12,28},{16,0},{20,4},{24,8},{28,12},{1,17},{... | collective-permute-start | bytes 331784 | tf_op jit(solution)/shard_map/ppermute | solution.py:793
  (124 other events, 1047.8 us)
Sparse Core Ops, SparseCore 0:
  234.0 97.0 reduce-scatter.1
